TPU v7x, 32 devices: a whole 2x2x4 slice. The times are simulated.
32 devices in a mesh: dp: 8 (over y, x, core), mp: 4 (over z).
Axes of the slice: x: 2, y: 2, z: 4, core: 2. Of those that a mesh axis runs over, the one named last changes fastest.
Arguments:
- tokens: bfloat16 [16384, 768], P(('dp', 'mp')), may hold values from -6 to 6
- bucket: int32 [32], P(('dp', 'mp')), may hold values from 0 to 1
- attn_gain: bfloat16 [768], P(('dp', 'mp')), may hold values from 0.25 to 1.75
- qk_weight: bfloat16 [2, 768, 768], P(None, ('dp', 'mp')), may hold values from -0.21875 to 0.21875
- value_weight: bfloat16 [768, 768], P(('dp', 'mp')), may hold values from -0.31835938 to 0.31835938
- inner_gain: bfloat16 [768], P(('dp', 'mp')), may hold values from 0.25 to 1.75
- out_weight: bfloat16 [768, 768], P(('dp', 'mp')), may hold values from -0.31835938 to 0.31835938
- ffn_gain: bfloat16 [768], P(('dp', 'mp')), may hold values from 0.25 to 1.75
- fc1_weight: bfloat16 [768, 3072], P('dp', 'mp'), may hold values from -0.31835938 to 0.31835938
- ffn_inner_gain: bfloat16 [3072], P('mp'), may hold values from 0.25 to 1.75
- fc2_weight: bfloat16 [3072, 768], P('mp', 'dp'), may hold values from -0.15917969 to 0.15917969
- cotangent: bfloat16 [16384, 768], P(('dp', 'mp')), may hold values from -6 to 6
Outputs:
- output: bfloat16 [16384, 768], P(('dp', 'mp'))
- token_gradient: float32 [16384, 768], P(('dp', 'mp'))
- grad_attn_gain: float32 [768], P(('dp', 'mp'))
- grad_qk_weight: float32 [2, 768, 768], P(None, ('dp', 'mp'))
- grad_value_weight: float32 [768, 768], P(('dp', 'mp'))
- grad_inner_gain: float32 [768], P(('dp', 'mp'))
- grad_out_weight: float32 [768, 768], P(('dp', 'mp'))
- grad_ffn_gain: float32 [768], P(('dp', 'mp'))
- grad_fc1_weight: float32 [768, 3072], P('dp', 'mp')
- grad_ffn_inner_gain: float32 [3072], P('mp')
- grad_fc2_weight: float32 [3072, 768], P('mp', 'dp')
Inputs may be any that keep to these rules, and one draw needn't show every extreme that they name: `bucket`: 0: a device's 512 tokens are 2 sequences of 256 tokens; 1: one sequence of 512 tokens.
All inputs are finite; a program needn't handle non-finite values.
Results may differ from a plain program's by a relative error of at most 0.018.
Values may be sent and summed in bfloat16 or wider, within the bound.
No kernel may reach another device: no remote copies, remote signals or barrier semaphores. Data moves between devices by JAX's collectives and lax.ppermute only.
A program may use at most 192 MiB of HBM per device.

v0:
```python
import jax
import jax.numpy as jnp
from jax import lax
from jax.sharding import PartitionSpec as P

D = 768
HEADS = 12
HEAD_DIM = 64
FEEDFWD_UNITS = 3072
SHORT = 256


EPSILON = 1e-05
NEGATIVE = -1e30


def gelu_exact(values):
    return jax.nn.gelu(values, approximate=False)


def apply_norm(values):
    mean_value = jnp.mean(values, axis=-1, keepdims=True)
    spread = jnp.mean(values * values, axis=-1, keepdims=True) - mean_value * mean_value
    inverse_deviation = lax.rsqrt(spread + EPSILON)
    return ((values - mean_value) * inverse_deviation, inverse_deviation)


def norm_backward(incoming_gradient, centered_rows, inverse_deviation, gain_vector):
    scaled_rows = incoming_gradient * gain_vector
    first_item = jnp.mean(scaled_rows, axis=-1, keepdims=True)
    second_item = jnp.mean(scaled_rows * centered_rows, axis=-1, keepdims=True)
    return inverse_deviation * (scaled_rows - first_item - centered_rows * second_item)


def matmul(left, right):
    return jnp.dot(left, right, preferred_element_type=jnp.float32)


def matmul_left_t(left, right):
    return jnp.einsum("ta,tb->ab", left, right, preferred_element_type=jnp.float32)


def matmul_right_t(left, right):
    return jnp.einsum("ta,ba->tb", left, right, preferred_element_type=jnp.float32)


def permitted_mask(bucket_id, offset, rows, keys, total):
    length = jnp.where(bucket_id == 0, SHORT, total).astype(jnp.int32)
    query_pos = offset + lax.broadcasted_iota(jnp.int32, (rows, keys), 0)
    key_pos = lax.broadcasted_iota(jnp.int32, (rows, keys), 1)
    return (key_pos <= query_pos) & (query_pos // length == key_pos // length)


def block_scores(queries, keys_all, bucket_id, offset, finish, total):
    scale = HEAD_DIM ** (-0.5)
    scores = (
        jnp.einsum("qhe,khe->hqk", queries, keys_all, preferred_element_type=jnp.float32) * scale
    )
    permitted = permitted_mask(bucket_id, offset, finish - offset, finish, total)
    return jnp.where(permitted[None], scores, NEGATIVE)


def attend(queries, keys_all, values_all, bucket_id):
    total = queries.shape[0]
    block = min(512, total)
    scores = block_scores(queries, keys_all, bucket_id, 0, block, total)
    peak = jnp.max(scores, axis=-1, keepdims=True)
    weights = jnp.exp(scores - peak)
    totals = jnp.sum(weights, axis=-1, keepdims=True)
    probs = (weights / totals).astype(jnp.bfloat16)
    outputs = jnp.einsum("hqk,khe->qhe", probs, values_all, preferred_element_type=jnp.float32)
    logsums = [peak + jnp.log(totals)]
    return (outputs, logsums)


def attend_back(queries, keys_all, values_all, grad_out, logsums, bucket_id):
    total = queries.shape[0]
    block = min(512, total)
    scale = HEAD_DIM ** (-0.5)
    grad_keys = jnp.zeros(keys_all.shape, jnp.float32)
    grad_values = jnp.zeros(values_all.shape, jnp.float32)
    scores = block_scores(queries, keys_all, bucket_id, 0, block, total)
    probs = jnp.exp(scores - logsums[0])
    rounded = probs.astype(jnp.bfloat16)
    grad_probs = jnp.einsum(
        "qhe,khe->hqk", grad_out, values_all, preferred_element_type=jnp.float32
    )
    centre = jnp.sum(probs * grad_probs, axis=-1, keepdims=True)
    grad_scores = (probs * (grad_probs - centre)).astype(jnp.bfloat16)
    grad_queries = (
        jnp.einsum("hqk,khe->qhe", grad_scores, keys_all, preferred_element_type=jnp.float32)
        * scale
    )
    grad_keys = grad_keys.at[:block].add(
        jnp.einsum("hqk,qhe->khe", grad_scores, queries, preferred_element_type=jnp.float32) * scale
    )
    grad_values = grad_values.at[:block].add(
        jnp.einsum("hqk,qhe->khe", rounded, grad_out, preferred_element_type=jnp.float32)
    )
    return (grad_queries, grad_keys, grad_values)


def on_device(
    tokens,
    bucket,
    attn_gain,
    qk_weight,
    value_weight,
    inner_gain,
    out_weight,
    ffn_gain,
    fc1_weight,
    ffn_inner_gain,
    fc2_weight,
    cotangent,
):
    input_gain, qk_all, value_all, middle_gain, out_all, feedforward_gain = (
        lax.all_gather(attn_gain, ("dp", "mp"), axis=0, tiled=True),
        lax.all_gather(qk_weight, ("dp", "mp"), axis=1, tiled=True),
        lax.all_gather(value_weight, ("dp", "mp"), axis=0, tiled=True),
        lax.all_gather(inner_gain, ("dp", "mp"), axis=0, tiled=True),
        lax.all_gather(out_weight, ("dp", "mp"), axis=0, tiled=True),
        lax.all_gather(ffn_gain, ("dp", "mp"), axis=0, tiled=True),
    )
    fc1_rows, fc2_rows = (
        lax.all_gather(fc1_weight, "dp", axis=0, tiled=True),
        lax.all_gather(fc2_weight, "dp", axis=1, tiled=True),
    )
    input_gain = input_gain.astype(jnp.float32)
    middle_gain = middle_gain.astype(jnp.float32)
    feedforward_gain = feedforward_gain.astype(jnp.float32)
    bucket_id = bucket[0]
    total = tokens.shape[0]
    head_layout = (total, HEADS, HEAD_DIM)
    input_rows = tokens.astype(jnp.float32)
    input_centered, input_inverse_deviation = apply_norm(input_rows)
    input_normed = (input_centered * input_gain).astype(jnp.bfloat16)
    queries = matmul(input_normed, qk_all[0]).astype(jnp.bfloat16).reshape(head_layout)
    keys_all = matmul(input_normed, qk_all[1]).astype(jnp.bfloat16).reshape(head_layout)
    values_all = matmul(input_normed, value_all).astype(jnp.bfloat16).reshape(head_layout)
    attended_rows, logsums = attend(queries, keys_all, values_all, bucket_id)
    attended_rows = attended_rows.reshape(total, D)
    middle_centered, middle_inverse_deviation = apply_norm(attended_rows)
    middle_normed = (middle_centered * middle_gain).astype(jnp.bfloat16)
    hidden_residual = input_rows + matmul(middle_normed, out_all)
    feedforward_centered, feedforward_inverse_deviation = apply_norm(hidden_residual)
    feedforward_normed = (feedforward_centered * feedforward_gain).astype(jnp.bfloat16)
    hidden_gain = ffn_inner_gain.astype(jnp.float32)
    normed_all = lax.all_gather(feedforward_normed, "mp", axis=0, tiled=True)
    hidden = matmul(normed_all, fc1_rows)
    activated_rows, gelu_back = jax.vjp(gelu_exact, hidden)
    bucket_pair = (
        jnp.sum(activated_rows, axis=-1),
        jnp.sum(activated_rows * activated_rows, axis=-1),
    )
    hidden_mean = (
        lax.psum(bucket_pair[0].astype(jnp.bfloat16), "mp").astype(jnp.float32) / FEEDFWD_UNITS
    )[:, None]
    spread_hidden = (
        lax.psum(bucket_pair[1].astype(jnp.bfloat16), "mp").astype(jnp.float32) / FEEDFWD_UNITS
    )[:, None] - hidden_mean * hidden_mean
    hidden_inverse_deviation = lax.rsqrt(spread_hidden + EPSILON)
    hidden_centered = (activated_rows - hidden_mean) * hidden_inverse_deviation
    squeezed_rows = (hidden_centered * hidden_gain).astype(jnp.bfloat16)
    branch_out = lax.psum_scatter(
        matmul(squeezed_rows, fc2_rows).astype(jnp.bfloat16), "mp", scatter_dimension=0, tiled=True
    ).astype(jnp.float32)
    piece = lax.all_gather(cotangent, "mp", axis=0, tiled=True)
    hidden_gradient = matmul_right_t(piece, fc2_rows)
    grad_down = matmul_left_t(squeezed_rows, piece)
    output = (hidden_residual + branch_out).astype(jnp.bfloat16)
    scaled_gradient = hidden_gradient * hidden_gain
    bucket_pair = (
        jnp.sum(scaled_gradient, axis=-1),
        jnp.sum(scaled_gradient * hidden_centered, axis=-1),
    )
    grad_activated = hidden_inverse_deviation * (
        scaled_gradient
        - (lax.psum(bucket_pair[0].astype(jnp.bfloat16), "mp").astype(jnp.float32) / FEEDFWD_UNITS)[
            :, None
        ]
        - hidden_centered
        * (lax.psum(bucket_pair[1].astype(jnp.bfloat16), "mp").astype(jnp.float32) / FEEDFWD_UNITS)[
            :, None
        ]
    )
    hidden_gain_gradient = jnp.sum(hidden_gradient * hidden_centered, axis=0)
    grad_hidden_b = gelu_back(grad_activated)[0].astype(jnp.bfloat16)
    grad_up = matmul_left_t(normed_all, grad_hidden_b)
    feedforward_normed_gradient = lax.psum_scatter(
        matmul_right_t(grad_hidden_b, fc1_rows).astype(jnp.bfloat16),
        "mp",
        scatter_dimension=0,
        tiled=True,
    ).astype(jnp.float32)
    grad_fc1, grad_fc2 = (
        lax.psum_scatter(
            grad_up.astype(jnp.bfloat16), "dp", scatter_dimension=0, tiled=True
        ).astype(jnp.float32),
        lax.psum_scatter(
            grad_down.astype(jnp.bfloat16), "dp", scatter_dimension=1, tiled=True
        ).astype(jnp.float32),
    )
    grad_hidden_gain = lax.psum(hidden_gain_gradient, "dp")
    residual_gradient = cotangent.astype(jnp.float32) + norm_backward(
        feedforward_normed_gradient,
        feedforward_centered,
        feedforward_inverse_deviation,
        feedforward_gain,
    )
    feedforward_gain_gradient = jnp.sum(feedforward_normed_gradient * feedforward_centered, axis=0)
    grad_branch = residual_gradient.astype(jnp.bfloat16)
    grad_out_proj = matmul_left_t(middle_normed, grad_branch)
    middle_gradient = matmul_right_t(grad_branch, out_all)
    middle_gain_gradient = jnp.sum(middle_gradient * middle_centered, axis=0)
    grad_attended = (
        norm_backward(middle_gradient, middle_centered, middle_inverse_deviation, middle_gain)
        .astype(jnp.bfloat16)
        .reshape(head_layout)
    )
    grad_queries, grad_keys, grad_values = attend_back(
        queries, keys_all, values_all, grad_attended, logsums, bucket_id
    )
    grad_queries = grad_queries.reshape(total, D).astype(jnp.bfloat16)
    grad_keys = grad_keys.reshape(total, D).astype(jnp.bfloat16)
    grad_values = grad_values.reshape(total, D).astype(jnp.bfloat16)
    grad_qk = jnp.stack(
        [matmul_left_t(input_normed, grad_queries), matmul_left_t(input_normed, grad_keys)]
    )
    grad_value_proj = matmul_left_t(input_normed, grad_values)
    input_normed_gradient = (
        matmul_right_t(grad_queries, qk_all[0])
        + matmul_right_t(grad_keys, qk_all[1])
        + matmul_right_t(grad_values, value_all)
    )
    token_gradient = residual_gradient + norm_backward(
        input_normed_gradient, input_centered, input_inverse_deviation, input_gain
    )
    input_gain_gradient = jnp.sum(input_normed_gradient * input_centered, axis=0)
    shares = (
        lax.psum_scatter(input_gain_gradient, ("dp", "mp"), scatter_dimension=0, tiled=True),
        lax.psum_scatter(grad_qk, ("dp", "mp"), scatter_dimension=1, tiled=True),
        lax.psum_scatter(grad_value_proj, ("dp", "mp"), scatter_dimension=0, tiled=True),
        lax.psum_scatter(middle_gain_gradient, ("dp", "mp"), scatter_dimension=0, tiled=True),
        lax.psum_scatter(grad_out_proj, ("dp", "mp"), scatter_dimension=0, tiled=True),
        lax.psum_scatter(feedforward_gain_gradient, ("dp", "mp"), scatter_dimension=0, tiled=True),
    )
    return (
        output,
        token_gradient,
        shares[0],
        shares[1],
        shares[2],
        shares[3],
        shares[4],
        shares[5],
        grad_fc1,
        grad_hidden_gain,
        grad_fc2,
    )


def solution(mesh):
    placed = (
        P(("dp", "mp"), None),
        P(("dp", "mp")),
        P(("dp", "mp")),
        P(None, ("dp", "mp"), None),
        P(("dp", "mp"), None),
        P(("dp", "mp")),
        P(("dp", "mp"), None),
        P(("dp", "mp")),
        P("dp", "mp"),
        P("mp"),
        P("mp", "dp"),
        P(("dp", "mp"), None),
    )
    return jax.shard_map(
        on_device,
        mesh=mesh,
        in_specs=placed,
        out_specs=(
            P(("dp", "mp"), None),
            P(("dp", "mp"), None),
            P(("dp", "mp")),
            P(None, ("dp", "mp"), None),
            P(("dp", "mp"), None),
            P(("dp", "mp")),
            P(("dp", "mp"), None),
            P(("dp", "mp")),
            P("dp", "mp"),
            P("mp"),
            P("mp", "dp"),
        ),
        check_vma=False,
    )
```

profile of v0, /device:TPU:0, one launch (start us, length us, event | category | flops | bytes accessed | tf_op | source)
XLA Modules:
  0.0 929.8 jit_solution(10899723531479557193)
XLA Ops:
  10.9 0.8 dynamic-update-slice.5
  11.8 0.8 dynamic-update-slice.4
  12.6 0.8 dynamic-update-slice.6
  13.5 42.1 %all-reduce.7 = (bf16[768]{0:T(1024)(128)(2,1)S(1)}, bf16[768]{0:T(1024)(128)(2,1)S(1)}, bf16[768]{0:T(1024)(128)(2,1)S(1)}) all-reduce(bf16[768]{0:T(1024)(128)(2,1)S(1)} %dynamic-update-slice.4, bf16[768]{0:T(1024)(128)(2,1)S(1)} %dynamic-update-slice.5, bf16[768]{0:T(1024)(128)(2,1)S(1)} %dynamic-update-slice.6), channel_id=1, replica_groups=mesh['dp'=8,'mp'=4] {'dp','mp'}, use_global_device_ids=true, to_apply=%add | all-reduce | flops 2304 | bytes 9216
  55.6 1.5 convert_reduce_fusion
  57.4 10.3 %all-gather.8.cloned.1.call-done = bf16[768,768]{1,0:T(8,128)(2,1)} async-done(((bf16[24,768]{1,0:T(8,128)(2,1)}), bf16[768,768]{1,0:T(8,128)(2,1)}) %all-gather.8.cloned.1.call-update) | async-done | bytes 1179664 | tf_op jit(solution)/shard_map/all_gather | solution.py:120
  67.7 2.4 convolution_convert_fusion.6
  70.0 1.2 copy.45
  71.2 55.9 %all-gather.10.cloned.1.call-done = bf16[2,768,768]{2,1,0:T(8,128)(2,1)} async-done(((bf16[2,24,768]{2,1,0:T(8,128)(2,1)}), bf16[2,768,768]{2,1,0:T(8,128)(2,1)}) %all-gather.10.cloned.1.call-update) | async-done | bytes 2359312 | tf_op jit(solution)/shard_map/all_gather | solution.py:119
  127.1 2.1 convolution_convert_fusion.4
  129.5 2.4 convolution_convert_fusion.5
  132.2 2.1 fusion.12
  134.3 2.6 fusion
  136.9 2.0 copy-done
  138.9 4.1 fusion.59
  143.7 39.3 %all-gather.12.cloned.1.call-done = bf16[768,768]{1,0:T(8,128)(2,1)} async-done(((bf16[24,768]{1,0:T(8,128)(2,1)}), bf16[768,768]{1,0:T(8,128)(2,1)}) %all-gather.12.cloned.1.call-update) | async-done | bytes 1179664 | tf_op jit(solution)/shard_map/all_gather | solution.py:122
  182.9 2.5 fusion.57
  185.4 1.4 multiply_convert_fusion.5
  187.4 0.7 all-gather.20.cloned.1.call-update
  188.2 19.5 %all-gather.16.cloned.1.call-done = bf16[768,768]{1,0:T(8,128)(2,1)} async-done(((bf16[96,768]{1,0:T(8,128)(2,1)}), bf16[768,768]{1,0:T(8,128)(2,1)}) %all-gather.16.cloned.1.call-update) | async-done | bytes 1179664 | tf_op jit(solution)/shard_map/all_gather | solution.py:126
  207.7 65.5 %all-gather.14.cloned.1.call-done = bf16[2048,768]{1,0:T(8,128)(2,1)} async-done(((bf16[512,768]{1,0:T(8,128)(2,1)}), bf16[2048,768]{1,0:T(8,128)(2,1)}) %all-gather.14.cloned.1.call-update) | async-done | bytes 3145744 | tf_op jit(solution)/shard_map/all_gather | solution.py:149
  273.2 20.0 %fusion.56 = (bf16[2048]{0:T(1024)(128)(2,1)S(1)}, bf16[2048]{0:T(1024)(128)(2,1)S(1)}, f32[2048,768]{0,1:T(8,128)}, f32[2048,768]{0,1:T(8,128)}, f32[2048,768]{0,1:T(8,128)}) fusion(bf16[2048,768]{1,0:T(8,128)(2,1)} %all-gather.14.cloned.1.call-done, bf16[768,768]{1,0:T(8,128)(2,1)} %all-gather.16.cloned.1.call-done), kind=kOutput, calls=%fused_computation.126 | convolution fusion | flops 2521296896 | bytes 23207936 | tf_op jit(solution)/shard_map/dot_general | solution.py:36
  293.2 9.2 all-reduce.9
  302.5 60.3 %all-gather.20.cloned.1.call-done = bf16[2048,768]{1,0:T(8,128)(2,1)} async-done(((bf16[512,768]{1,0:T(8,128)(2,1)}), bf16[2048,768]{1,0:T(8,128)(2,1)}) %all-gather.20.cloned.1.call-update) | async-done | bytes 3145744 | tf_op jit(solution)/shard_map/all_gather | solution.py:168
  362.8 10.6 %multiply_reduce_fusion.1 = (f32[768]{0:T(1024)S(1)}, bf16[2048]{0:T(1024)(128)(2,1)S(1)}, bf16[2048]{0:T(1024)(128)(2,1)S(1)}, f32[2048,768]{0,1:T(8,128)}) fusion(f32[2048,768]{0,1:T(8,128)} %get-tuple-element.79, f32[2048]{0:T(1024)S(1)} %get-tuple-element.84, f32[2048]{0:T(1024)S(1)} %get-tuple-element.83, f32[768]{0:T(1024)S(1)} %convert_element_type.154, ...), kind=kOutput, calls=%fused_computation.11 | convolution fusion | flops 2428497152 | bytes 16939008 | tf_op jit(solution)/shard_map/ta,ba->tb/dot_general | solution.py:44
  373.4 9.2 all-reduce.8
  382.7 10.6 %add_convert_fusion = bf16[2048,768]{0,1:T(8,128)(2,1)S(1)} fusion(f32[2048,768]{0,1:T(8,128)} %get-tuple-element.80, f32[2048,768]{0,1:T(8,128)} %get-tuple-element.96, f32[2048,768]{0,1:T(8,128)} %get-tuple-element.97, f32[2048,768]{0,1:T(8,128)} %get-tuple-element.79, f32[2048]{0:T(1024)S(1)} %convert_multiply_fusion.3, ...), kind=kLoop, calls=%fused_computation.13 | loop fusion | flops 33030144 | bytes 28347392 | tf_op jit(solution)/shard_map/convert_element_type | solution.py:188
  393.4 1.6 copy-done.11
  395.0 4.1 convolution_convert_fusion
  399.2 7.8 convolution_convert_fusion.1
  407.1 7.7 convolution_convert_fusion.2
  415.1 6.6 convolution_convert_fusion.3
  421.8 36.7 %reduce-scatter.10.cloned.1.call-done = bf16[512,768]{1,0:T(8,128)(2,1)} async-done(((bf16[2048,768]{1,0:T(8,128)(2,1)}), bf16[512,768]{1,0:T(8,128)(2,1)}) %reduce-scatter.10.cloned.1.call-update) | async-done | bytes 786448 | tf_op jit(solution)/shard_map/reduce_scatter | solution.py:190
  458.4 1.9 fusion.20
  460.4 60.7 %reduce-scatter.8.cloned.1.call-done = bf16[512,768]{1,0:T(8,128)(2,1)} async-done(((bf16[2048,768]{1,0:T(8,128)(2,1)}), bf16[512,768]{1,0:T(8,128)(2,1)}) %reduce-scatter.8.cloned.1.call-update) | async-done | bytes 786448 | tf_op jit(solution)/shard_map/reduce_scatter | solution.py:165
  521.0 3.6 fusion.18
  524.6 2.4 fusion.40
  527.1 2.4 multiply_reduce_fusion.5
  529.5 1.4 multiply_convert_fusion.4
  530.9 1.4 copy.50
  532.3 6.9 fusion.34
  539.3 0.9 copy-done.15
  540.2 2.4 fusion.49
  542.9 7.7 multiply_reduce_fusion
  550.6 7.1 multiply_convert_fusion
  557.8 1.1 multiply_convert_fusion.3
  558.9 0.9 copy-done.12
  559.8 1.0 convolution_bitcast_fusion.1
  560.8 2.0 multiply_convert_fusion.2
  562.9 0.9 copy-done.17
  563.8 1.0 convolution_bitcast_fusion
  564.8 2.4 pad_maximum_fusion
  567.2 14.1 %psum.39 = f32[768]{0:T(1024)} all-reduce(f32[768]{0:T(1024)S(1)} %get-tuple-element.51), channel_id=1, replica_groups=mesh['dp'=8,'mp'=4] {'dp'}, use_global_device_ids=true, to_apply=%region_36.37 | all-reduce | flops 768 | bytes 6144 | tf_op jit(solution)/shard_map/psum | solution.py:204
  581.3 1.6 convert_element_type.183
  583.0 18.3 %reduce-scatter.18.cloned.1.call-done = bf16[96,768]{1,0:T(8,128)(2,1)} async-done(((bf16[768,768]{1,0:T(8,128)(2,1)}), bf16[96,768]{1,0:T(8,128)(2,1)}) %reduce-scatter.18.cloned.1.call-update) | async-done | bytes 147472 | tf_op jit(solution)/shard_map/reduce_scatter | solution.py:197
  601.3 1.8 convert_element_type.181
  603.1 2.5 fusion.39
  605.6 0.8 fusion.38
  606.5 2.5 fusion.31
  609.0 39.5 %all-reduce.6 = (f32[768]{0:T(1024)S(1)}, f32[768]{0:T(1024)S(1)}, f32[768]{0:T(1024)S(1)}) all-reduce(f32[768]{0:T(1024)S(1)} %get-tuple-element.60, f32[768]{0:T(1024)S(1)} %get-tuple-element.56, f32[768]{0:T(1024)S(1)} %get-tuple-element.58), channel_id=4, replica_groups=mesh['dp'=8,'mp'=4] {'dp','mp'}, use_global_device_ids=true, to_apply=%region_26.27.clone | all-reduce | flops 2304 | bytes 18432
  650.2 3.1 fusion.30
  653.3 52.8 %reduce-scatter.16.cloned.1.call-done = f32[24,768]{1,0:T(8,128)} async-done(((f32[768,768]{1,0:T(8,128)}), f32[24,768]{1,0:T(8,128)}) %reduce-scatter.16.cloned.1.call-update) | async-done | bytes 73744 | tf_op jit(solution)/shard_map/reduce_scatter | solution.py:245
  706.1 104.7 %reduce-scatter.14.cloned.1.call-done = f32[24,768]{1,0:T(8,128)} async-done(((f32[768,768]{1,0:T(8,128)}), f32[24,768]{1,0:T(8,128)}) %reduce-scatter.14.cloned.1.call-update) | async-done | bytes 73744 | tf_op jit(solution)/shard_map/reduce_scatter | solution.py:243
  810.8 112.0 %reduce-scatter.12.cloned.1.call-done = f32[2,24,768]{2,1,0:T(8,128)} async-done(((f32[2,768,768]{2,1,0:T(8,128)}), f32[2,24,768]{2,1,0:T(8,128)}) %reduce-scatter.12.cloned.1.call-update) | async-done | bytes 147472 | tf_op jit(solution)/shard_map/reduce_scatter | solution.py:242
  (96 shorter events, 7.9 us)
Async XLA Ops:
  7.2 60.5 %all-gather.8.cloned.1.call-start = ((), (), s32[]{:S(2)}) async-start(), calls=%async_computation.7 | async-start | bytes 1216512 | tf_op jit(solution)/shard_map/all_gather | solution.py:120
  7.9 119.2 %all-gather.10.cloned.1.call-start = ((), (), s32[]{:S(2)}) async-start(), calls=%async_computation.8 | async-start | bytes 2433024 | tf_op jit(solution)/shard_map/all_gather | solution.py:119
  8.7 174.2 %all-gather.12.cloned.1.call-start = ((), (), s32[]{:S(2)}) async-start(), calls=%async_computation.9 | async-start | bytes 1216512 | tf_op jit(solution)/shard_map/all_gather | solution.py:122
  9.4 198.3 %all-gather.16.cloned.1.call-start = ((), (), s32[]{:S(2)}) async-start(), calls=%async_computation.11 | async-start | bytes 1327104 | tf_op jit(solution)/shard_map/all_gather | solution.py:126
  10.0 263.2 %all-gather.14.cloned.1.call-start = ((), (), s32[]{:S(2)}) async-start(), calls=%async_computation.10 | async-start | bytes 3932160 | tf_op jit(solution)/shard_map/all_gather | solution.py:149
  57.1 70.0 %copy-start.4 = (bf16[512,768]{1,0:T(8,128)(2,1)S(1)}, bf16[512,768]{1,0:T(8,128)(2,1)}, u32[]{:S(2)}) copy-start(bf16[512,768]{1,0:T(8,128)(2,1)} %param.20) | copy-start | bytes 2359300
  129.5 2.7 copy-start.2
  132.2 2.1 copy-start.6
  134.3 4.6 copy-start
  134.3 4.6 copy-start.8
  185.4 273.0 %copy-start.1 = (f32[512,768]{1,0:T(8,128)}, f32[512,768]{1,0:T(8,128)S(1)}, u32[]{:S(2)}) copy-start(f32[512,768]{1,0:T(8,128)S(1)} %get-tuple-element.95) | copy-start | bytes 4718596
  185.4 2.8 copy-start.18
  186.8 115.7 %all-gather.18.cloned.1.call-start = ((), (), s32[]{:S(2)}) async-start(), calls=%async_computation.12 | async-start | bytes 1327104 | tf_op jit(solution)/shard_map/all_gather | solution.py:127
  187.4 175.4 %all-gather.20.cloned.1.call-start = ((), (), s32[]{:S(2)}) async-start(), calls=%async_computation.14 | async-start | bytes 3932160 | tf_op jit(solution)/shard_map/all_gather | solution.py:168
  188.1 270.3 %reduce-scatter.10.cloned.1.call-start = ((), (), s32[]{:S(2)}) async-start(), calls=%async_computation.15 | async-start | bytes 3932160 | tf_op jit(solution)/shard_map/reduce_scatter | solution.py:190
  382.7 12.3 %copy-start.20 = (bf16[768,768]{1,0:T(8,128)(2,1)S(1)}, bf16[768,768]{1,0:T(8,128)(2,1)}, u32[]{:S(2)}) copy-start(bf16[768,768]{1,0:T(8,128)(2,1)} %all-gather.16.cloned.1.call-done) | copy-start | bytes 3538948
  393.4 1.7 copy-start.11
  399.1 121.9 %reduce-scatter.8.cloned.1.call-start = ((), (), s32[]{:S(2)}) async-start(), calls=%async_computation.13 | async-start | bytes 3932160 | tf_op jit(solution)/shard_map/reduce_scatter | solution.py:165
  407.0 174.3 %reduce-scatter.20.cloned.1.call-start = ((), (), s32[]{:S(2)}) async-start(), calls=%async_computation.20 | async-start | bytes 1327104 | tf_op jit(solution)/shard_map/reduce_scatter | solution.py:200
  414.8 186.5 %reduce-scatter.18.cloned.1.call-start = ((), (), s32[]{:S(2)}) async-start(), calls=%async_computation.19 | async-start | bytes 1327104 | tf_op jit(solution)/shard_map/reduce_scatter | solution.py:197
  421.7 284.4 %reduce-scatter.16.cloned.1.call-start = ((), (), s32[]{:S(2)}) async-start(), calls=%async_computation.18 | async-start | bytes 2433024 | tf_op jit(solution)/shard_map/reduce_scatter | solution.py:245
  527.0 283.8 %reduce-scatter.14.cloned.1.call-start = ((), (), s32[]{:S(2)}) async-start(), calls=%async_computation.17 | async-start | bytes 2433024 | tf_op jit(solution)/shard_map/reduce_scatter | solution.py:243
  532.3 6.9 copy-start.10
  532.3 7.8 copy-start.5
  539.3 0.9 copy-start.15
  540.2 2.8 copy-start.9
  542.6 380.3 %reduce-scatter.12.cloned.1.call-start = ((), (), s32[]{:S(2)}) async-start(), calls=%async_computation.16 | async-start | bytes 4866048 | tf_op jit(solution)/shard_map/reduce_scatter | solution.py:242
  550.6 7.1 copy-start.3
  558.9 0.9 copy-start.12
  558.9 1.9 copy-start.7
  562.9 0.9 copy-start.17
  567.2 38.4 %copy-start.13 = (bf16[12,64,512]{2,1,0:T(8,128)(2,1)S(1)}, bf16[12,64,512]{2,1,0:T(8,128)(2,1)}, u32[]{:S(2)}) copy-start(bf16[12,64,512]{2,1,0:T(8,128)(2,1)} %copy-done.12) | copy-start | bytes 2359300
  601.3 4.3 copy-start.19
  603.1 3.3 copy-start.14
  603.1 3.3 copy-start.16
Sparse Core Ops, SparseCore 0:
  10.8 56.8 all-gather.7
  70.7 56.2 all-gather.9
  129.9 52.9 all-gather.11
  184.6 22.9 all-gather.15
  209.7 63.4 all-gather.13
  275.0 22.6 all-gather.17
  299.3 63.4 all-gather.19
  399.3 59.1 reduce-scatter.9
  460.7 60.2 reduce-scatter.7
  524.1 36.7 reduce-scatter.19
  564.5 36.7 reduce-scatter.17
  607.0 99.0 reduce-scatter.15
  712.8 97.9 reduce-scatter.13
  816.7 106.0 reduce-scatter.11
where the time goes:
time: 939 us; the launch traced here: 930 us
  waiting for transfers between devices  640 us (68%)
  blocking collectives  114 us (12%)
  matrix products  105 us (11%)
  other arithmetic  39.8 us (4%)
  between operations  15.5 us (2%)
  local copies, waits for them, and re-layouts  14.3 us (2%)
    reduce_scatter x1, waiting for transfers between devices, on_device(): lax.psum_scatter(grad_qk, ('dp', 'mp'), scatter_dimension=1, tiled=True)  112 us
    reduce_scatter x1, waiting for transfers between devices, on_device(): lax.psum_scatter(grad_value_proj, ('dp', 'mp'), scatter_dimension=0, tile...  105 us
    unnamed x2, blocking collectives  81.6 us
    all_gather x1, waiting for transfers between devices, on_device(): normed_all = lax.all_gather(feedforward_normed, 'mp', axis=0, tiled=True)  65.5 us
    reduce_scatter x1, waiting for transfers between devices, on_device(): lax.psum_scatter(matmul(squeezed_rows, fc2_rows).astype(jnp.bfloat16), 'm...  60.7 us
    all_gather x1, waiting for transfers between devices, on_device(): piece = lax.all_gather(cotangent, 'mp', axis=0, tiled=True)  60.3 us
    all_gather x1, waiting for transfers between devices, on_device(): lax.all_gather(qk_weight, ('dp', 'mp'), axis=1, tiled=True)  55.9 us
    reduce_scatter x1, waiting for transfers between devices, on_device(): lax.psum_scatter(grad_out_proj, ('dp', 'mp'), scatter_dimension=0, tiled=...  52.8 us
  transfers between devices with their start and end apart: 14, of which 12 were waited for; matrix products, arithmetic and copies ran while one was open for 14% of the time, Pallas kernels for 0%

commit v1 on v0

v1 whole, which is shorter than its diff:
```python
import jax
import jax.numpy as jnp
from jax import lax
from jax.sharding import PartitionSpec as P

D = 768
HEADS = 12
HEAD_DIM = 64
HIDDEN = 3072
SHORT = 256
EPSILON = 1e-05
NEGATIVE = -1e30
BOTH = ("dp", "mp")


def apply_norm(values):
    mean_value = jnp.mean(values, axis=-1, keepdims=True)
    spread = jnp.mean(values * values, axis=-1, keepdims=True) - mean_value * mean_value
    inverse_deviation = lax.rsqrt(spread + EPSILON)
    return ((values - mean_value) * inverse_deviation, inverse_deviation)


def norm_backward(incoming_gradient, centered_rows, inverse_deviation, gain_vector):
    scaled_rows = incoming_gradient * gain_vector
    first_item = jnp.mean(scaled_rows, axis=-1, keepdims=True)
    second_item = jnp.mean(scaled_rows * centered_rows, axis=-1, keepdims=True)
    return inverse_deviation * (scaled_rows - first_item - centered_rows * second_item)


def matmul(left, right):
    return jnp.dot(left, right, preferred_element_type=jnp.float32)


def matmul_left_t(left, right):
    return jnp.einsum("ta,tb->ab", left, right, preferred_element_type=jnp.float32)


def matmul_right_t(left, right):
    return jnp.einsum("ta,ba->tb", left, right, preferred_element_type=jnp.float32)


def scores_of(queries, keys_all, bucket_id):
    total = queries.shape[0]
    scale = HEAD_DIM ** (-0.5)
    scores = (
        jnp.einsum("qhe,khe->hqk", queries, keys_all, preferred_element_type=jnp.float32) * scale
    )
    length = jnp.where(bucket_id == 0, SHORT, total).astype(jnp.int32)
    query_pos = lax.broadcasted_iota(jnp.int32, (total, total), 0)
    key_pos = lax.broadcasted_iota(jnp.int32, (total, total), 1)
    permitted = (key_pos <= query_pos) & (query_pos // length == key_pos // length)
    return jnp.where(permitted[None], scores, NEGATIVE)


def attend(queries, keys_all, values_all, bucket_id):
    scores = scores_of(queries, keys_all, bucket_id)
    peak = jnp.max(scores, axis=-1, keepdims=True)
    weights = jnp.exp(scores - peak)
    totals = jnp.sum(weights, axis=-1, keepdims=True)
    probs = (weights / totals).astype(jnp.bfloat16)
    outputs = jnp.einsum("hqk,khe->qhe", probs, values_all, preferred_element_type=jnp.float32)
    return (outputs, peak + jnp.log(totals))


def attend_back(queries, keys_all, values_all, grad_out, logsums, bucket_id):
    scale = HEAD_DIM ** (-0.5)
    scores = scores_of(queries, keys_all, bucket_id)
    probs = jnp.exp(scores - logsums)
    rounded = probs.astype(jnp.bfloat16)
    grad_probs = jnp.einsum(
        "qhe,khe->hqk", grad_out, values_all, preferred_element_type=jnp.float32
    )
    centre = jnp.sum(probs * grad_probs, axis=-1, keepdims=True)
    grad_scores = (probs * (grad_probs - centre)).astype(jnp.bfloat16)
    grad_queries = (
        jnp.einsum("hqk,khe->qhe", grad_scores, keys_all, preferred_element_type=jnp.float32)
        * scale
    )
    grad_keys = (
        jnp.einsum("hqk,qhe->khe", grad_scores, queries, preferred_element_type=jnp.float32) * scale
    )
    grad_values = jnp.einsum("hqk,qhe->khe", rounded, grad_out, preferred_element_type=jnp.float32)
    return (grad_queries, grad_keys, grad_values)


def on_device(n_dp, n_mp):
    def body(
        tokens,
        bucket,
        attn_gain,
        qk_weight,
        value_weight,
        inner_gain,
        out_weight,
        ffn_gain,
        fc1_weight,
        ffn_inner_gain,
        fc2_weight,
        cotangent,
    ):
        bf16, f32 = jnp.bfloat16, jnp.float32
        n = n_dp * n_mp
        rows = value_weight.shape[0]
        ffn_rows, ffn_cols = fc1_weight.shape
        gains = jnp.stack([attn_gain, inner_gain, ffn_gain], axis=1)
        gains = jnp.pad(gains, ((0, 0), (0, 125)))
        attn_shard = jnp.concatenate(
            [qk_weight[0], qk_weight[1], value_weight, out_weight, gains], axis=1
        )
        attn_all = lax.all_gather(attn_shard, BOTH, axis=0, tiled=True)
        ffn_shard = jnp.stack([fc1_weight, fc2_weight.T])
        ffn_all = lax.all_gather(ffn_shard, BOTH, axis=0)
        inner_all = lax.all_gather(ffn_inner_gain, "mp", axis=0, tiled=True)
        ffn_all = (
            ffn_all.reshape(n_dp, n_mp, 2, ffn_rows, ffn_cols)
            .transpose(2, 0, 3, 1, 4)
            .reshape(2, D, HIDDEN)
        )
        fc1, fc2_t = ffn_all[0], ffn_all[1]
        hidden_gain = inner_all.astype(f32)
        qkv = attn_all[:, : 3 * D]
        out_all = attn_all[:, 3 * D : 4 * D]
        input_gain = attn_all[:, 4 * D].astype(f32)
        middle_gain = attn_all[:, 4 * D + 1].astype(f32)
        feedforward_gain = attn_all[:, 4 * D + 2].astype(f32)
        bucket_id = bucket[0]
        total = tokens.shape[0]
        head_layout = (total, HEADS, HEAD_DIM)

        input_rows = tokens.astype(f32)
        input_centered, input_inverse = apply_norm(input_rows)
        input_normed = (input_centered * input_gain).astype(bf16)
        joined = matmul(input_normed, qkv).astype(bf16)
        queries = joined[:, :D].reshape(head_layout)
        keys_all = joined[:, D : 2 * D].reshape(head_layout)
        values_all = joined[:, 2 * D :].reshape(head_layout)
        attended_rows, logsums = attend(queries, keys_all, values_all, bucket_id)
        attended_rows = attended_rows.reshape(total, D)
        middle_centered, middle_inverse = apply_norm(attended_rows)
        middle_normed = (middle_centered * middle_gain).astype(bf16)
        hidden_residual = input_rows + matmul(middle_normed, out_all)
        ff_centered, ff_inverse = apply_norm(hidden_residual)
        ff_normed = (ff_centered * feedforward_gain).astype(bf16)

        hidden = matmul(ff_normed, fc1)
        half_erf = 0.5 + 0.5 * lax.erf(hidden * (0.5**0.5))
        activated = hidden * half_erf
        slope = half_erf + hidden * jnp.exp(-0.5 * hidden * hidden) * 0.3989422804014327
        hidden_centered, hidden_inverse = apply_norm(activated)
        squeezed = (hidden_centered * hidden_gain).astype(bf16)
        output = (hidden_residual + matmul_right_t(squeezed, fc2_t)).astype(bf16)

        grad_squeezed = matmul(cotangent, fc2_t)
        grad_fc2_t = matmul_left_t(cotangent, squeezed)
        hidden_gain_gradient = jnp.sum(grad_squeezed * hidden_centered, axis=0)
        grad_hidden = (
            norm_backward(grad_squeezed, hidden_centered, hidden_inverse, hidden_gain) * slope
        ).astype(bf16)
        grad_fc1 = matmul_left_t(ff_normed, grad_hidden)
        ff_normed_gradient = matmul_right_t(grad_hidden, fc1)
        ffn_grads = (
            jnp.stack([grad_fc1, grad_fc2_t])
            .astype(bf16)
            .reshape(2, n_dp, ffn_rows, n_mp, ffn_cols)
            .transpose(1, 3, 0, 2, 4)
            .reshape(n, 2, ffn_rows, ffn_cols)
        )
        ffn_share = lax.psum_scatter(ffn_grads, BOTH, scatter_dimension=0).astype(f32)
        grad_inner = lax.psum_scatter(hidden_gain_gradient, "mp", scatter_dimension=0, tiled=True)
        grad_inner = lax.psum(grad_inner, "dp")

        residual_gradient = cotangent.astype(f32) + norm_backward(
            ff_normed_gradient, ff_centered, ff_inverse, feedforward_gain
        )
        ff_gain_gradient = jnp.sum(ff_normed_gradient * ff_centered, axis=0)
        grad_branch = residual_gradient.astype(bf16)
        grad_out_proj = matmul_left_t(middle_normed, grad_branch)
        middle_gradient = matmul_right_t(grad_branch, out_all)
        middle_gain_gradient = jnp.sum(middle_gradient * middle_centered, axis=0)
        grad_attended = (
            norm_backward(middle_gradient, middle_centered, middle_inverse, middle_gain)
            .astype(bf16)
            .reshape(head_layout)
        )
        grads = attend_back(queries, keys_all, values_all, grad_attended, logsums, bucket_id)
        grad_joined = jnp.concatenate([g.reshape(total, D).astype(bf16) for g in grads], axis=1)
        grad_qkv = matmul_left_t(input_normed, grad_joined)
        input_normed_gradient = matmul_right_t(grad_joined, qkv)
        token_gradient = residual_gradient + norm_backward(
            input_normed_gradient, input_centered, input_inverse, input_gain
        )
        input_gain_gradient = jnp.sum(input_normed_gradient * input_centered, axis=0)
        gain_grads = jnp.stack(
            [input_gain_gradient, middle_gain_gradient, ff_gain_gradient], axis=1
        )
        gain_grads = jnp.pad(gain_grads, ((0, 0), (0, 125)))
        attn_grads = jnp.concatenate([grad_qkv, grad_out_proj, gain_grads], axis=1).astype(bf16)
        attn_share = lax.psum_scatter(
            attn_grads, BOTH, scatter_dimension=0, tiled=True
        ).astype(f32)
        return (
            output,
            token_gradient,
            attn_share[:, 4 * D],
            jnp.stack([attn_share[:, :D], attn_share[:, D : 2 * D]]),
            attn_share[:, 2 * D : 3 * D],
            attn_share[:, 4 * D + 1],
            attn_share[:, 3 * D : 4 * D],
            attn_share[:, 4 * D + 2],
            ffn_share[0],
            grad_inner,
            ffn_share[1].T,
        )

    return body


def solution(mesh):
    flat = P(BOTH)
    rows = P(BOTH, None)
    pair = P(None, BOTH, None)
    placed = (
        rows, flat, flat, pair, rows, flat, rows, flat,
        P("dp", "mp"), P("mp"), P("mp", "dp"), rows,
    )
    given = (
        rows, rows, flat, pair, rows, flat, rows, flat,
        P("dp", "mp"), P("mp"), P("mp", "dp"),
    )
    return jax.shard_map(
        on_device(mesh.shape["dp"], mesh.shape["mp"]),
        mesh=mesh,
        in_specs=placed,
        out_specs=given,
        check_vma=False,
    )
```

time: 939 us -> 527 us (0.56)
  waiting for transfers between devices: 640 us -> 246 us
  blocking collectives: 114 us -> 44.9 us
  local copies, waits for them, and re-layouts: 14.3 us -> 79.8 us
  matrix products: 105 us -> 78.7 us
  other arithmetic: 39.8 us -> 53.2 us
    reduce_scatter x7 -> x1, waiting for transfers between devices: 385 us -> 136 us  [body(): lax.psum_scatter(ffn_grads, BOTH, scatter_dimension=0).astype(f32)]
    all_gather x7 -> x2, waiting for transfers between devices: 251 us -> 110 us  [the longest x1 62.6 us: body(): ffn_all = lax.all_gather(ffn_shard, BOTH, axis=0)]
    unnamed x2 -> x1, blocking collectives: 81.6 us -> 17.3 us
    dot_general x6 -> x4, matrix products: 37.2 us -> 14.5 us  [matmul(): return jnp.dot(left, right, preferred_element_type=jnp.float32)]
    another operation x0 -> x7, local copies, waits for them, and re-layouts: none -> 19.9 us  [the longest x2 19.7 us: body(): jnp.stack([grad_fc1, grad_fc2_t]).astype(bf16)]
    psum x3 -> x1, blocking collectives: 32.5 us -> 12.9 us  [body(): grad_inner = lax.psum(grad_inner, 'dp')]
    slice x0 -> x7, local copies, waits for them, and re-layouts: none -> 14.8 us  [the longest x1 10.8 us: body(): fc1, fc2_t = (ffn_all[0], ffn_all[1])]
    all_gather x0 -> x1, blocking collectives: none -> 14.7 us  [body(): inner_all = lax.all_gather(ffn_inner_gain, 'mp', axis=0, tiled=True)]
  transfers between devices with their start and end apart: 14 -> 4, of which waited for: 12 -> 3; matrix products, arithmetic and copies ran while one was open for 14% -> 19% of each run, Pallas kernels for 0% -> 0%
where the time goes in v1:
time: 527 us; the launch traced here: 519 us
  waiting for transfers between devices  246 us (47%)
  local copies, waits for them, and re-layouts  79.8 us (15%)
  matrix products  78.7 us (15%)
  other arithmetic  53.2 us (10%)
  blocking collectives  44.9 us (9%)
  between operations  16.1 us (3%)
    reduce_scatter x1, waiting for transfers between devices, body(): lax.psum_scatter(ffn_grads, BOTH, scatter_dimension=0).astype(f32)  136 us
    all_gather x1, waiting for transfers between devices, body(): ffn_all = lax.all_gather(ffn_shard, BOTH, axis=0)  62.6 us
    all_gather x1, waiting for transfers between devices, body(): attn_all = lax.all_gather(attn_shard, BOTH, axis=0, tiled=True)  47.3 us
    dot_general x4, matrix products, matmul_left_t(): jnp.einsum('ta,tb->ab', left, right, preferred_element_type=jnp.float32)  20.5 us
    another operation x2, local copies, waits for them, and re-layouts, body(): jnp.stack([grad_fc1, grad_fc2_t]).astype(bf16)  19.7 us
    dot_general x4, matrix products, matmul_right_t(): jnp.einsum('ta,ba->tb', left, right, preferred_element_type=jnp.float32)  18.5 us
    unnamed x1, blocking collectives  17.3 us
    all_gather x1, blocking collectives, body(): inner_all = lax.all_gather(ffn_inner_gain, 'mp', axis=0, tiled=True)  14.7 us
  transfers between devices with their start and end apart: 4, of which 3 were waited for; matrix products, arithmetic and copies ran while one was open for 19% of the time, Pallas kernels for 0%

profile of v1, /device:TPU:0, one launch (start us, length us, event | category | flops | bytes accessed | tf_op | source)
XLA Modules:
  0.0 518.9 jit_solution(3220191441501213428)
XLA Ops:
  7.2 0.7 pad_maximum_fusion.6
  8.0 0.8 bitcast_dynamic-update-slice_fusion.1
  8.8 0.8 bitcast_dynamic-update-slice_fusion
  9.6 0.8 constant_dynamic-update-slice_fusion.2
  10.3 0.8 constant_dynamic-update-slice_fusion.1
  11.1 0.7 copy-done.20
  11.9 1.7 pad_maximum_fusion.3
  14.3 0.7 reshape.311
  15.0 14.7 %all-gather.1 = bf16[4,1,768]{2,1,0:T(2,128)(2,1)S(1)} all-gather(bf16[1,1,768]{2,1,0:T(2,128)(2,1)S(1)} %reshape.311), channel_id=1, replica_groups=mesh['dp'=8,'mp'=4] {'mp'}, dimensions={0}, use_global_device_ids=true | all-gather | bytes 7680 | tf_op jit(solution)/shard_map/all_gather | solution.py:113
  30.0 1.5 convert_reduce_fusion
  31.5 0.3 fusion.37
  31.7 47.3 %all-gather.5.cloned.1.call-done = bf16[768,3200]{1,0:T(8,128)(2,1)} async-done(((bf16[24,3200]{1,0:T(8,128)(2,1)}), bf16[768,3200]{1,0:T(8,128)(2,1)}) %all-gather.5.cloned.1.call-update) | async-done | bytes 4915216 | tf_op jit(solution)/shard_map/all_gather | solution.py:110
  79.0 1.6 convert_reduce_fusion.1
  80.6 4.4 convolution_convert_fusion.3
  85.7 1.2 copy.77
  86.9 2.1 fusion.17
  89.0 2.6 fusion
  91.6 2.0 copy-done
  93.6 3.9 fusion.60
  97.5 0.5 copy.81
  98.1 2.5 fusion.55
  100.7 62.6 %all-gather.7.cloned.1.call-done = bf16[64,96,768]{2,1,0:T(8,128)(2,1)} async-done(((bf16[2,96,768]{2,1,0:T(8,128)(2,1)}), bf16[64,96,768]{2,1,0:T(8,128)(2,1)}) %all-gather.7.cloned.1.call-update) | async-done | bytes 9437200 | tf_op jit(solution)/shard_map/all_gather | solution.py:112
  163.3 12.4 %copy.102 = bf16[8,4,2,96,768]{4,1,3,0,2:T(4,128)(2,1)} copy(bf16[8,4,2,96,768]{4,3,2,1,0:T(8,128)(2,1)} %bitcast.95) | data formatting | bytes 18874368 | tf_op jit(solution)/shard_map/reshape | solution.py:115
  175.7 10.8 %fusion.57 = (bf16[1,8,96,4,768]{4,3,2,1,0:T(4,128)(2,1)}, bf16[1,8,96,4,768]{4,3,2,1,0:T(4,128)(2,1)}) fusion(bf16[2,8,96,4,768]{4,3,2,1,0:T(4,128)(2,1)} %bitcast.90), kind=kLoop, calls=%fused_computation.138 | loop fusion | bytes 18874368 | tf_op jit(solution)/shard_map/slice | solution.py:119
  186.4 3.5 copy.99
  190.2 1.0 copy.100
  191.3 3.8 fusion.54
  195.2 3.8 fusion.11
  199.0 13.4 %fusion.8 = bf16[512,3072]{1,0:T(8,128)(2,1)S(1)} fusion(f32[512,3072]{1,0:T(8,128)S(1)} %get-tuple-element.60, f32[3072,512]{0,1:T(8,128)S(1)} %get-tuple-element.61, f32[512,3072]{1,0:T(8,128)S(1)} %get-tuple-element.35, f32[512]{0:T(512)S(1)} %broadcast_multiply_fusion, f32[512]{0:T(512)S(1)} %broadcast_multiply_fusion.1, f32[3072]{0:T(1024)S(1)} %bitcast.116, ...), kind=kLoop, calls=%fused_computation.18 | loop fusion | flops 26738688 | bytes 22040576 | tf_op jit(solution)/shard_map/convert_element_type | solution.py:158
  212.4 3.0 multiply_reduce_fusion.3
  215.4 2.0 multiply_add_fusion.1
  217.4 2.0 convolution_convert_fusion.4
  219.4 3.0 multiply_reduce_fusion.4
  222.3 1.3 multiply_convert_fusion.4
  223.7 1.4 copy.84
  225.1 6.5 %fusion.34 = bf16[12,64,512]{2,1,0:T(8,128)(2,1)S(1)} fusion(bf16[512,12,64]{0,2,1:T(8,128)(2,1)S(1)} %bitcast.105, f32[12,512]{1,0:T(8,128)S(1)} %log_add_fusion, f32[12,512,512]{1,2,0:T(8,128)} %copy-done, pred[512,512]{0,1:T(8,128)(4,1)S(1)} %fusion.37), kind=kOutput, calls=%fused_computation.75 | convolution fusion | flops 415629312 | bytes 14442496 | tf_op jit(solution)/shard_map/hqk,qhe->khe/dot_general | solution.py:82
  231.6 9.7 %multiply_reduce_fusion = (f32[12,512]{1,0:T(8,128)S(1)}, f32[12,512,512]{1,2,0:T(8,128)}) fusion(f32[12,512]{1,0:T(8,128)S(1)} %log_add_fusion, f32[12,512,512]{1,2,0:T(8,128)} %copy-done, pred[512,512]{0,1:T(8,128)(4,1)S(1)} %fusion.37, bf16[512,12,64]{0,2,1:T(8,128)(2,1)S(1)} %bitcast.106, bf16[512,12,64]{0,2,1:T(8,128)(2,1)S(1)} %bitcast.104), kind=kOutput, calls=%fused_computation.1 | convolution fusion | flops 418375680 | bytes 27049984 | tf_op jit(solution)/shard_map/qhe,khe->hqk/dot_general | solution.py:70
  241.3 7.3 %multiply_convert_fusion = bf16[12,512,512]{1,2,0:T(8,128)(2,1)S(1)} fusion(f32[12,512,512]{1,2,0:T(8,128)} %get-tuple-element.65, f32[12,512]{1,0:T(8,128)S(1)} %get-tuple-element.64, f32[12,512]{1,0:T(8,128)S(1)} %log_add_fusion, f32[12,512,512]{1,2,0:T(8,128)S(1)} %bitcast.88, pred[512,512]{0,1:T(8,128)(4,1)S(1)} %fusion.37), kind=kLoop, calls=%fused_computation | loop fusion | flops 18874368 | bytes 31768576 | tf_op jit(solution)/shard_map/convert_element_type | solution.py:74
  248.6 2.0 multiply_convert_fusion.2
  250.7 1.1 multiply_convert_fusion.3
  251.9 4.1 convolution_convert_fusion.2
  256.0 4.8 fusion.31
  261.0 4.9 fusion.15
  266.0 1.1 copy-done.19
  267.1 7.8 %fusion.16 = bf16[768,3072]{0,1:T(8,128)(2,1)} fusion(bf16[512,768]{1,0:T(8,128)(2,1)S(1)} %copy-done.19, f32[512,3072]{1,0:T(8,128)} %copy-done.6, f32[3072]{0:T(1024)S(1)} %bitcast.117, f32[512]{0:T(512)S(1)} %get-tuple-element.48, f32[512]{0:T(512)S(1)} %get-tuple-element.47), kind=kOutput, calls=%fused_computation.35 | convolution fusion | flops 2424569856 | bytes 11812864 | tf_op jit(solution)/shard_map/ta,tb->ab/dot_general | solution.py:35
  274.9 6.9 %copy.90 = bf16[768,3072]{1,0:T(8,128)(2,1)} copy(bf16[768,3072]{0,1:T(8,128)(2,1)} %fusion.16) | data formatting | bytes 9437184 | tf_op jit(solution)/shard_map/ta,tb->ab/dot_general | solution.py:35
  281.9 10.0 %stack.70 = bf16[1,8,96,4,768]{4,3,2,1,0:T(4,128)(2,1)} reshape(bf16[768,3072]{1,0:T(8,128)(2,1)} %copy.90) | data formatting | bytes 9437184 | tf_op jit(solution)/shard_map/stack | solution.py:162
  291.8 6.6 %convolution_convert_fusion.1 = bf16[768,3072]{1,0:T(8,128)(2,1)} fusion(bf16[512,3072]{1,0:T(8,128)(2,1)} %copy-done.13, f32[512,768]{1,0:T(8,128)S(1)} %copy-done.15, f32[768]{0:T(1024)S(1)} %get-tuple-element.16, f32[512]{0:T(512)S(1)} %get-tuple-element.50, f32[512]{0:T(512)S(1)} %get-tuple-element.49), kind=kOutput, calls=%fused_computation.32 | convolution fusion | flops 2419851264 | bytes 9444352 | tf_op jit(solution)/shard_map/ta,tb->ab/dot_general | solution.py:35
  298.4 9.7 %stack.69 = bf16[1,8,96,4,768]{4,3,2,1,0:T(4,128)(2,1)} reshape(bf16[768,3072]{1,0:T(8,128)(2,1)} %convolution_convert_fusion.1) | data formatting | bytes 9437184 | tf_op jit(solution)/shard_map/stack | solution.py:162
  308.2 9.6 %maximum_bitcast_fusion = bf16[8,4,2,96,768]{4,1,3,0,2:T(4,128)(2,1)} fusion(bf16[1,8,96,4,768]{4,3,2,1,0:T(4,128)(2,1)} %stack.70, bf16[1,8,96,4,768]{4,3,2,1,0:T(4,128)(2,1)} %stack.69), kind=kLoop, calls=%fused_computation.11 | loop fusion | flops 4718592 | bytes 18874368 | tf_op jit(solution)/shard_map/transpose | solution.py:165
  317.8 9.2 %copy.91 = bf16[8,4,2,96,768]{4,3,2,1,0:T(8,128)(2,1)} copy(bf16[8,4,2,96,768]{4,1,3,0,2:T(4,128)(2,1)} %maximum_bitcast_fusion) | data formatting | bytes 18874368 | tf_op jit(solution)/shard_map/transpose | solution.py:165
  327.1 0.6 copy-done.23
  327.7 0.6 dynamic-slice.1
  328.9 17.3 %all-reduce.3 = f32[3072]{0:T(1024)S(1)} all-reduce(f32[3072]{0:T(1024)S(1)} %get-tuple-element.11), channel_id=5, replica_groups=mesh['dp'=8,'mp'=4] {'mp'}, use_global_device_ids=true, to_apply=%region_25.26.clone | all-reduce | flops 3072 | bytes 24576
  346.3 12.9 %psum.7 = f32[768]{0:T(1024)} all-reduce(f32[768]{0:T(1024)S(1)} %dynamic-slice.2), channel_id=1, replica_groups=mesh['dp'=8,'mp'=4] {'dp'}, use_global_device_ids=true, to_apply=%region_26.27 | all-reduce | flops 768 | bytes 6144 | tf_op jit(solution)/shard_map/psum | solution.py:170
  359.2 3.2 fusion.30
  362.4 7.8 %add_convert_fusion = bf16[512,768]{1,0:T(8,128)(2,1)} fusion(f32[512,768]{1,0:T(8,128)S(1)} %copy-done.16, bf16[768,3072]{1,0:T(8,128)(2,1)} %bitcast.100, f32[512,3072]{1,0:T(8,128)} %copy-done.6, f32[3072]{0:T(1024)S(1)} %bitcast.118, f32[512]{0:T(512)S(1)} %get-tuple-element.48, f32[512]{0:T(512)S(1)} %get-tuple-element.47), kind=kOutput, calls=%fused_computation.68 | convolution fusion | flops 2422996992 | bytes 13385728 | tf_op jit(solution)/shard_map/ta,ba->tb/dot_general | solution.py:39
  370.2 0.9 convert_element_type.146
  371.1 0.7 slice_reduce_fusion
  371.9 0.7 pad_maximum_fusion.4
  372.5 1.4 fusion.59
  374.0 136.1 %reduce-scatter.5.cloned.1.call-done = bf16[1,2,96,768]{3,2,1,0:T(8,128)(2,1)} async-done(((bf16[32,2,96,768]{3,2,1,0:T(8,128)(2,1)}), bf16[1,2,96,768]{3,2,1,0:T(8,128)(2,1)}) %reduce-scatter.5.cloned.1.call-update) | async-done | bytes 294928 | tf_op jit(solution)/shard_map/reduce_scatter | solution.py:168
  510.1 1.0 convert_element_type.147
  511.1 0.8 slice_bitcast_fusion
  (94 shorter events, 2.2 us)
Async XLA Ops:
  7.2 71.9 %all-gather.5.cloned.1.call-start = ((), (), s32[]{:S(2)}) async-start(), calls=%async_computation.2 | async-start | bytes 5068800 | tf_op jit(solution)/shard_map/all_gather | solution.py:110
  11.1 0.7 copy-start.20
  11.8 151.5 %all-gather.7.cloned.1.call-start = ((), (), s32[]{:S(2)}) async-start(), calls=%async_computation.4 | async-start | bytes 9732096 | tf_op jit(solution)/shard_map/all_gather | solution.py:112
  13.6 356.6 %reduce-scatter.7.cloned.1.call-start = ((), (), s32[]{:S(2)}) async-start(), calls=%async_computation.5 | async-start | bytes 5068800
  85.4 3.5 copy-start.2
  85.7 3.3 copy-start.4
  89.0 4.6 copy-start
  89.0 4.6 copy-start.9
  100.6 111.7 %copy-start.14 = (f32[512,768]{1,0:T(8,128)}, f32[512,768]{1,0:T(8,128)S(1)}, u32[]{:S(2)}) copy-start(f32[512,768]{1,0:T(8,128)S(1)} %get-tuple-element.59) | copy-start | bytes 4718596
  186.4 3.8 copy-start.1
  191.2 3.9 copy-start.8
  191.3 3.9 copy-start.17
  195.1 3.8 copy-start.6
  212.3 3.0 copy-start.13
  212.4 3.0 copy-start.18
  225.1 6.5 %copy-start.10 = (bf16[512,768]{0,1:T(8,128)(2,1)S(1)}, bf16[512,768]{0,1:T(8,128)(2,1)}, u32[]{:S(2)}) copy-start(bf16[512,768]{0,1:T(8,128)(2,1)} %copy.77) | copy-start | bytes 2359300
  225.1 16.2 %slice-start = ((s8[12582912]{0:T(1024)(128)(4,1)}), s8[4194304]{0:T(1024)(128)(4,1)S(1)}, s32[]{:S(2)}) async-start(s8[12582912]{0:T(1024)(128)(4,1)} %bitcast.87), calls=%async_computation.6 | async-start | bytes 8388608
  225.1 16.2 %slice-start.1 = ((s8[12582912]{0:T(1024)(128)(4,1)}), s8[4194304]{0:T(1024)(128)(4,1)S(1)}, s32[]{:S(2)}) async-start(s8[12582912]{0:T(1024)(128)(4,1)} %bitcast.87), calls=%async_computation.7 | async-start | bytes 8388608
  231.6 20.2 %copy-start.22 = (bf16[12,64,512]{2,1,0:T(8,128)(2,1)}, bf16[12,64,512]{2,1,0:T(8,128)(2,1)S(1)}, u32[]{:S(2)}) copy-start(bf16[12,64,512]{2,1,0:T(8,128)(2,1)S(1)} %fusion.34) | copy-start | bytes 2359300
  231.6 9.7 %slice-start.2 = ((s8[12582912]{0:T(1024)(128)(4,1)}), s8[4194304]{0:T(1024)(128)(4,1)S(1)}, s32[]{:S(2)}) async-start(s8[12582912]{0:T(1024)(128)(4,1)} %bitcast.87), calls=%async_computation.8 | async-start | bytes 8388608
  241.3 7.3 %copy-start.5 = (bf16[512,768]{0,1:T(8,128)(2,1)S(1)}, bf16[512,768]{0,1:T(8,128)(2,1)}, u32[]{:S(2)}) copy-start(bf16[512,768]{0,1:T(8,128)(2,1)} %copy-done.4) | copy-start | bytes 2359300
  248.6 2.0 copy-start.3
  248.6 7.3 %slice-start.3 = ((s8[4915200]{0:T(1024)(128)(4,1)}), s8[4194304]{0:T(1024)(128)(4,1)S(1)}, s32[]{:S(2)}) async-start(s8[4915200]{0:T(1024)(128)(4,1)} %bitcast.113), calls=%async_computation.9 | async-start | bytes 8388608
  250.7 1.2 copy-start.21
  250.7 1.2 copy-start.11
  250.7 5.3 %slice-start.4 = ((s8[4915200]{0:T(1024)(128)(4,1)}), s8[720896]{0:T(1024)(128)(4,1)S(1)}, s32[]{:S(2)}) async-start(s8[4915200]{0:T(1024)(128)(4,1)} %bitcast.113), calls=%async_computation.10 | async-start | bytes 1441792
  256.0 5.1 copy-start.7
  266.0 1.1 copy-start.19
  266.0 244.1 %reduce-scatter.5.cloned.1.call-start = ((), (), s32[]{:S(2)}) async-start(), calls=%async_computation.3 | async-start | bytes 9732096 | tf_op jit(solution)/shard_map/reduce_scatter | solution.py:168
  281.9 10.0 %copy-start.15 = (f32[512,768]{1,0:T(8,128)S(1)}, f32[512,768]{1,0:T(8,128)}, u32[]{:S(2)}) copy-start(f32[512,768]{1,0:T(8,128)} %copy-done.14) | copy-start | bytes 4718596
  327.0 0.7 copy-start.23
  327.0 32.2 %copy-start.12 = (bf16[512,768]{1,0:T(8,128)(2,1)S(1)}, bf16[512,768]{1,0:T(8,128)(2,1)}, u32[]{:S(2)}) copy-start(bf16[512,768]{1,0:T(8,128)(2,1)} %param.12) | copy-start | bytes 2359300
  359.2 3.2 copy-start.16
Sparse Core Ops, SparseCore 0:
  11.9 67.0 all-gather.4
  82.4 80.8 all-gather.6
  266.1 102.5 reduce-scatter.6
  375.5 134.5 reduce-scatter.4

commit v2 on v1

v2 whole, which is shorter than its diff:
```python
import jax
import jax.numpy as jnp
from jax import lax
from jax.experimental import pallas as pl
from jax.experimental.pallas import tpu as pltpu
from jax.sharding import PartitionSpec as P

D = 768
HEADS = 12
HEAD_DIM = 64
HIDDEN = 3072
SHORT = 256
EPSILON = 1e-05
NEGATIVE = -1e30
PAIRS = HEADS // 2
PAIR = 2 * HEAD_DIM
TILE = 256
BOTH = ("dp", "mp")
BF16, F32 = jnp.bfloat16, jnp.float32
VMEM_BYTES = 60 * 1024 * 1024


def dot(left, right):
    return jnp.dot(left, right, preferred_element_type=F32)


def dot_nt(left, right):
    return lax.dot_general(left, right, (((1,), (1,)), ((), ())), preferred_element_type=F32)


def dot_tn(left, right):
    return lax.dot_general(left, right, (((0,), (0,)), ((), ())), preferred_element_type=F32)


def apply_norm(values):
    mean_value = jnp.mean(values, axis=-1, keepdims=True)
    spread = jnp.mean(values * values, axis=-1, keepdims=True) - mean_value * mean_value
    inverse = lax.rsqrt(spread + EPSILON)
    return (values - mean_value) * inverse, inverse


def norm_backward(incoming, centered, inverse, gain):
    scaled = incoming * gain
    first = jnp.mean(scaled, axis=-1, keepdims=True)
    second = jnp.mean(scaled * centered, axis=-1, keepdims=True)
    return inverse * (scaled - first - centered * second)


def causal_bias():
    key_pos = lax.broadcasted_iota(jnp.int32, (TILE, TILE), 0)
    query_pos = lax.broadcasted_iota(jnp.int32, (TILE, TILE), 1)
    return jnp.where(key_pos <= query_pos, 0.0, NEGATIVE).astype(F32)


def lane_half(rows):
    return lax.broadcasted_iota(jnp.int32, (rows, PAIR), 1) // HEAD_DIM


def tiles(total, body):
    def step(i, carry):
        body(pl.ds(pl.multiple_of(i * TILE, TILE), TILE))
        return carry

    lax.fori_loop(0, total // TILE, step, 0)


def attn_forward_kernel(
    bucket, x, w, wo, gains, qkv, lse, o, h, c, out_t, bias
):
    total = x.shape[0]
    input_gain, middle_gain, ff_gain = gains[0:1], gains[1:2], gains[2:3]

    def project(rows):
        centered, _ = apply_norm(x[rows].astype(F32))
        normed = (centered * input_gain).astype(BF16)
        for part in range(3):
            result = dot(normed, w[:, part * D : (part + 1) * D]).astype(BF16)
            for j in range(PAIRS):
                qkv[part * PAIRS + j, rows] = result[:, j * PAIR : (j + 1) * PAIR]

    tiles(total, project)
    bias[...] = causal_bias()
    across = jnp.where(bucket[0] == 0, NEGATIVE, 0.0).astype(F32)

    def heads(j, carry):
        scaled = qkv[j] * jnp.asarray(HEAD_DIM**-0.5, BF16)
        keys = qkv[PAIRS + j]
        values_t = jnp.transpose(qkv[2 * PAIRS + j])
        half = lane_half(total)
        for side in range(2):
            queries = jnp.where(half == side, scaled, jnp.zeros_like(scaled))
            mine = values_t[side * HEAD_DIM : (side + 1) * HEAD_DIM]
            for block in range(total // TILE):
                cut = slice(block * TILE, (block + 1) * TILE)
                own = dot_nt(keys[cut], queries[cut]) + bias[...]
                if block:
                    before = dot_nt(keys[: block * TILE], queries[cut]) + across
                    scores = jnp.concatenate([before, own], axis=0)
                else:
                    scores = own
                peak = jnp.max(scores, axis=0, keepdims=True)
                weights = jnp.exp(scores - peak)
                totals = jnp.sum(weights, axis=0, keepdims=True)
                rows_t = dot(mine[:, : (block + 1) * TILE], weights.astype(BF16))
                out_t[j, side * HEAD_DIM : (side + 1) * HEAD_DIM, cut] = rows_t * (1.0 / totals)
                lse[2 * j + side, :, cut] = peak + jnp.log(totals)
        return carry

    lax.fori_loop(0, PAIRS, heads, 0)
    for j in range(PAIRS):
        o[:, j * PAIR : (j + 1) * PAIR] = jnp.transpose(out_t[j])

    def finish(rows):
        centered, _ = apply_norm(o[rows])
        mixed = (centered * middle_gain).astype(BF16)
        residual = x[rows].astype(F32) + dot(mixed, wo[...])
        h[rows] = residual
        centered, _ = apply_norm(residual)
        c[rows] = (centered * ff_gain).astype(BF16)

    tiles(total, finish)


def vmem(n):
    return [pl.BlockSpec(memory_space=pltpu.VMEM)] * n


def params():
    return pltpu.CompilerParams(vmem_limit_bytes=VMEM_BYTES)


def attn_forward(bucket, x, w, wo, gains):
    total = x.shape[0]
    shape = jax.ShapeDtypeStruct
    return pl.pallas_call(
        attn_forward_kernel,
        out_shape=(
            shape((3 * PAIRS, total, PAIR), BF16),
            shape((HEADS, 1, total), F32),
            shape((total, D), F32),
            shape((total, D), F32),
            shape((total, D), BF16),
        ),
        in_specs=[pl.BlockSpec(memory_space=pltpu.SMEM)] + vmem(4),
        out_specs=tuple(vmem(5)),
        scratch_shapes=[
            pltpu.VMEM((PAIRS, PAIR, total), F32),
            pltpu.VMEM((TILE, TILE), F32),
        ],
        compiler_params=params(),
        name="attn_forward",
    )(bucket, x, w, wo, gains)


def ffn_kernel(
    c, h, cot, w1, w2, gain, out, grad1, grad2, grad_gain, dc, act, slope, back, squeezed, grad_f
):
    total = c.shape[0]
    blocks, _, cols = w1.shape
    units = blocks * cols
    steps = total // TILE

    def lanes(values):
        partial = values[:, 0:128]
        for i in range(1, cols // 128):
            partial = partial + values[:, i * 128 : (i + 1) * 128]
        return partial

    def rows_of(i):
        return pl.ds(pl.multiple_of(i * TILE, TILE), TILE)

    def tile(i, carry):
        rows = rows_of(i)
        zero = jnp.zeros((TILE, 128), F32)

        def first(b, sums):
            hidden = dot(c[rows], w1[b])
            half_erf = 0.5 + 0.5 * lax.erf(hidden * (0.5**0.5))
            active = hidden * half_erf
            act[b, rows] = active
            slope[b, rows] = half_erf + hidden * (
                jnp.exp(-0.5 * hidden * hidden) * 0.3989422804014327
            )
            back[b, rows] = dot(cot[rows], w2[b])
            return sums[0] + lanes(active), sums[1] + lanes(active * active)

        sums = lax.fori_loop(0, blocks, first, (zero, zero))
        mean = jnp.sum(sums[0], axis=1, keepdims=True) * (1.0 / units)
        spread = jnp.sum(sums[1], axis=1, keepdims=True) * (1.0 / units) - mean * mean
        inverse = lax.rsqrt(spread + EPSILON)
        shift = mean * inverse
        out[rows] = jnp.zeros((TILE, D), F32).astype(BF16)
        dc[rows] = h[rows]

        def second(b, sums):
            centered = act[b, rows] * inverse - shift
            incoming = back[b, rows]
            grad_gain[b] += jnp.sum(incoming * centered, axis=0, keepdims=True)
            scaled = incoming * gain[b]
            act[b, rows] = centered
            back[b, rows] = scaled
            z = (centered * gain[b]).astype(BF16)
            squeezed[b, rows] = z
            dc[rows] += dot_nt(z, w2[b])
            return sums[0] + lanes(scaled), sums[1] + lanes(scaled * centered)

        sums = lax.fori_loop(0, blocks, second, (zero, zero))
        out[rows] = dc[rows].astype(BF16)
        first_item = jnp.sum(sums[0], axis=1, keepdims=True) * (1.0 / units) * inverse
        second_item = jnp.sum(sums[1], axis=1, keepdims=True) * (1.0 / units) * inverse
        dc[rows] = jnp.zeros((TILE, D), F32)

        def third(b, carry):
            grad = (back[b, rows] * inverse - first_item - act[b, rows] * second_item) * slope[
                b, rows
            ]
            grad = grad.astype(BF16)
            grad_f[b, rows] = grad
            dc[rows] += dot_nt(grad, w1[b])
            return carry

        lax.fori_loop(0, blocks, third, 0)
        return carry

    grad_gain[...] = jnp.zeros(grad_gain.shape, F32)
    lax.fori_loop(0, steps, tile, 0)

    def fourth(b, carry):
        grad1[b] = dot_tn(c[...], grad_f[b]).astype(BF16)
        grad2[b] = dot_tn(cot[...], squeezed[b]).astype(BF16)
        return carry

    lax.fori_loop(0, blocks, fourth, 0)


def feed_forward(c, h, cot, w1, w2, gain):
    total = c.shape[0]
    blocks, _, cols = w1.shape
    shape = jax.ShapeDtypeStruct
    return pl.pallas_call(
        ffn_kernel,
        out_shape=(
            shape((total, D), BF16),
            shape((blocks, D, cols), BF16),
            shape((blocks, D, cols), BF16),
            shape((blocks, 1, cols), F32),
            shape((total, D), F32),
        ),
        in_specs=vmem(6),
        out_specs=tuple(vmem(5)),
        scratch_shapes=[
            pltpu.VMEM((blocks, total, cols), F32),
            pltpu.VMEM((blocks, total, cols), F32),
            pltpu.VMEM((blocks, total, cols), F32),
            pltpu.VMEM((blocks, total, cols), BF16),
            pltpu.VMEM((blocks, total, cols), BF16),
        ],
        compiler_params=params(),
        name="feed_forward",
    )(c, h, cot, w1, w2, gain)


def out_backward_kernel(dc, cot, h, o, wo, gains, dh, do, grad_wo, gain_rows, dy, mixed):
    total = dc.shape[0]
    middle_gain, ff_gain = gains[1:2], gains[2:3]
    gain_rows[...] = jnp.zeros(gain_rows.shape, F32)

    def part(rows):
        incoming = dc[rows]
        centered, inverse = apply_norm(h[rows])
        gain_rows[2:3] += jnp.sum(incoming * centered, axis=0, keepdims=True)
        residual = cot[rows].astype(F32) + norm_backward(incoming, centered, inverse, ff_gain)
        dh[rows] = residual
        branch = residual.astype(BF16)
        dy[rows] = branch
        incoming = dot_nt(branch, wo[...])
        centered, inverse = apply_norm(o[rows])
        gain_rows[1:2] += jnp.sum(incoming * centered, axis=0, keepdims=True)
        mixed[rows] = (centered * middle_gain).astype(BF16)
        result = norm_backward(incoming, centered, inverse, middle_gain).astype(BF16)
        for j in range(PAIRS):
            do[j, rows] = result[:, j * PAIR : (j + 1) * PAIR]

    tiles(total, part)
    grad_wo[...] = dot_tn(mixed[...], dy[...]).astype(BF16)


def out_backward(dc, cot, h, o, wo, gains):
    total = dc.shape[0]
    shape = jax.ShapeDtypeStruct
    return pl.pallas_call(
        out_backward_kernel,
        out_shape=(
            shape((total, D), F32),
            shape((PAIRS, total, PAIR), BF16),
            shape((D, D), BF16),
            shape((8, D), F32),
        ),
        in_specs=vmem(6),
        out_specs=tuple(vmem(4)),
        scratch_shapes=[pltpu.VMEM((total, D), BF16), pltpu.VMEM((total, D), BF16)],
        compiler_params=params(),
        name="out_backward",
    )(dc, cot, h, o, wo, gains)


def attn_backward_kernel(
    bucket, x, qkv, do, lse, gains, joined, grad_w, grad_q_t, bias, normed
):
    total = x.shape[0]
    input_gain = gains[0:1]

    def norm(rows):
        centered, _ = apply_norm(x[rows].astype(F32))
        normed[rows] = (centered * input_gain).astype(BF16)

    tiles(total, norm)
    bias[...] = causal_bias()
    across = jnp.where(bucket[0] == 0, NEGATIVE, 0.0).astype(F32)
    scale = HEAD_DIM**-0.5

    def heads(j, carry):
        scaled = qkv[j] * jnp.asarray(scale, BF16)
        keys = qkv[PAIRS + j]
        keys_t = jnp.transpose(keys)
        values = qkv[2 * PAIRS + j]
        grads = do[j]
        half = lane_half(total)
        grad_keys = [jnp.zeros((TILE, PAIR), F32) for _ in range(total // TILE)]
        grad_values = [jnp.zeros((TILE, PAIR), F32) for _ in range(total // TILE)]
        for side in range(2):
            queries = jnp.where(half == side, scaled, jnp.zeros_like(scaled))
            outs = jnp.where(half == side, grads, jnp.zeros_like(grads))
            keys_side = keys_t[side * HEAD_DIM : (side + 1) * HEAD_DIM]
            for block in range(total // TILE):
                cut = slice(block * TILE, (block + 1) * TILE)
                level = lse[2 * j + side, :, cut]
                parts = []
                centre = jnp.zeros((1, TILE), F32)
                for key_block in range(block + 1):
                    key_cut = slice(key_block * TILE, (key_block + 1) * TILE)
                    scores = dot_nt(keys[key_cut], queries[cut])
                    scores = scores + (bias[...] if key_block == block else across)
                    probs = jnp.exp(scores - level)
                    grad_probs = dot_nt(values[key_cut], outs[cut])
                    centre = centre + jnp.sum(probs * grad_probs, axis=0, keepdims=True)
                    parts.append((probs, grad_probs))
                total_t = jnp.zeros((HEAD_DIM, TILE), F32)
                for key_block in range(block + 1):
                    key_cut = slice(key_block * TILE, (key_block + 1) * TILE)
                    probs, grad_probs = parts[key_block]
                    grad_scores = (probs * (grad_probs - centre)).astype(BF16)
                    total_t = total_t + dot(keys_side[:, key_cut], grad_scores)
                    grad_keys[key_block] = grad_keys[key_block] + dot(grad_scores, queries[cut])
                    grad_values[key_block] = grad_values[key_block] + dot(
                        probs.astype(BF16), outs[cut]
                    )
                grad_q_t[j, side * HEAD_DIM : (side + 1) * HEAD_DIM, cut] = (
                    total_t * scale
                ).astype(BF16)
        joined[j] = jnp.transpose(grad_q_t[j])
        for block in range(total // TILE):
            cut = slice(block * TILE, (block + 1) * TILE)
            joined[PAIRS + j, cut] = grad_keys[block].astype(BF16)
            joined[2 * PAIRS + j, cut] = grad_values[block].astype(BF16)
        return carry

    lax.fori_loop(0, PAIRS, heads, 0)

    def weight(k, carry):
        right = jnp.concatenate([joined[2 * k], joined[2 * k + 1]], axis=1)
        cut = pl.ds(pl.multiple_of(k * 2 * PAIR, 2 * PAIR), 2 * PAIR)
        grad_w[:, cut] = dot_tn(normed[...], right).astype(BF16)
        return carry

    lax.fori_loop(0, 3 * PAIRS // 2, weight, 0)


def attn_backward(bucket, x, qkv, do, lse, gains):
    total = x.shape[0]
    shape = jax.ShapeDtypeStruct
    return pl.pallas_call(
        attn_backward_kernel,
        out_shape=(
            shape((3 * PAIRS, total, PAIR), BF16),
            shape((D, 3 * D), BF16),
        ),
        in_specs=[pl.BlockSpec(memory_space=pltpu.SMEM)] + vmem(5),
        out_specs=tuple(vmem(2)),
        scratch_shapes=[
            pltpu.VMEM((PAIRS, PAIR, total), BF16),
            pltpu.VMEM((TILE, TILE), F32),
            pltpu.VMEM((total, D), BF16),
        ],
        compiler_params=params(),
        name="attn_backward",
    )(bucket, x, qkv, do, lse, gains)


def input_backward_kernel(x, joined, w, dh, gains, grad_x, gain_row):
    total = x.shape[0]
    input_gain = gains[0:1]
    gain_row[...] = jnp.zeros(gain_row.shape, F32)

    def part(rows):
        incoming = jnp.zeros((TILE, D), F32)
        for third in range(3):
            left = jnp.concatenate(
                [joined[third * PAIRS + j, rows] for j in range(PAIRS)], axis=1
            )
            incoming = incoming + dot_nt(left, w[:, third * D : (third + 1) * D])
        centered, inverse = apply_norm(x[rows].astype(F32))
        gain_row[0:1] += jnp.sum(incoming * centered, axis=0, keepdims=True)
        grad_x[rows] = dh[rows] + norm_backward(incoming, centered, inverse, input_gain)

    tiles(total, part)


def input_backward(x, joined, w, dh, gains):
    total = x.shape[0]
    shape = jax.ShapeDtypeStruct
    return pl.pallas_call(
        input_backward_kernel,
        out_shape=(shape((total, D), F32), shape((8, D), F32)),
        in_specs=vmem(5),
        out_specs=tuple(vmem(2)),
        compiler_params=params(),
        name="input_backward",
    )(x, joined, w, dh, gains)


def on_device(n_dp, n_mp):
    def body(
        tokens,
        bucket,
        attn_gain,
        qk_weight,
        value_weight,
        inner_gain,
        out_weight,
        ffn_gain,
        fc1_weight,
        ffn_inner_gain,
        fc2_weight,
        cotangent,
    ):
        n = n_dp * n_mp
        ffn_rows, ffn_cols = fc1_weight.shape
        gains = jnp.stack([attn_gain, inner_gain, ffn_gain], axis=1)
        gains = jnp.pad(gains, ((0, 0), (0, 125)))
        attn_shard = jnp.concatenate(
            [qk_weight[0], qk_weight[1], value_weight, out_weight, gains], axis=1
        )
        attn_all = lax.all_gather(attn_shard, BOTH, axis=0, tiled=True)
        ffn_shard = jnp.stack([fc1_weight, fc2_weight.T])
        ffn_all = lax.all_gather(ffn_shard, BOTH, axis=0)
        inner_all = lax.all_gather(ffn_inner_gain, "mp", axis=0, tiled=True)
        ffn_all = (
            ffn_all.reshape(n_dp, n_mp, 2, ffn_rows, ffn_cols)
            .transpose(2, 1, 0, 3, 4)
            .reshape(2, n_mp, D, ffn_cols)
        )
        hidden_gain = inner_all.astype(F32).reshape(n_mp, 1, ffn_cols)
        qkv_weight = attn_all[:, : 3 * D]
        wo = attn_all[:, 3 * D : 4 * D]
        rows8 = jnp.pad(attn_all[:, 4 * D : 4 * D + 3].astype(F32).T, ((0, 5), (0, 0)))

        qkv, lse, o, h, c = attn_forward(bucket, tokens, qkv_weight, wo, rows8)
        output, grad1, grad2, grad_inner, dc = feed_forward(
            c, h, cotangent, ffn_all[0], ffn_all[1], hidden_gain
        )
        ffn_grads = (
            jnp.stack([grad1, grad2])
            .reshape(2, n_mp, n_dp, ffn_rows, ffn_cols)
            .transpose(2, 1, 0, 3, 4)
            .reshape(n, 2, ffn_rows, ffn_cols)
        )
        ffn_share = lax.psum_scatter(ffn_grads, BOTH, scatter_dimension=0).astype(F32)
        grad_inner = lax.psum_scatter(
            grad_inner.reshape(-1), "mp", scatter_dimension=0, tiled=True
        )
        grad_inner = lax.psum(grad_inner, "dp")
        dh, do, grad_wo, gain_rows = out_backward(dc, cotangent, h, o, wo, rows8)
        joined, grad_qkv = attn_backward(bucket, tokens, qkv, do, lse, rows8)
        token_gradient, gain_row = input_backward(tokens, joined, qkv_weight, dh, rows8)
        gain_grads = jnp.stack([gain_row[0], gain_rows[1], gain_rows[2]], axis=1)
        gain_grads = jnp.pad(gain_grads, ((0, 0), (0, 125))).astype(BF16)
        attn_grads = jnp.concatenate([grad_qkv, grad_wo, gain_grads], axis=1)
        attn_share = lax.psum_scatter(
            attn_grads, BOTH, scatter_dimension=0, tiled=True
        ).astype(F32)
        return (
            output,
            token_gradient,
            attn_share[:, 4 * D],
            jnp.stack([attn_share[:, :D], attn_share[:, D : 2 * D]]),
            attn_share[:, 2 * D : 3 * D],
            attn_share[:, 4 * D + 1],
            attn_share[:, 3 * D : 4 * D],
            attn_share[:, 4 * D + 2],
            ffn_share[0],
            grad_inner,
            ffn_share[1].T,
        )

    return body


def solution(mesh):
    flat = P(BOTH)
    rows = P(BOTH, None)
    pair = P(None, BOTH, None)
    placed = (
        rows, flat, flat, pair, rows, flat, rows, flat,
        P("dp", "mp"), P("mp"), P("mp", "dp"), rows,
    )
    given = (
        rows, rows, flat, pair, rows, flat, rows, flat,
        P("dp", "mp"), P("mp"), P("mp", "dp"),
    )
    return jax.shard_map(
        on_device(mesh.shape["dp"], mesh.shape["mp"]),
        mesh=mesh,
        in_specs=placed,
        out_specs=given,
        check_vma=False,
    )
```

time: 527 us -> 505 us (0.958); the launches traced: 519 us -> 504 us
  Pallas kernels: 0 us -> 81.6 us
  matrix products: 78.7 us -> 0 us
  waiting for transfers between devices: 246 us -> 301 us
  local copies, waits for them, and re-layouts: 79.8 us -> 42.7 us
  other arithmetic: 53.2 us -> 19.2 us
    pallas_call x0 -> x5, Pallas kernels: none -> 81.6 us  [the longest x1 31.3 us: feed_forward(): pl.pallas_call(ffn_kernel, out_shape=(shape((total, D), BF16), shape((blo...]
    dot_general x18 -> x0, matrix products: 78.7 us -> none  [the longest x4 20.5 us: matmul_left_t(): jnp.einsum('ta,tb->ab', left, right, preferred_element_type=jnp.float32)]
    unnamed x5, waiting for transfers between devices: 0.07 us -> 54.1 us
    convert_element_type x6 -> x1, other arithmetic: 24.6 us -> 1 us  [body(): lax.psum_scatter(ffn_grads, BOTH, scatter_dimension=0).astype(F32)]
    another operation x6 -> x2, local copies, waits for them, and re-layouts: 19.9 us -> 1.59 us  [body(): gain_grads = jnp.stack([gain_row[0], gain_rows[1], gain_rows[2]], axis=1)]
    unnamed x68 -> x17, local copies, waits for them, and re-layouts: 13.7 us -> 5.93 us
    dot_general x1 -> x0, local copies, waits for them, and re-layouts: 6.94 us -> none  [matmul_left_t(): jnp.einsum('ta,tb->ab', left, right, preferred_element_type=jnp.float32)]
    reshape x2 -> x1, local copies, waits for them, and re-layouts: 12.8 us -> 8.16 us  [body(): ffn_all.reshape(n_dp, n_mp, 2, ffn_rows, ffn_cols).transpose(2, 1, 0, 3, 4)]
  transfers between devices with their start and end apart: 4 -> 4, of which waited for: 3 -> 4; matrix products, arithmetic and copies ran while one was open for 19% -> 6% of each run, Pallas kernels for 0% -> 3%
where the time goes in v2:
time: 505 us; the launch traced here: 504 us
  waiting for transfers between devices  301 us (60%)
  Pallas kernels  81.6 us (16%)
  blocking collectives  44.5 us (9%)
  local copies, waits for them, and re-layouts  42.7 us (8%)
  other arithmetic  19.2 us (4%)
  between operations  15.1 us (3%)
    reduce_scatter x1, waiting for transfers between devices, body(): lax.psum_scatter(ffn_grads, BOTH, scatter_dimension=0).astype(F32)  138 us
    all_gather x1, waiting for transfers between devices, body(): ffn_all = lax.all_gather(ffn_shard, BOTH, axis=0)  60.3 us
    unnamed x5, waiting for transfers between devices  54.1 us
    all_gather x1, waiting for transfers between devices, body(): attn_all = lax.all_gather(attn_shard, BOTH, axis=0, tiled=True)  48.7 us
    pallas_call x1, Pallas kernels, feed_forward(): pl.pallas_call(ffn_kernel, out_shape=(shape((total, D), BF16), shape((blo...  31.3 us
    pallas_call x1, Pallas kernels, attn_backward(): pl.pallas_call(attn_backward_kernel, out_shape=(shape((3 * PAIRS, total,...  19.9 us
    unnamed x1, blocking collectives  17.2 us
    pallas_call x1, Pallas kernels, attn_forward(): pl.pallas_call(attn_forward_kernel, out_shape=(shape((3 * PAIRS, total, P...  15.8 us
  transfers between devices with their start and end apart: 4, of which 4 were waited for; matrix products, arithmetic and copies ran while one was open for 6% of the time, Pallas kernels for 3%

profile of v2, /device:TPU:0, one launch (start us, length us, event | category | flops | bytes accessed | tf_op | source)
XLA Modules:
  0.0 503.9 jit_solution(7972320199727199988)
XLA Ops:
  7.2 0.0 all-gather.5.cloned.1.call-start
  7.2 0.8 bitcast_dynamic-update-slice_fusion.1
  8.0 0.8 bitcast_dynamic-update-slice_fusion
  8.8 0.7 pad_maximum_fusion.3
  9.5 0.1 copy.52
  9.6 0.8 constant_dynamic-update-slice_fusion.2
  10.3 0.8 constant_dynamic-update-slice_fusion.1
  11.1 0.0 copy-start.1
  11.1 0.7 copy-done.1
  11.8 0.0 all-gather.5.cloned.1.call-update
  11.8 0.0 all-gather.7.cloned.1.call-start
  11.9 1.7 pad_maximum_fusion
  13.6 0.0 all-gather.7.cloned.1.call-update
  13.6 0.0 reduce-scatter.7.cloned.1.call-start
  14.3 0.7 reshape.60
  15.0 14.7 %all-gather.1 = bf16[4,1,768]{2,1,0:T(2,128)(2,1)S(1)} all-gather(bf16[1,1,768]{2,1,0:T(2,128)(2,1)S(1)} %reshape.60), channel_id=1, replica_groups=mesh['dp'=8,'mp'=4] {'mp'}, dimensions={0}, use_global_device_ids=true | all-gather | bytes 7680 | tf_op jit(solution)/shard_map/all_gather | solution.py:457
  29.7 0.6 reshape.62.gain
  30.3 48.7 %all-gather.5.cloned.1.call-done = bf16[768,3200]{1,0:T(8,128)(2,1)} async-done(((bf16[24,3200]{1,0:T(8,128)(2,1)}), bf16[768,3200]{1,0:T(8,128)(2,1)}) %all-gather.5.cloned.1.call-update) | async-done | bytes 4915216 | tf_op jit(solution)/shard_map/all_gather | solution.py:454
  79.0 0.9 slice.85
  80.0 0.1 copy.51
  80.1 4.1 slice.83.w
  84.2 2.4 slice.84.wo
  86.6 0.6 pad_convert_fusion.gains
  87.2 15.8 %attn_forward.1 = (bf16[18,512,128]{2,1,0:T(8,128)(2,1)}, f32[12,1,512]{2,1,0:T(1,128)}, f32[512,768]{1,0:T(8,128)}, f32[512,768]{1,0:T(8,128)}, bf16[512,768]{1,0:T(8,128)(2,1)}) custom-call(s32[1]{0:T(128)S(6)} %copy.59.bucket, bf16[512,768]{1,0:T(8,128)(2,1)} %x.11, bf16[768,2304]{1,0:T(8,128)(2,1)} %slice.83.w, bf16[768,768]{1,0:T(8,128)(2,1)} %slice.84.wo, ...), custom_call_target="tpu_custom_call" | custom-call | tf_op jit(solution)/shard_map/attn_forward/pallas_call | solution.py:135
  103.0 60.3 %all-gather.7.cloned.1.call-done = bf16[64,96,768]{2,1,0:T(8,128)(2,1)} async-done(((bf16[2,96,768]{2,1,0:T(8,128)(2,1)}), bf16[64,96,768]{2,1,0:T(8,128)(2,1)}) %all-gather.7.cloned.1.call-update) | async-done | bytes 9437200 | tf_op jit(solution)/shard_map/all_gather | solution.py:456
  163.3 8.2 %copy.54 = bf16[8,4,2,96,768]{4,3,0,1,2:T(8,128)(2,1)} copy(bf16[8,4,2,96,768]{4,3,2,1,0:T(8,128)(2,1)} %bitcast.45) | data formatting | bytes 18874368 | tf_op jit(solution)/shard_map/reshape | solution.py:459
  171.4 8.1 %fusion.3 = (bf16[1,4,8,96,768]{4,3,2,1,0:T(8,128)(2,1)}, bf16[1,4,8,96,768]{4,3,2,1,0:T(8,128)(2,1)}) fusion(bf16[2,4,8,96,768]{4,3,2,1,0:T(8,128)(2,1)} %bitcast.42), kind=kLoop, calls=%fused_computation.26 | loop fusion | bytes 18874368 | tf_op jit(solution)/shard_map/slice | solution.py:470
  179.6 31.3 %feed_forward.1 = (bf16[512,768]{1,0:T(8,128)(2,1)}, bf16[4,768,768]{2,1,0:T(8,128)(2,1)}, bf16[4,768,768]{2,1,0:T(8,128)(2,1)}, f32[4,1,768]{2,1,0:T(1,128)}, f32[512,768]{1,0:T(8,128)}) custom-call(bf16[512,768]{1,0:T(8,128)(2,1)} %get-tuple-element.29.c, f32[512,768]{1,0:T(8,128)} %get-tuple-element.30.h, bf16[512,768]{1,0:T(8,128)(2,1)} %cot.3, ...), custom_call_target="tpu_custom_call" | custom-call | tf_op jit(solution)/shard_map/feed_forward/pallas_call | solution.py:240
  210.9 7.1 %out_backward.1 = (f32[512,768]{1,0:T(8,128)}, bf16[6,512,128]{2,1,0:T(8,128)(2,1)}, bf16[768,768]{1,0:T(8,128)(2,1)}, f32[8,768]{1,0:T(8,128)}) custom-call(f32[512,768]{1,0:T(8,128)} %get-tuple-element.33.dc, bf16[512,768]{1,0:T(8,128)(2,1)} %cot.3, f32[512,768]{1,0:T(8,128)} %get-tuple-element.30.h, f32[512,768]{1,0:T(8,128)} %get-tuple-element.34.o, ...), custom_call_target="tpu_custom_call" | custom-call | tf_op jit(solution)/shard_map/out_backward/pallas_call | solution.py:291
  218.0 0.7 convert.20
  218.7 19.9 %attn_backward.1 = (bf16[18,512,128]{2,1,0:T(8,128)(2,1)}, bf16[768,2304]{1,0:T(8,128)(2,1)}) custom-call(s32[1]{0:T(128)S(6)} %copy.59.bucket, bf16[512,768]{1,0:T(8,128)(2,1)} %x.11, bf16[18,512,128]{2,1,0:T(8,128)(2,1)} %get-tuple-element.32.qkv, bf16[6,512,128]{2,1,0:T(8,128)(2,1)} %get-tuple-element.35.do, f32[12,1,512]{2,1,0:T(1,128)} %get-tuple-element.36.lse, ...), custom_call_target="tpu_custom_call" | custom-call | tf_op jit(solution)/shard_map/attn_backward/pallas_call | solution.py:382
  238.6 0.0 copy-start
  238.6 7.4 %input_backward.1 = (f32[512,768]{1,0:T(8,128)}, f32[8,768]{1,0:T(8,128)}) custom-call(bf16[512,768]{1,0:T(8,128)(2,1)} %x.11, bf16[18,512,128]{2,1,0:T(8,128)(2,1)} %get-tuple-element.37.joined, bf16[768,2304]{1,0:T(8,128)(2,1)} %slice.83.w, f32[512,768]{1,0:T(8,128)} %get-tuple-element.38.dh, f32[8,768]{1,0:T(8,128)} %pad_convert_fusion.gains), custom_call_target="tpu_custom_call" | custom-call | tf_op jit(solution)/shard_map/input_backward/pallas_call | solution.py:422
  246.1 0.7 slice_bitcast_fusion.5
  246.8 0.8 copy.49
  247.7 0.0 copy-done
  247.7 3.9 fusion.1
  251.5 0.0 reduce-scatter.7.cloned.1.call-update
  251.6 0.0 reduce-scatter.5.cloned.1.call-start
  251.6 8.3 %maximum_bitcast_fusion = bf16[8,4,2,96,768]{4,3,0,1,2:T(8,128)(2,1)} fusion(bf16[1,4,8,96,768]{4,3,2,1,0:T(8,128)(2,1)} %bitcast.47, bf16[1,4,8,96,768]{4,3,2,1,0:T(8,128)(2,1)} %bitcast.46), kind=kLoop, calls=%fused_computation.2 | loop fusion | flops 4718592 | bytes 18874368 | tf_op jit(solution)/shard_map/transpose | solution.py:475
  259.9 8.5 %copy.50 = bf16[8,4,2,96,768]{4,3,2,1,0:T(8,128)(2,1)} copy(bf16[8,4,2,96,768]{4,3,0,1,2:T(8,128)(2,1)} %maximum_bitcast_fusion) | data formatting | bytes 18874368 | tf_op jit(solution)/shard_map/transpose | solution.py:475
  268.4 0.0 copy-start.3
  268.4 0.0 copy-start.2
  268.4 0.0 reduce-scatter.5.cloned.1.call-update
  268.4 0.6 copy-done.3
  269.0 0.6 dynamic-slice.1
  270.3 0.0 copy-done.2
  270.3 17.2 %all-reduce.4 = f32[3072]{0:T(1024)S(1)} all-reduce(f32[3072]{0:T(1024)S(1)} %bitcast.51), channel_id=5, replica_groups=mesh['dp'=8,'mp'=4] {'mp'}, use_global_device_ids=true, to_apply=%region_2.3.clone | all-reduce | flops 3072 | bytes 24576
  287.5 0.1 dynamic-slice.2
  287.6 12.6 %psum.7 = f32[768]{0:T(1024)} all-reduce(f32[768]{0:T(1024)S(1)} %dynamic-slice.2), channel_id=1, replica_groups=mesh['dp'=8,'mp'=4] {'dp'}, use_global_device_ids=true, to_apply=%region_3.4 | all-reduce | flops 768 | bytes 6144 | tf_op jit(solution)/shard_map/psum | solution.py:482
  300.2 54.0 %reduce-scatter.7.cloned.1.call-done = bf16[24,3200]{1,0:T(8,128)(2,1)} async-done(((bf16[768,3200]{1,0:T(8,128)(2,1)}), bf16[24,3200]{1,0:T(8,128)(2,1)}) %reduce-scatter.7.cloned.1.call-update) | async-done | bytes 153616
  354.2 0.9 convert_element_type.16
  355.1 0.7 slice_reduce_fusion
  355.9 0.7 pad_maximum_fusion.1
  356.5 1.4 fusion.4
  358.0 137.5 %reduce-scatter.5.cloned.1.call-done = bf16[1,2,96,768]{3,2,1,0:T(8,128)(2,1)} async-done(((bf16[32,2,96,768]{3,2,1,0:T(8,128)(2,1)}), bf16[1,2,96,768]{3,2,1,0:T(8,128)(2,1)}) %reduce-scatter.5.cloned.1.call-update) | async-done | bytes 294928 | tf_op jit(solution)/shard_map/reduce_scatter | solution.py:478
  495.5 1.0 convert_element_type.17
  496.5 0.8 slice_bitcast_fusion
  (3 shorter events, 0.0 us)
Async XLA Ops:
  7.2 71.9 %all-gather.5.cloned.1.call-start = ((), (), s32[]{:S(2)}) async-start(), calls=%async_computation.2 | async-start | bytes 5068800 | tf_op jit(solution)/shard_map/all_gather | solution.py:454
  11.1 0.7 copy-start.1
  11.8 151.5 %all-gather.7.cloned.1.call-start = ((), (), s32[]{:S(2)}) async-start(), calls=%async_computation.4 | async-start | bytes 9732096 | tf_op jit(solution)/shard_map/all_gather | solution.py:456
  13.6 340.6 %reduce-scatter.7.cloned.1.call-start = ((), (), s32[]{:S(2)}) async-start(), calls=%async_computation.5 | async-start | bytes 5068800
  238.6 9.0 %copy-start = (bf16[768,2304]{1,0:T(8,128)(2,1)S(1)}, bf16[768,2304]{1,0:T(8,128)(2,1)}, u32[]{:S(2)}) copy-start(bf16[768,2304]{1,0:T(8,128)(2,1)} %get-tuple-element.40) | copy-start | bytes 10616836
  251.6 244.0 %reduce-scatter.5.cloned.1.call-start = ((), (), s32[]{:S(2)}) async-start(), calls=%async_computation.3 | async-start | bytes 9732096 | tf_op jit(solution)/shard_map/reduce_scatter | solution.py:478
  268.4 0.7 copy-start.3
  268.4 1.9 copy-start.2
Sparse Core Ops, SparseCore 0:
  11.9 67.0 all-gather.4
  82.4 80.8 all-gather.6
  251.7 102.4 reduce-scatter.6
  360.9 134.5 reduce-scatter.4

commit v3 on v2

--- a/solution.py
+++ b/solution.py
@@ -506,6 +506,632 @@
     return body
 
 
+CORE, ALONG_X, ALONG_Y = 1, 2, 4
+GAIN_LANES = 128
+PAD = 16
+
+
+def assemble(meta, pieces, place):
+    copies = []
+    for flip, ref in pieces:
+        copies += [pltpu.make_async_copy(*triple) for triple in place(meta[0] ^ flip, ref)]
+    for copy in copies:
+        copy.start()
+    return copies
+
+
+def attn_places(shapes):
+    cut = shapes // 2 // 128 * 128
+    whole = [(0, 0, shapes), (ALONG_X, 0, shapes), (ALONG_Y, 0, shapes)]
+    diagonal = ALONG_X | ALONG_Y
+    whole += [(diagonal, 0, cut), (diagonal, cut, shapes - cut)]
+    return whole + [(flip | CORE, at, size) for flip, at, size in whole]
+
+
+def load_attn(meta, pieces, w, sem):
+    rows = pieces[0].shape[0]
+    copies = []
+    for (flip, at, size), ref in zip(attn_places(w.shape[1]), pieces):
+        top = pl.multiple_of((meta[0] ^ flip) * rows, rows)
+        copies.append(
+            pltpu.make_async_copy(ref, w.at[pl.ds(top, rows), at : at + size], sem)
+        )
+    for copy in copies:
+        copy.start()
+    return copies
+
+
+def wait_all(copies):
+    for copy in copies:
+        copy.wait()
+
+
+def fast_forward_kernel(meta, bucket, x, *rest):
+    pieces, rest = rest[:10], rest[10:]
+    qkv, lse, o, h, c, gains, w, out_t, bias, sem = rest
+    copies = load_attn(meta, pieces, w, sem)
+    bias[...] = causal_bias()
+    wait_all(copies)
+    gains[...] = jnp.transpose(w[:, 4 * D :].astype(F32))[0:8]
+    attn_forward_kernel(bucket, x, w, w.at[:, 3 * D : 4 * D], gains, qkv, lse, o, h, c, out_t, bias)
+
+
+def fast_forward(meta, bucket, x, pieces):
+    total = x.shape[0]
+    shape = jax.ShapeDtypeStruct
+    return pl.pallas_call(
+        fast_forward_kernel,
+        out_shape=(
+            shape((3 * PAIRS, total, PAIR), BF16),
+            shape((HEADS, 1, total), F32),
+            shape((total, D), F32),
+            shape((total, D), F32),
+            shape((total, D), BF16),
+            shape((8, D), F32),
+        ),
+        in_specs=smem(2) + vmem(1) + [pl.BlockSpec(memory_space=pl.ANY)] * 10,
+        out_specs=tuple(vmem(6)),
+        scratch_shapes=[
+            pltpu.VMEM((D, 4 * D + GAIN_LANES), BF16),
+            pltpu.VMEM((PAIRS, PAIR, total), F32),
+            pltpu.VMEM((TILE, TILE), F32),
+            pltpu.SemaphoreType.DMA,
+        ],
+        compiler_params=params(),
+        cost_estimate=cost(4.2e9, 10e6),
+        name="attn_forward",
+    )(meta, bucket, x, *pieces)
+
+
+def smem(n):
+    return [pl.BlockSpec(memory_space=pltpu.SMEM)] * n
+
+
+def cost(flops, bytes_accessed):
+    return pl.CostEstimate(
+        flops=int(flops), bytes_accessed=int(bytes_accessed), transcendentals=0
+    )
+
+
+def load_ffn(meta, pieces, w1, w2, sem):
+    blocks, rows = w1.shape[0], pieces[0].shape[2]
+    copies = []
+    for core in range(2):
+        own, from_x, from_y, first, second = pieces[5 * core : 5 * core + 5]
+        for flip, one, two in (
+            (0, own.at[:, 0], own.at[:, 1]),
+            (ALONG_X, from_x.at[:, 0], from_x.at[:, 1]),
+            (ALONG_Y, from_y.at[:, 0], from_y.at[:, 1]),
+            (ALONG_X | ALONG_Y, first, second),
+        ):
+            top = pl.multiple_of((meta[0] ^ (flip | core)) * rows, rows)
+            for k in range(blocks):
+                block = lax.rem(meta[1] + (blocks - k), blocks)
+                for source, target, slot in ((one, w1, 0), (two, w2, 1)):
+                    copies.append(
+                        pltpu.make_async_copy(
+                            source.at[k], target.at[block, pl.ds(top, rows)], sem.at[slot]
+                        )
+                    )
+    for copy in copies:
+        copy.start()
+    return copies
+
+
+def split_rows(meta, values_t, target, rows):
+    for flip in range(8):
+        top = pl.multiple_of((meta[0] ^ flip) * rows, rows)
+        target[flip] = values_t[pl.ds(top, rows)]
+
+
+def order_of(first, second):
+    return [(a, b, a * first | b * second) for a in range(2) for b in range(2)]
+
+
+def fast_ffn_kernel(meta, c, h, cot, gain, *rest):
+    pieces, rest = rest[:10], rest[10:]
+    (out, keep1, send1, keep2, send2, dc) = rest[:6]
+    (w1, w2, act, slope, back, squeezed, grad_f, grad_gain, c_t, cot_t, turned, sem) = rest[6:]
+    blocks, _, cols = w1.shape
+    rows = pieces[0].shape[2]
+    copies = load_ffn(meta, pieces, w1, w2, sem)
+    turned[...] = jnp.transpose(c[...])
+    split_rows(meta, turned, c_t, rows)
+    turned[...] = jnp.transpose(cot[...])
+    split_rows(meta, turned, cot_t, rows)
+    wait_all(copies)
+    ffn_passes(meta, c, h, cot, w1, w2, gain, out, dc, act, slope, back, squeezed, grad_f, grad_gain)
+
+    def fourth(k, carry):
+        block = lax.rem(meta[1] + k, blocks)
+        where = pl.ds(pl.multiple_of(k * rows, rows), rows)
+        for left, right, keep, send, order in (
+            (c_t, grad_f, keep1, send1, order_of(ALONG_X, ALONG_Y)),
+            (cot_t, squeezed, keep2, send2, order_of(ALONG_Y, ALONG_X)),
+        ):
+            for core, target in ((0, keep), (1, send)):
+                stacked = jnp.concatenate([left[flip | core] for _, _, flip in order], axis=0)
+                result = dot(stacked, right[block]).astype(BF16)
+                for i, (a, b, _) in enumerate(order):
+                    target[a, b, where] = result[i * rows : (i + 1) * rows]
+        return carry
+
+    lax.fori_loop(0, blocks, fourth, 0)
+    extra = jnp.concatenate(
+        [grad_gain[lax.rem(meta[1] + k, blocks)] for k in range(blocks)]
+        + [jnp.zeros((PAD - blocks, cols), F32)],
+        axis=0,
+    ).astype(BF16)
+    for target in (keep2, send2):
+        for a in range(2):
+            for b in range(2):
+                target[a, b, blocks * rows :] = extra
+
+
+def ffn_passes(meta, c, h, cot, w1, w2, gain, out, dc, act, slope, back, squeezed, grad_f, grad_gain):
+    total = c.shape[0]
+    blocks, _, cols = w1.shape
+    units = blocks * cols
+
+    def lanes(values):
+        partial = values[:, 0:128]
+        for i in range(1, cols // 128):
+            partial = partial + values[:, i * 128 : (i + 1) * 128]
+        return partial
+
+    def gain_of(b):
+        return gain[lax.rem(meta[1] + (blocks - b), blocks)]
+
+    def tile(i, carry):
+        rows = pl.ds(pl.multiple_of(i * TILE, TILE), TILE)
+        zero = jnp.zeros((TILE, 128), F32)
+
+        def first(b, sums):
+            hidden = dot(c[rows], w1[b])
+            half_erf = 0.5 + 0.5 * lax.erf(hidden * (0.5**0.5))
+            active = hidden * half_erf
+            act[b, rows] = active
+            slope[b, rows] = half_erf + hidden * (
+                jnp.exp(-0.5 * hidden * hidden) * 0.3989422804014327
+            )
+            back[b, rows] = dot(cot[rows], w2[b])
+            return sums[0] + lanes(active), sums[1] + lanes(active * active)
+
+        sums = lax.fori_loop(0, blocks, first, (zero, zero))
+        mean = jnp.sum(sums[0], axis=1, keepdims=True) * (1.0 / units)
+        spread = jnp.sum(sums[1], axis=1, keepdims=True) * (1.0 / units) - mean * mean
+        inverse = lax.rsqrt(spread + EPSILON)
+        shift = mean * inverse
+        dc[rows] = h[rows]
+
+        def second(b, sums):
+            centered = act[b, rows] * inverse - shift
+            incoming = back[b, rows]
+            grad_gain[b] += jnp.sum(incoming * centered, axis=0, keepdims=True)
+            weights = gain_of(b)
+            scaled = incoming * weights
+            act[b, rows] = centered
+            back[b, rows] = scaled
+            z = (centered * weights).astype(BF16)
+            squeezed[b, rows] = z
+            dc[rows] += dot_nt(z, w2[b])
+            return sums[0] + lanes(scaled), sums[1] + lanes(scaled * centered)
+
+        sums = lax.fori_loop(0, blocks, second, (zero, zero))
+        out[rows] = dc[rows].astype(BF16)
+        first_item = jnp.sum(sums[0], axis=1, keepdims=True) * (1.0 / units) * inverse
+        second_item = jnp.sum(sums[1], axis=1, keepdims=True) * (1.0 / units) * inverse
+        dc[rows] = jnp.zeros((TILE, D), F32)
+
+        def third(b, carry):
+            grad = (back[b, rows] * inverse - first_item - act[b, rows] * second_item) * slope[
+                b, rows
+            ]
+            grad = grad.astype(BF16)
+            grad_f[b, rows] = grad
+            dc[rows] += dot_nt(grad, w1[b])
+            return carry
+
+        lax.fori_loop(0, blocks, third, 0)
+        return carry
+
+    grad_gain[...] = jnp.zeros(grad_gain.shape, F32)
+    lax.fori_loop(0, total // TILE, tile, 0)
+
+
+def fast_ffn(meta, c, h, cot, gain, pieces):
+    total = c.shape[0]
+    blocks, _, rows, cols = pieces[0].shape
+    shape = jax.ShapeDtypeStruct
+    size = blocks * rows
+    one, two = shape((2, 2, size, cols), BF16), shape((2, 2, size + PAD, cols), BF16)
+    wide = pltpu.VMEM((blocks, total, cols), F32)
+    narrow = pltpu.VMEM((blocks, total, cols), BF16)
+    return pl.pallas_call(
+        fast_ffn_kernel,
+        out_shape=(shape((total, D), BF16), one, one, two, two, shape((total, D), F32)),
+        in_specs=smem(1) + vmem(4) + [pl.BlockSpec(memory_space=pl.ANY)] * 10,
+        out_specs=tuple(vmem(6)),
+        scratch_shapes=[
+            pltpu.VMEM((blocks, D, cols), BF16),
+            pltpu.VMEM((blocks, D, cols), BF16),
+            wide,
+            wide,
+            wide,
+            narrow,
+            narrow,
+            pltpu.VMEM((blocks, 1, cols), F32),
+            pltpu.VMEM((8, rows, total), BF16),
+            pltpu.VMEM((8, rows, total), BF16),
+            pltpu.VMEM((D, total), BF16),
+            pltpu.SemaphoreType.DMA((2,)),
+        ],
+        compiler_params=params(),
+        cost_estimate=cost(14.5e9, 20e6),
+        name="feed_forward",
+    )(meta, c, h, cot, gain, *pieces)
+
+
+def fast_out_backward_kernel(meta, dc, cot, h, o, gains, *rest):
+    pieces, rest = rest[:10], rest[10:]
+    dh, do, dy, mixed, gain_rows, w, sem = rest
+    copies = load_attn(meta, pieces, w, sem)
+    wait_all(copies)
+    wo = w.at[:, 3 * D : 4 * D]
+    total = dc.shape[0]
+    middle_gain, ff_gain = gains[1:2], gains[2:3]
+    gain_rows[...] = jnp.zeros(gain_rows.shape, F32)
+
+    def part(rows):
+        incoming = dc[rows]
+        centered, inverse = apply_norm(h[rows])
+        gain_rows[0:1] += jnp.sum(incoming * centered, axis=0, keepdims=True)
+        residual = cot[rows].astype(F32) + norm_backward(incoming, centered, inverse, ff_gain)
+        dh[rows] = residual
+        branch = residual.astype(BF16)
+        dy[rows] = branch
+        incoming = dot_nt(branch, wo[...])
+        centered, inverse = apply_norm(o[rows])
+        gain_rows[1:2] += jnp.sum(incoming * centered, axis=0, keepdims=True)
+        mixed[rows] = (centered * middle_gain).astype(BF16)
+        result = norm_backward(incoming, centered, inverse, middle_gain).astype(BF16)
+        for j in range(PAIRS):
+            do[j, rows] = result[:, j * PAIR : (j + 1) * PAIR]
+
+    tiles(total, part)
+
+
+def fast_out_backward(meta, dc, cot, h, o, gains, pieces):
+    total = dc.shape[0]
+    shape = jax.ShapeDtypeStruct
+    return pl.pallas_call(
+        fast_out_backward_kernel,
+        out_shape=(
+            shape((total, D), F32),
+            shape((PAIRS, total, PAIR), BF16),
+            shape((total, D), BF16),
+            shape((total, D), BF16),
+            shape((8, D), F32),
+        ),
+        in_specs=smem(1) + vmem(5) + [pl.BlockSpec(memory_space=pl.ANY)] * 10,
+        out_specs=tuple(vmem(5)),
+        scratch_shapes=[
+            pltpu.VMEM((D, 4 * D + GAIN_LANES), BF16),
+            pltpu.SemaphoreType.DMA,
+        ],
+        compiler_params=params(),
+        cost_estimate=cost(1.2e9, 10e6),
+        name="out_backward",
+    )(meta, dc, cot, h, o, gains, *pieces)
+
+
+def fast_attn_backward_kernel(
+    meta, bucket, x, qkv, do, lse, gains, dy, mixed, gain_rows,
+    joined, keep1, send1, keep2, send2, grad_q_t, bias, normed, normed_t, mixed_t, turned,
+):
+    rows = normed_t.shape[1]
+    attn_backward_passes(bucket, x, qkv, do, lse, gains, joined, grad_q_t, bias, normed)
+    turned[...] = jnp.transpose(normed[...])
+    split_rows(meta, turned, normed_t, rows)
+    turned[...] = jnp.transpose(mixed[...])
+    split_rows(meta, turned, mixed_t, rows)
+    step = 2 * PAIR
+
+    def weight(k, carry):
+        right = jnp.concatenate([joined[2 * k], joined[2 * k + 1]], axis=1)
+
+        def place(keep, send, order, start):
+            cut = pl.ds(pl.multiple_of((k - start) * step, step), step)
+            for core, target in ((0, keep), (1, send)):
+                stacked = jnp.concatenate([normed_t[flip | core] for _, _, flip in order], axis=0)
+                result = dot(stacked, right).astype(BF16)
+                for i, (a, b, _) in enumerate(order):
+                    target[a, b, :rows, cut] = result[i * rows : (i + 1) * rows]
+
+        @pl.when(k < 2 * D // step)
+        def _():
+            place(keep1, send1, order_of(ALONG_X, ALONG_Y), 0)
+
+        @pl.when(k >= 2 * D // step)
+        def _():
+            place(keep2, send2, order_of(ALONG_Y, ALONG_X), 2 * D // step)
+
+        return carry
+
+    lax.fori_loop(0, 3 * D // step, weight, 0)
+    extra = jnp.concatenate([gain_rows[...], jnp.zeros((8, D), F32)], axis=0).astype(BF16)
+    order = order_of(ALONG_Y, ALONG_X)
+    for core, target in ((0, keep2), (1, send2)):
+        stacked = jnp.concatenate([mixed_t[flip | core] for _, _, flip in order], axis=0)
+        result = dot(stacked, dy[...]).astype(BF16)
+        for i, (a, b, _) in enumerate(order):
+            target[a, b, :rows, D:] = result[i * rows : (i + 1) * rows]
+            target[a, b, rows:, :D] = extra
+            target[a, b, rows:, D:] = jnp.zeros((PAD, D), BF16)
+
+
+def attn_backward_passes(bucket, x, qkv, do, lse, gains, joined, grad_q_t, bias, normed):
+    total = x.shape[0]
+    input_gain = gains[0:1]
+
+    def norm(rows):
+        centered, _ = apply_norm(x[rows].astype(F32))
+        normed[rows] = (centered * input_gain).astype(BF16)
+
+    tiles(total, norm)
+    bias[...] = causal_bias()
+    across = jnp.where(bucket[0] == 0, NEGATIVE, 0.0).astype(F32)
+    scale = HEAD_DIM**-0.5
+
+    def heads(j, carry):
+        scaled = qkv[j] * jnp.asarray(scale, BF16)
+        keys = qkv[PAIRS + j]
+        keys_t = jnp.transpose(keys)
+        values = qkv[2 * PAIRS + j]
+        grads = do[j]
+        half = lane_half(total)
+        grad_keys = [jnp.zeros((TILE, PAIR), F32) for _ in range(total // TILE)]
+        grad_values = [jnp.zeros((TILE, PAIR), F32) for _ in range(total // TILE)]
+        for side in range(2):
+            queries = jnp.where(half == side, scaled, jnp.zeros_like(scaled))
+            outs = jnp.where(half == side, grads, jnp.zeros_like(grads))
+            keys_side = keys_t[side * HEAD_DIM : (side + 1) * HEAD_DIM]
+            for block in range(total // TILE):
+                cut = slice(block * TILE, (block + 1) * TILE)
+                level = lse[2 * j + side, :, cut]
+                parts = []
+                centre = jnp.zeros((1, TILE), F32)
+                for key_block in range(block + 1):
+                    key_cut = slice(key_block * TILE, (key_block + 1) * TILE)
+                    scores = dot_nt(keys[key_cut], queries[cut])
+                    scores = scores + (bias[...] if key_block == block else across)
+                    probs = jnp.exp(scores - level)
+                    grad_probs = dot_nt(values[key_cut], outs[cut])
+                    centre = centre + jnp.sum(probs * grad_probs, axis=0, keepdims=True)
+                    parts.append((probs, grad_probs))
+                total_t = jnp.zeros((HEAD_DIM, TILE), F32)
+                for key_block in range(block + 1):
+                    key_cut = slice(key_block * TILE, (key_block + 1) * TILE)
+                    probs, grad_probs = parts[key_block]
+                    grad_scores = (probs * (grad_probs - centre)).astype(BF16)
+                    total_t = total_t + dot(keys_side[:, key_cut], grad_scores)
+                    grad_keys[key_block] = grad_keys[key_block] + dot(grad_scores, queries[cut])
+                    grad_values[key_block] = grad_values[key_block] + dot(
+                        probs.astype(BF16), outs[cut]
+                    )
+                grad_q_t[j, side * HEAD_DIM : (side + 1) * HEAD_DIM, cut] = (
+                    total_t * scale
+                ).astype(BF16)
+        joined[j] = jnp.transpose(grad_q_t[j])
+        for block in range(total // TILE):
+            cut = slice(block * TILE, (block + 1) * TILE)
+            joined[PAIRS + j, cut] = grad_keys[block].astype(BF16)
+            joined[2 * PAIRS + j, cut] = grad_values[block].astype(BF16)
+        return carry
+
+    lax.fori_loop(0, PAIRS, heads, 0)
+
+
+def fast_attn_backward(meta, bucket, x, qkv, do, lse, gains, dy, mixed, gain_rows):
+    total = x.shape[0]
+    rows = D // 8
+    shape = jax.ShapeDtypeStruct
+    one, two = shape((2, 2, rows, 2 * D), BF16), shape((2, 2, rows + PAD, 2 * D), BF16)
+    return pl.pallas_call(
+        fast_attn_backward_kernel,
+        out_shape=(shape((3 * PAIRS, total, PAIR), BF16), one, one, two, two),
+        in_specs=smem(2) + vmem(8),
+        out_specs=tuple(vmem(5)),
+        scratch_shapes=[
+            pltpu.VMEM((PAIRS, PAIR, total), BF16),
+            pltpu.VMEM((TILE, TILE), F32),
+            pltpu.VMEM((total, D), BF16),
+            pltpu.VMEM((8, rows, total), BF16),
+            pltpu.VMEM((8, rows, total), BF16),
+            pltpu.VMEM((D, total), BF16),
+        ],
+        compiler_params=params(),
+        cost_estimate=cost(9e9, 15e6),
+        name="attn_backward",
+    )(meta, bucket, x, qkv, do, lse, gains, dy, mixed, gain_rows)
+
+
+def fast_input_backward_kernel(meta, x, joined, dh, gains, *rest):
+    pieces, rest = rest[:10], rest[10:]
+    grad_x, w, sem = rest
+    total = x.shape[0]
+    input_gain = gains[0:1]
+    wait_all(load_attn(meta, pieces, w, sem))
+
+    def part(rows):
+        incoming = jnp.zeros((TILE, D), F32)
+        for third in range(3):
+            left = jnp.concatenate(
+                [joined[third * PAIRS + j, rows] for j in range(PAIRS)], axis=1
+            )
+            incoming = incoming + dot_nt(left, w[:, third * D : (third + 1) * D])
+        centered, inverse = apply_norm(x[rows].astype(F32))
+        grad_x[rows] = dh[rows] + norm_backward(incoming, centered, inverse, input_gain)
+
+    tiles(total, part)
+
+
+def fast_input_backward(meta, x, joined, dh, gains, pieces):
+    total = x.shape[0]
+    return pl.pallas_call(
+        fast_input_backward_kernel,
+        out_shape=jax.ShapeDtypeStruct((total, D), F32),
+        in_specs=smem(1) + vmem(4) + [pl.BlockSpec(memory_space=pl.ANY)] * 10,
+        out_specs=pl.BlockSpec(memory_space=pltpu.VMEM),
+        scratch_shapes=[
+            pltpu.VMEM((D, 4 * D + GAIN_LANES), BF16),
+            pltpu.SemaphoreType.DMA,
+        ],
+        compiler_params=params(),
+        cost_estimate=cost(1.8e9, 10e6),
+        name="input_backward",
+    )(meta, x, joined, dh, gains, *pieces)
+
+
+def swap(values, flip):
+    return lax.ppermute(values, "dp", [(i, i ^ flip) for i in range(8)])
+
+
+def turn(values, k, n):
+    return lax.ppermute(values, "mp", [(i, (i + k) % n) for i in range(n)])
+
+
+def wide(values):
+    return values.astype(F32)
+
+
+def reduce_rows(keep, send, first, second):
+    other = swap(send, CORE)
+    one = swap((wide(keep[1]) + wide(other[1])).astype(BF16), first)
+    two = swap((wide(keep[0, 1]) + wide(other[0, 1]) + wide(one[1])).astype(BF16), second)
+    return wide(keep[0, 0]) + wide(other[0, 0]) + wide(one[0]) + wide(two)
+
+
+def fast_on_device(n_mp):
+    def body(
+        tokens,
+        bucket,
+        attn_gain,
+        qk_weight,
+        value_weight,
+        inner_gain,
+        out_weight,
+        ffn_gain,
+        fc1_weight,
+        ffn_inner_gain,
+        fc2_weight,
+        cotangent,
+    ):
+        at_dp, at_mp = lax.axis_index("dp"), lax.axis_index("mp")
+        meta = jnp.stack([at_dp, at_mp]).astype(jnp.int32)
+        slim = value_weight.shape[0]
+        rows, cols = fc1_weight.shape
+
+        gains = jnp.stack([attn_gain, inner_gain, ffn_gain], axis=1)
+        gains = jnp.pad(gains, ((0, 0), (0, GAIN_LANES - 3)))
+        shard = jnp.concatenate(
+            [qk_weight[0], qk_weight[1], value_weight, out_weight, gains], axis=1
+        )
+        ring = [turn(shard, k, n_mp) for k in range(n_mp - 1, 0, -1)] + [shard]
+        ring = jnp.concatenate(ring + ring[:-1], axis=0)
+        own = lax.dynamic_slice_in_dim(ring, (n_mp - 1 - at_mp) * slim, n_mp * slim, 0)
+        from_x, from_y = swap(own, ALONG_X), swap(own, ALONG_Y)
+        cut = own.shape[1] // 2 // 128 * 128
+        near = [
+            own,
+            from_x,
+            from_y,
+            swap(from_x[:, :cut], ALONG_Y),
+            swap(from_y[:, cut:], ALONG_X),
+        ]
+        attn_pieces = near + [swap(piece, CORE) for piece in near]
+
+        shard = jnp.concatenate(
+            [fc1_weight, fc2_weight.T, jnp.pad(ffn_inner_gain[None], ((0, PAD - 1), (0, 0)))],
+            axis=0,
+        )
+        ring = [shard] + [turn(shard, k, n_mp) for k in range(1, n_mp)]
+        hidden_gain = jnp.stack([piece[2 * rows] for piece in ring]).astype(F32)[:, None]
+        own = jnp.stack([piece[: 2 * rows].reshape(2, rows, cols) for piece in ring])
+        from_x, from_y = swap(own, ALONG_X), swap(own, ALONG_Y)
+        near = [
+            own,
+            from_x,
+            from_y,
+            swap(from_x[:, 0], ALONG_Y),
+            swap(from_y[:, 1], ALONG_X),
+        ]
+        ffn_pieces = near + [swap(piece, CORE) for piece in near]
+
+        qkv, lse, o, h, c, gains = fast_forward(meta, bucket, tokens, attn_pieces)
+        output, keep1, send1, keep2, send2, dc = fast_ffn(
+            meta, c, h, cotangent, hidden_gain, ffn_pieces
+        )
+        sum1 = reduce_rows(keep1, send1, ALONG_X, ALONG_Y)
+        sum2 = reduce_rows(keep2, send2, ALONG_Y, ALONG_X)
+        size = n_mp * rows
+        blocks = [
+            jnp.concatenate(
+                [
+                    sum1[k * rows : (k + 1) * rows],
+                    sum2[k * rows : (k + 1) * rows],
+                    sum2[size + k : size + k + 1],
+                ],
+                axis=0,
+            )
+            for k in range(n_mp)
+        ]
+        ffn_share = blocks[0]
+        for k in range(1, n_mp):
+            ffn_share = ffn_share + wide(turn(blocks[k].astype(BF16), k, n_mp))
+
+        dh, do, dy, mixed, gain_rows = fast_out_backward(
+            meta, dc, cotangent, h, o, gains, attn_pieces
+        )
+        joined, keep1, send1, keep2, send2 = fast_attn_backward(
+            meta, bucket, tokens, qkv, do, lse, gains, dy, mixed, gain_rows
+        )
+        token_gradient = fast_input_backward(meta, tokens, joined, dh, gains, attn_pieces)
+        sum1 = reduce_rows(keep1, send1, ALONG_X, ALONG_Y)
+        sum2 = reduce_rows(keep2, send2, ALONG_Y, ALONG_X)
+        both = jnp.concatenate([sum1, sum2[:rows]], axis=1)
+        extra = jnp.pad(sum2[rows : rows + 1], ((0, 0), (0, 2 * D)))
+
+        def block(k):
+            at = lax.rem(at_mp + k, n_mp) * slim
+            return jnp.concatenate([lax.dynamic_slice_in_dim(both, at, slim, 0), extra], axis=0)
+
+        share = block(0)
+        for k in range(1, n_mp):
+            share = share + wide(turn(block(k).astype(BF16), k, n_mp))
+        place = (at_dp * n_mp + at_mp) * slim
+        grad_ffn_gain = lax.dynamic_slice_in_dim(share[slim, :D], place, slim, 0)
+        share = share[:slim]
+        own_qkv = jnp.concatenate([qk_weight[0], qk_weight[1], value_weight], axis=1)
+        grad_attn_gain = jnp.sum(share[:, : 3 * D] * wide(own_qkv), axis=1) / wide(attn_gain)
+        grad_inner_gain = jnp.sum(share[:, 3 * D :] * wide(out_weight), axis=1) / wide(inner_gain)
+        return (
+            output,
+            token_gradient,
+            grad_attn_gain,
+            jnp.stack([share[:, :D], share[:, D : 2 * D]]),
+            share[:, 2 * D : 3 * D],
+            grad_inner_gain,
+            share[:, 3 * D :],
+            grad_ffn_gain,
+            ffn_share[:rows],
+            ffn_share[2 * rows],
+            ffn_share[rows : 2 * rows].T,
+        )
+
+    return body
+
+
 def solution(mesh):
     flat = P(BOTH)
     rows = P(BOTH, None)
@@ -518,8 +1144,13 @@
         rows, rows, flat, pair, rows, flat, rows, flat,
         P("dp", "mp"), P("mp"), P("mp", "dp"),
     )
+    n_dp, n_mp = mesh.shape["dp"], mesh.shape["mp"]
+    if (n_dp, n_mp) == (8, 4):
+        body = fast_on_device(n_mp)
+    else:
+        body = on_device(n_dp, n_mp)
     return jax.shard_map(
-        on_device(mesh.shape["dp"], mesh.shape["mp"]),
+        body,
         mesh=mesh,
         in_specs=placed,
         out_specs=given,

time: 505 us -> 329 us (0.65); the launches traced: 504 us -> 323 us
  waiting for transfers between devices: 301 us -> 143 us
  blocking collectives: 44.5 us -> 0 us
  starting transfers between devices: 0.16 us -> 43.7 us
  local copies, waits for them, and re-layouts: 42.7 us -> 24 us
  between operations: 15.1 us -> 1.85 us
  Pallas kernels: 81.6 us -> 89.3 us
    ppermute x0 -> x42, waiting for transfers between devices: none -> 143 us  [the longest x30 92.2 us: swap(): return lax.ppermute(values, 'dp', [(i, i ^ flip) for i in range(8)])]
    reduce_scatter x1 -> x0, waiting for transfers between devices: 138 us -> none  [body(): lax.psum_scatter(ffn_grads, BOTH, scatter_dimension=0).astype(F32)]
    all_gather x2 -> x0, waiting for transfers between devices: 109 us -> none  [the longest x1 60.3 us: body(): ffn_all = lax.all_gather(ffn_shard, BOTH, axis=0)]
    unnamed x5 -> x0, waiting for transfers between devices: 54.1 us -> none
    ppermute x0 -> x42, starting transfers between devices: none -> 43.7 us  [the longest x12 26.2 us: turn(): return lax.ppermute(values, 'mp', [(i, (i + k) % n) for i in range(n)])]
    unnamed x1 -> x0, blocking collectives: 17.2 us -> none
    slice x6 -> x14, local copies, waits for them, and re-layouts: 17.7 us -> 0.88 us  [the longest x1 0.6 us: body(): ffn_share[2 * rows]]
    all_gather x1 -> x0, blocking collectives: 14.7 us -> none  [body(): inner_all = lax.all_gather(ffn_inner_gain, 'mp', axis=0, tiled=True)]
  transfers between devices with their start and end apart: 4 -> 42, of which waited for: 4 -> 19; matrix products, arithmetic and copies ran while one was open for 6% -> 11% of each run, Pallas kernels for 3% -> 8%
where the time goes in v3:
time: 329 us; the launch traced here: 323 us
  waiting for transfers between devices  143 us (43%)
  Pallas kernels  89.3 us (27%)
  starting transfers between devices  43.7 us (13%)
  local copies, waits for them, and re-layouts  24 us (7%)
  other arithmetic  21.1 us (6%)
    ppermute x30, waiting for transfers between devices, swap(): return lax.ppermute(values, 'dp', [(i, i ^ flip) for i in range(8)])  92.2 us
    ppermute x12, waiting for transfers between devices, turn(): return lax.ppermute(values, 'mp', [(i, (i + k) % n) for i in range(n)])  50.4 us
    pallas_call x1, Pallas kernels, fast_ffn(): pl.pallas_call(fast_ffn_kernel, out_shape=(shape((total, D), BF16), one,...  33.1 us
    ppermute x12, starting transfers between devices, turn(): return lax.ppermute(values, 'mp', [(i, (i + k) % n) for i in range(n)])  26.2 us
    pallas_call x1, Pallas kernels, fast_attn_backward(): pl.pallas_call(fast_attn_backward_kernel, out_shape=(shape((3 * PAIRS, to...  21.8 us
    ppermute x30, starting transfers between devices, swap(): return lax.ppermute(values, 'dp', [(i, i ^ flip) for i in range(8)])  17.5 us
    pallas_call x1, Pallas kernels, fast_forward(): pl.pallas_call(fast_forward_kernel, out_shape=(shape((3 * PAIRS, total, P...  17 us
    ppermute x5, local copies, waits for them, and re-layouts, swap(): return lax.ppermute(values, 'dp', [(i, i ^ flip) for i in range(8)])  9.44 us
  transfers between devices with their start and end apart: 42, of which 19 were waited for; matrix products, arithmetic and copies ran while one was open for 11% of the time, Pallas kernels for 8%

profile of v3, /device:TPU:0, one launch (start us, length us, event | category | flops | bytes accessed | tf_op | source)
XLA Modules:
  0.0 322.6 jit_solution(16083527379577706260)
XLA Ops:
  1.4 0.8 constant_dynamic-update-slice_fusion.4
  2.2 0.8 constant_dynamic-update-slice_fusion.3
  3.8 0.8 constant_dynamic-update-slice_fusion.1
  4.6 5.1 %collective-permute-start = (bf16[24,3200]{1,0:T(8,128)(2,1)S(1)}, bf16[24,3200]{1,0:T(8,128)(2,1)S(1)}, u32[]{:S(2)}, u32[]{:S(2)}) collective-permute-start(bf16[24,3200]{1,0:T(8,128)(2,1)S(1)} %constant_dynamic-update-slice_fusion), channel_id=1, source_target_pairs={{0,3},{1,0},{2,1},{3,2},{4,7},{5,4},{6,5},{7,6},{8,11},{9,8},{10,9... | collective-permute-start | bytes 460808 | tf_op jit(solution)/shard_map/ppermute | solution.py:1001
  9.7 1.0 collective-permute-start.2
  11.4 1.0 fusion.17
  12.4 2.5 collective-permute-start.12
  15.0 0.9 collective-permute-start.13
  15.9 1.0 pad_maximum_fusion.7
  16.9 1.6 collective-permute-start.14
  18.5 18.6 %collective-permute-done.1 = bf16[24,3200]{1,0:T(8,128)(2,1)S(1)} collective-permute-done((bf16[24,3200]{1,0:T(8,128)(2,1)S(1)}, bf16[24,3200]{1,0:T(8,128)(2,1)S(1)}, u32[]{:S(2)}, u32[]{:S(2)}) %collective-permute-start.1) | collective-permute-done | bytes 153632 | tf_op jit(solution)/shard_map/ppermute | solution.py:1001
  37.4 6.6 %collective-permute-done.13 = bf16[208,768]{1,0:T(8,128)(2,1)S(1)} collective-permute-done((bf16[208,768]{1,0:T(8,128)(2,1)S(1)}, bf16[208,768]{1,0:T(8,128)(2,1)S(1)}, u32[]{:S(2)}, u32[]{:S(2)}) %collective-permute-start.13) | collective-permute-done | bytes 319520 | tf_op jit(solution)/shard_map/ppermute | solution.py:1001
  44.8 1.5 collective-permute-start.15
  46.4 1.6 collective-permute-start.4
  49.0 14.2 %collective-permute-done.4.rest_2_ = bf16[96,3200]{1,0:T(8,128)(2,1)S(1)} collective-permute-done((bf16[96,3200]{1,0:T(8,128)(2,1)S(1)}, bf16[96,3200]{1,0:T(8,128)(2,1)S(1)}, u32[]{:S(2)}, u32[]{:S(2)}) %collective-permute-start.4) | collective-permute-done | bytes 614432 | tf_op jit(solution)/shard_map/ppermute | solution.py:997
  63.8 23.0 %collective-permute-done.3.rest_1_ = bf16[96,3200]{1,0:T(8,128)(2,1)S(1)} collective-permute-done((bf16[96,3200]{1,0:T(8,128)(2,1)S(1)}, bf16[96,3200]{1,0:T(8,128)(2,1)S(1)}, u32[]{:S(2)}, u32[]{:S(2)}) %collective-permute-start.3) | collective-permute-done | bytes 614432 | tf_op jit(solution)/shard_map/ppermute | solution.py:997
  86.9 1.6 collective-permute-start.5
  88.5 5.2 %collective-permute-done.5.rest_3_ = bf16[96,1536]{1,0:T(8,128)(2,1)S(1)} collective-permute-done((bf16[96,1536]{1,0:T(8,128)(2,1)S(1)}, bf16[96,1536]{1,0:T(8,128)(2,1)S(1)}, u32[]{:S(2)}, u32[]{:S(2)}) %collective-permute-start.5) | collective-permute-done | bytes 294944 | tf_op jit(solution)/shard_map/ppermute | solution.py:997
  94.3 1.0 slice_bitcast_fusion.5
  95.7 0.9 slice_bitcast_fusion.4
  96.6 1.6 collective-permute-start.17
  98.9 1.5 collective-permute-start.18
  103.7 8.8 %collective-permute-done.17.rest_3_ = bf16[4,96,768]{2,1,0:T(8,128)(2,1)} collective-permute-done((bf16[4,96,768]{2,1,0:T(8,128)(2,1)}, bf16[4,96,768]{2,1,0:T(8,128)(2,1)}, u32[]{:S(2)}, u32[]{:S(2)}) %collective-permute-start.17) | collective-permute-done | bytes 589856 | tf_op jit(solution)/shard_map/ppermute | solution.py:997
  112.5 2.0 collective-permute-done.18.rest_4_
  115.1 1.1 copy.33.rest_0_
  116.9 17.0 %attn_forward.1 = (bf16[18,512,128]{2,1,0:T(8,128)(2,1)}, f32[12,1,512]{2,1,0:T(1,128)}, f32[512,768]{1,0:T(8,128)}, f32[512,768]{1,0:T(8,128)}, bf16[512,768]{1,0:T(8,128)(2,1)}, /*index=5*/f32[8,768]{1,0:T(8,128)}) custom-call(s32[2]{0:T(128)} %pad_add_fusion.meta, s32[1]{0:T(128)S(6)} %copy.53.bucket, bf16[512,768]{1,0:T(8,128)(2,1)} %x.11, ...), custom_call_target="tpu_custom_call" | custom-call | flops 4200000000 | bytes 10000000 | tf_op jit(solution)/shard_map/attn_forward/pallas_call | solution.py:562
  133.9 1.2 copy.34.rest_1_
  135.6 1.1 copy.35.rest_2_
  136.7 2.4 copy.36.rest_5_
  139.1 2.4 copy.37.rest_6_
  141.5 2.4 copy.38.rest_7_
  143.9 33.1 %feed_forward.1 = (bf16[512,768]{1,0:T(8,128)(2,1)}, bf16[2,2,384,768]{3,2,1,0:T(8,128)(2,1)}, bf16[2,2,384,768]{3,2,1,0:T(8,128)(2,1)}, bf16[2,2,400,768]{3,2,1...) custom-call(s32[2]{0:T(128)} %pad_add_fusion.meta, bf16[512,768]{1,0:T(8,128)(2,1)} %get-tuple-element.33.c, ...), custom_call_target="tpu_custom_call" | custom-call | flops 14499999744 | bytes 20000000 | tf_op jit(solution)/shard_map/feed_forward/pallas_call | solution.py:750
  177.0 8.8 %out_backward.1 = (f32[512,768]{1,0:T(8,128)}, bf16[6,512,128]{2,1,0:T(8,128)(2,1)}, bf16[512,768]{1,0:T(8,128)(2,1)}, bf16[512,768]{1,0:T(8,128)(2,1)}, f32[8,768]{1,0:T(8,128)}) custom-call(s32[2]{0:T(128)} %pad_add_fusion.meta, f32[512,768]{1,0:T(8,128)} %get-tuple-element.37.dc, bf16[512,768]{1,0:T(8,128)(2,1)} %cot.3, f32[512,768]{1,0:T(8,128)} %get-tuple-element.34.h, ...), custom_call_target="tpu_custom_call" | custom-call | flops 1200000000 | bytes 10000000 | tf_op jit(solution)/shard_map/out_backward/pallas_call | solution.py:807
  185.8 21.8 %attn_backward.1 = (bf16[18,512,128]{2,1,0:T(8,128)(2,1)}, bf16[2,2,96,1536]{3,2,1,0:T(8,128)(2,1)}, bf16[2,2,96,1536]{3,2,1,0:T(8,128)(2,1)}, bf16[2,2,112,1536...) custom-call(s32[2]{0:T(128)} %pad_add_fusion.meta, s32[1]{0:T(128)S(6)} %copy.53.bucket, bf16[512,768]{1,0:T(8,128)(2,1)} %x.11, ...), custom_call_target="tpu_custom_call" | custom-call | flops 8999999488 | bytes 15000000 | tf_op jit(solution)/shard_map/attn_backward/pallas_call | solution.py:940
  208.6 3.1 collective-permute-done.24
  211.7 1.1 copy-done.14
  212.8 2.0 fusion.12
  214.8 1.5 collective-permute-start.25
  216.3 2.1 fusion.6
  219.0 8.6 %input_backward.1 = f32[512,768]{1,0:T(8,128)} custom-call(s32[2]{0:T(128)} %pad_add_fusion.meta, bf16[512,768]{1,0:T(8,128)(2,1)} %x.11, bf16[18,512,128]{2,1,0:T(8,128)(2,1)} %get-tuple-element.45.joined, f32[512,768]{1,0:T(8,128)} %get-tuple-element.46.dh, f32[8,768]{1,0:T(8,128)} %get-tuple-element.39.gains, bf16[96,3200]{1,0:T(8,128)(2,1)} %copy-done, ...), custom_call_target="tpu_custom_call" | custom-call | flops 1800000000 | bytes 10000000 | tf_op jit(solution)/shard_map/input_backward/pallas_call | solution.py:981
  227.6 3.2 collective-permute-done.25
  230.7 1.2 fusion.13
  232.6 4.5 %collective-permute-done.28 = bf16[2,112,1536]{2,1,0:T(8,128)(2,1)} collective-permute-done((bf16[2,112,1536]{2,1,0:T(8,128)(2,1)}, bf16[2,112,1536]{2,1,0:T(8,128)(2,1)}, u32[]{:S(2)}, u32[]{:S(2)}) %collective-permute-start.28) | collective-permute-done | bytes 688160 | tf_op jit(solution)/shard_map/ppermute | solution.py:997
  237.0 1.4 fusion.7
  239.0 3.4 %collective-permute-done.26 = bf16[96,1536]{1,0:T(8,128)(2,1)S(1)} collective-permute-done((bf16[96,1536]{1,0:T(8,128)(2,1)S(1)}, bf16[96,1536]{1,0:T(8,128)(2,1)S(1)}, u32[]{:S(2)}, u32[]{:S(2)}) %collective-permute-start.26) | collective-permute-done | bytes 294944 | tf_op jit(solution)/shard_map/ppermute | solution.py:997
  242.4 1.3 fusion.14
  243.7 1.6 fusion.3
  245.9 0.9 collective-permute-done.29
  246.8 1.2 fusion.8
  248.3 7.1 %collective-permute-start.30 = (bf16[25,3072]{1,0:T(8,128)(2,1)S(1)}, bf16[25,3072]{1,0:T(8,128)(2,1)S(1)}, u32[]{:S(2)}, u32[]{:S(2)}) collective-permute-start(bf16[25,3072]{1,0:T(8,128)(2,1)S(1)} %get-tuple-element.80), channel_id=1, source_target_pairs={{0,1},{1,2},{2,3},{3,0},{4,5},{5,6},{6,7},{7,4},{8,9},{9,10},{10,1... | collective-permute-start | bytes 460808 | tf_op jit(solution)/shard_map/ppermute | solution.py:1001
  255.3 3.4 %collective-permute-start.31 = (bf16[25,3072]{1,0:T(8,128)(2,1)S(1)}, bf16[25,3072]{1,0:T(8,128)(2,1)S(1)}, u32[]{:S(2)}, u32[]{:S(2)}) collective-permute-start(bf16[25,3072]{1,0:T(8,128)(2,1)S(1)} %get-tuple-element.81), channel_id=1, source_target_pairs={{0,2},{1,3},{2,0},{3,1},{4,6},{5,7},{6,4},{7,5},{8,10},{9,11},{10,... | collective-permute-start | bytes 460808 | tf_op jit(solution)/shard_map/ppermute | solution.py:1001
  259.6 4.4 %collective-permute-done.30 = bf16[25,3072]{1,0:T(8,128)(2,1)S(1)} collective-permute-done((bf16[25,3072]{1,0:T(8,128)(2,1)S(1)}, bf16[25,3072]{1,0:T(8,128)(2,1)S(1)}, u32[]{:S(2)}, u32[]{:S(2)}) %collective-permute-start.30) | collective-permute-done | bytes 153632 | tf_op jit(solution)/shard_map/ppermute | solution.py:1001
  264.0 5.8 %collective-permute-done.31 = bf16[25,3072]{1,0:T(8,128)(2,1)S(1)} collective-permute-done((bf16[25,3072]{1,0:T(8,128)(2,1)S(1)}, bf16[25,3072]{1,0:T(8,128)(2,1)S(1)}, u32[]{:S(2)}, u32[]{:S(2)}) %collective-permute-start.31) | collective-permute-done | bytes 153632 | tf_op jit(solution)/shard_map/ppermute | solution.py:1001
  269.9 2.5 collective-permute-done.34
  272.4 1.3 fusion.4
  274.3 14.7 %collective-permute-done.37 = bf16[2,400,768]{2,1,0:T(8,128)(2,1)S(1)} collective-permute-done((bf16[2,400,768]{2,1,0:T(8,128)(2,1)S(1)}, bf16[2,400,768]{2,1,0:T(8,128)(2,1)S(1)}, u32[]{:S(2)}, u32[]{:S(2)}) %collective-permute-start.37) | collective-permute-done | bytes 1228832 | tf_op jit(solution)/shard_map/ppermute | solution.py:997
  289.9 0.8 multiply_reduce_fusion
  291.5 6.6 %collective-permute-done.35 = bf16[384,768]{1,0:T(8,128)(2,1)S(1)} collective-permute-done((bf16[384,768]{1,0:T(8,128)(2,1)S(1)}, bf16[384,768]{1,0:T(8,128)(2,1)S(1)}, u32[]{:S(2)}, u32[]{:S(2)}) %collective-permute-start.35) | collective-permute-done | bytes 589856 | tf_op jit(solution)/shard_map/ppermute | solution.py:997
  298.1 1.4 fusion.27
  300.1 2.0 collective-permute-start.39
  302.3 2.5 collective-permute-start.41
  305.9 6.3 %collective-permute-done.39 = bf16[193,768]{1,0:T(8,128)(2,1)S(1)} collective-permute-done((bf16[193,768]{1,0:T(8,128)(2,1)S(1)}, bf16[193,768]{1,0:T(8,128)(2,1)S(1)}, u32[]{:S(2)}, u32[]{:S(2)}) %collective-permute-start.39) | collective-permute-done | bytes 296480 | tf_op jit(solution)/shard_map/ppermute | solution.py:1001
  312.2 8.8 %collective-permute-done.40 = bf16[193,768]{1,0:T(8,128)(2,1)S(1)} collective-permute-done((bf16[193,768]{1,0:T(8,128)(2,1)S(1)}, bf16[193,768]{1,0:T(8,128)(2,1)S(1)}, u32[]{:S(2)}, u32[]{:S(2)}) %collective-permute-start.40) | collective-permute-done | bytes 296480 | tf_op jit(solution)/shard_map/ppermute | solution.py:1001
  321.2 0.8 slice_bitcast_fusion.8
  (153 shorter events, 20.5 us)
Async XLA Ops:
  2.2 35.0 %copy-start.15 = (bf16[2,24,768]{2,1,0:T(8,128)(2,1)S(1)}, bf16[2,24,768]{2,1,0:T(8,128)(2,1)}, u32[]{:S(2)}) copy-start(bf16[2,24,768]{2,1,0:T(8,128)(2,1)} %param.15) | copy-start | bytes 221188
  3.8 33.4 %copy-start.17 = (bf16[24,768]{1,0:T(8,128)(2,1)S(1)}, bf16[24,768]{1,0:T(8,128)(2,1)}, u32[]{:S(2)}) copy-start(bf16[24,768]{1,0:T(8,128)(2,1)} %param.16) | copy-start | bytes 110596
  4.6 12.3 %collective-permute-start = (bf16[24,3200]{1,0:T(8,128)(2,1)S(1)}, bf16[24,3200]{1,0:T(8,128)(2,1)S(1)}, u32[]{:S(2)}, u32[]{:S(2)}) collective-permute-start(bf16[24,3200]{1,0:T(8,128)(2,1)S(1)} %constant_dynamic-update-slice_fusion), channel_id=1, source_target_pairs={{0,3},{1,0},{2,1},{3,2},{4,7},{5,4},{6,5},{7,6},{8,11},{9,8},{10,9... | collective-permute-start | bytes 460808 | tf_op jit(solution)/shard_map/ppermute | solution.py:1001
  9.7 27.4 %collective-permute-start.1 = (bf16[24,3200]{1,0:T(8,128)(2,1)S(1)}, bf16[24,3200]{1,0:T(8,128)(2,1)S(1)}, u32[]{:S(2)}, u32[]{:S(2)}) collective-permute-start(bf16[24,3200]{1,0:T(8,128)(2,1)S(1)} %constant_dynamic-update-slice_fusion), channel_id=1, source_target_pairs={{0,2},{1,3},{2,0},{3,1},{4,6},{5,7},{6,4},{7,5},{8,10},{9,11},{10,... | collective-permute-start | bytes 460808 | tf_op jit(solution)/shard_map/ppermute | solution.py:1001
  9.7 27.4 %collective-permute-start.2 = (bf16[24,3200]{1,0:T(8,128)(2,1)S(1)}, bf16[24,3200]{1,0:T(8,128)(2,1)S(1)}, u32[]{:S(2)}, u32[]{:S(2)}) collective-permute-start(bf16[24,3200]{1,0:T(8,128)(2,1)S(1)} %constant_dynamic-update-slice_fusion), channel_id=1, source_target_pairs={{0,1},{1,2},{2,3},{3,0},{4,5},{5,6},{6,7},{7,4},{8,9},{9,10},{10,1... | collective-permute-start | bytes 460808 | tf_op jit(solution)/shard_map/ppermute | solution.py:1001
  11.4 25.8 %copy-start.16 = (bf16[24,768]{1,0:T(8,128)(2,1)S(1)}, bf16[24,768]{1,0:T(8,128)(2,1)}, u32[]{:S(2)}) copy-start(bf16[24,768]{1,0:T(8,128)(2,1)} %param.18) | copy-start | bytes 110596
  12.4 24.9 %collective-permute-start.12 = (bf16[208,768]{1,0:T(8,128)(2,1)S(1)}, bf16[208,768]{1,0:T(8,128)(2,1)S(1)}, u32[]{:S(2)}, u32[]{:S(2)}) collective-permute-start(bf16[208,768]{1,0:T(8,128)(2,1)S(1)} %fusion.17), channel_id=1, source_target_pairs={{0,1},{1,2},{2,3},{3,0},{4,5},{5,6},{6,7},{7,4},{8,9},{9,10},{10,1... | collective-permute-start | bytes 958472 | tf_op jit(solution)/shard_map/ppermute | solution.py:1001
  15.0 29.0 %collective-permute-start.13 = (bf16[208,768]{1,0:T(8,128)(2,1)S(1)}, bf16[208,768]{1,0:T(8,128)(2,1)S(1)}, u32[]{:S(2)}, u32[]{:S(2)}) collective-permute-start(bf16[208,768]{1,0:T(8,128)(2,1)S(1)} %fusion.17), channel_id=1, source_target_pairs={{0,2},{1,3},{2,0},{3,1},{4,6},{5,7},{6,4},{7,5},{8,10},{9,11},{10,... | collective-permute-start | bytes 958472 | tf_op jit(solution)/shard_map/ppermute | solution.py:1001
  16.9 27.1 %collective-permute-start.14 = (bf16[208,768]{1,0:T(8,128)(2,1)S(1)}, bf16[208,768]{1,0:T(8,128)(2,1)S(1)}, u32[]{:S(2)}, u32[]{:S(2)}) collective-permute-start(bf16[208,768]{1,0:T(8,128)(2,1)S(1)} %fusion.17), channel_id=1, source_target_pairs={{0,3},{1,0},{2,1},{3,2},{4,7},{5,4},{6,5},{7,6},{8,11},{9,8},{10,9... | collective-permute-start | bytes 958472 | tf_op jit(solution)/shard_map/ppermute | solution.py:1001
  37.3 6.7 %copy-start.18 = (bf16[208,768]{1,0:T(8,128)(2,1)}, bf16[208,768]{1,0:T(8,128)(2,1)S(1)}, u32[]{:S(2)}) copy-start(bf16[208,768]{1,0:T(8,128)(2,1)S(1)} %collective-permute-done.12) | copy-start | bytes 958468
  44.0 0.8 copy-start.20
  44.8 49.4 %collective-permute-start.15 = (bf16[4,2,96,768]{3,2,0,1:T(8,128)(2,1)S(1)}, bf16[4,2,96,768]{3,2,0,1:T(8,128)(2,1)S(1)}, u32[]{:S(2)}, u32[]{:S(2)}) collective-permute-start(bf16[4,2,96,768]{3,2,0,1:T(8,128)(2,1)S(1)} %pad_maximum_fusion), channel_id=1, source_target_pairs={{0,8},{4,12},{8,0},{12,4},{16,24},{20,28},{24,16},{28,20},{1,9},{5... | collective-permute-start | bytes 3538952 | tf_op jit(solution)/shard_map/ppermute | solution.py:997
  46.4 48.9 %copy-start = (bf16[96,3200]{1,0:T(8,128)(2,1)}, bf16[96,3200]{1,0:T(8,128)(2,1)S(1)}, u32[]{:S(2)}) copy-start(bf16[96,3200]{1,0:T(8,128)(2,1)S(1)} %constant_dynamic-slice_fusion.1.rest_0_) | copy-start | bytes 1843204
  46.4 16.9 %collective-permute-start.4 = (bf16[96,3200]{1,0:T(8,128)(2,1)S(1)}, bf16[96,3200]{1,0:T(8,128)(2,1)S(1)}, u32[]{:S(2)}, u32[]{:S(2)}) collective-permute-start(bf16[96,3200]{1,0:T(8,128)(2,1)S(1)} %constant_dynamic-slice_fusion.1.rest_0_), channel_id=1, source_target_pairs={{0,16},{4,20},{8,24},{12,28},{16,0},{20,4},{24,8},{28,12},{1,17},{... | collective-permute-start | bytes 1843208 | tf_op jit(solution)/shard_map/ppermute | solution.py:997
  47.9 47.4 %collective-permute-start.16 = (bf16[4,2,96,768]{3,2,0,1:T(8,128)(2,1)S(1)}, bf16[4,2,96,768]{3,2,0,1:T(8,128)(2,1)S(1)}, u32[]{:S(2)}, u32[]{:S(2)}) collective-permute-start(bf16[4,2,96,768]{3,2,0,1:T(8,128)(2,1)S(1)} %pad_maximum_fusion), channel_id=1, source_target_pairs={{0,16},{4,20},{8,24},{12,28},{16,0},{20,4},{24,8},{28,12},{1,17},{... | collective-permute-start | bytes 3538952 | tf_op jit(solution)/shard_map/ppermute | solution.py:997
  48.5 38.4 %collective-permute-start.3 = (bf16[96,3200]{1,0:T(8,128)(2,1)S(1)}, bf16[96,3200]{1,0:T(8,128)(2,1)S(1)}, u32[]{:S(2)}, u32[]{:S(2)}) collective-permute-start(bf16[96,3200]{1,0:T(8,128)(2,1)S(1)} %constant_dynamic-slice_fusion.1.rest_0_), channel_id=1, source_target_pairs={{0,8},{4,12},{8,0},{12,4},{16,24},{20,28},{24,16},{28,20},{1,9},{5... | collective-permute-start | bytes 1843208 | tf_op jit(solution)/shard_map/ppermute | solution.py:997
  63.2 32.1 %copy-start.1 = (bf16[96,3200]{1,0:T(8,128)(2,1)}, bf16[96,3200]{1,0:T(8,128)(2,1)S(1)}, u32[]{:S(2)}) copy-start(bf16[96,3200]{1,0:T(8,128)(2,1)S(1)} %collective-permute-done.4.rest_2_) | copy-start | bytes 1843204
  63.2 30.5 %collective-permute-start.6 = (bf16[96,1664]{1,0:T(8,128)(2,1)S(1)}, bf16[96,1664]{1,0:T(8,128)(2,1)S(1)}, u32[]{:S(2)}, u32[]{:S(2)}) collective-permute-start(bf16[96,1664]{1,0:T(8,128)(2,1)S(1)} %slice.290), channel_id=1, source_target_pairs={{0,8},{4,12},{8,0},{12,4},{16,24},{20,28},{24,16},{28,20},{1,9},{5... | collective-permute-start | bytes 958472 | tf_op jit(solution)/shard_map/ppermute | solution.py:997
  86.9 9.7 %copy-start.2 = (bf16[96,3200]{1,0:T(8,128)(2,1)}, bf16[96,3200]{1,0:T(8,128)(2,1)S(1)}, u32[]{:S(2)}) copy-start(bf16[96,3200]{1,0:T(8,128)(2,1)S(1)} %collective-permute-done.3.rest_1_) | copy-start | bytes 1843204
  86.9 13.5 %copy-start.21 = (bf16[768]{0:T(1024)(128)(2,1)S(1)}, bf16[768]{0:T(1024)(128)(2,1)}, u32[]{:S(2)}) copy-start(bf16[768]{0:T(1024)(128)(2,1)} %param.21) | copy-start | bytes 4612
  86.9 6.8 %collective-permute-start.5 = (bf16[96,1536]{1,0:T(8,128)(2,1)S(1)}, bf16[96,1536]{1,0:T(8,128)(2,1)S(1)}, u32[]{:S(2)}, u32[]{:S(2)}) collective-permute-start(bf16[96,1536]{1,0:T(8,128)(2,1)S(1)} %slice.289), channel_id=1, source_target_pairs={{0,16},{4,20},{8,24},{12,28},{16,0},{20,4},{24,8},{28,12},{1,17},{... | collective-permute-start | bytes 884744 | tf_op jit(solution)/shard_map/ppermute | solution.py:997
  88.5 8.1 %collective-permute-start.7 = (bf16[96,3200]{1,0:T(8,128)(2,1)S(1)}, bf16[96,3200]{1,0:T(8,128)(2,1)S(1)}, u32[]{:S(2)}, u32[]{:S(2)}) collective-permute-start(bf16[96,3200]{1,0:T(8,128)(2,1)S(1)} %constant_dynamic-slice_fusion.1.rest_0_), channel_id=1, source_target_pairs={{0,4},{4,0},{8,12},{12,8},{16,20},{20,16},{24,28},{28,24},{1,5},{5... | collective-permute-start | bytes 1843208 | tf_op jit(solution)/shard_map/ppermute | solution.py:997
  93.7 4.5 %copy-start.12 = (bf16[96,1536]{1,0:T(8,128)(2,1)}, bf16[96,1536]{1,0:T(8,128)(2,1)S(1)}, u32[]{:S(2)}) copy-start(bf16[96,1536]{1,0:T(8,128)(2,1)S(1)} %collective-permute-done.5.rest_3_) | copy-start | bytes 884740
  93.7 7.9 %collective-permute-start.8 = (bf16[96,3200]{1,0:T(8,128)(2,1)S(1)}, bf16[96,3200]{1,0:T(8,128)(2,1)}, u32[]{:S(2)}, u32[]{:S(2)}) collective-permute-start(bf16[96,3200]{1,0:T(8,128)(2,1)S(1)} %collective-permute-done.3.rest_1_), channel_id=1, source_target_pairs={{0,4},{4,0},{8,12},{12,8},{16,20},{20,16},{24,28},{28,24},{1,5},{5... | collective-permute-start | bytes 1843208 | tf_op jit(solution)/shard_map/ppermute | solution.py:997
  93.7 2.8 copy-start.11
  93.7 7.9 %collective-permute-start.9 = (bf16[96,3200]{1,0:T(8,128)(2,1)S(1)}, bf16[96,3200]{1,0:T(8,128)(2,1)}, u32[]{:S(2)}, u32[]{:S(2)}) collective-permute-start(bf16[96,3200]{1,0:T(8,128)(2,1)S(1)} %collective-permute-done.4.rest_2_), channel_id=1, source_target_pairs={{0,4},{4,0},{8,12},{12,8},{16,20},{20,16},{24,28},{28,24},{1,5},{5... | collective-permute-start | bytes 1843208 | tf_op jit(solution)/shard_map/ppermute | solution.py:997
  94.2 2.3 copy-start.3
  94.2 3.9 %collective-permute-start.10 = (bf16[96,1536]{1,0:T(8,128)(2,1)S(1)}, bf16[96,1536]{1,0:T(8,128)(2,1)S(1)}, u32[]{:S(2)}, u32[]{:S(2)}) collective-permute-start(bf16[96,1536]{1,0:T(8,128)(2,1)S(1)} %collective-permute-done.5.rest_3_), channel_id=1, source_target_pairs={{0,4},{4,0},{8,12},{12,8},{16,20},{20,16},{24,28},{28,24},{1,5},{5... | collective-permute-start | bytes 884744 | tf_op jit(solution)/shard_map/ppermute | solution.py:997
  95.3 1.3 copy-start.5
  95.3 6.8 %collective-permute-start.11 = (bf16[96,1664]{1,0:T(8,128)(2,1)S(1)}, bf16[96,1664]{1,0:T(8,128)(2,1)}, u32[]{:S(2)}, u32[]{:S(2)}) collective-permute-start(bf16[96,1664]{1,0:T(8,128)(2,1)S(1)} %collective-permute-done.6.rest_4_), channel_id=1, source_target_pairs={{0,4},{4,0},{8,12},{12,8},{16,20},{20,16},{24,28},{28,24},{1,5},{5... | collective-permute-start | bytes 958472 | tf_op jit(solution)/shard_map/ppermute | solution.py:997
  96.6 19.7 %copy-start.7 = (bf16[96,3200]{1,0:T(8,128)(2,1)}, bf16[96,3200]{1,0:T(8,128)(2,1)S(1)}, u32[]{:S(2)}) copy-start(bf16[96,3200]{1,0:T(8,128)(2,1)S(1)} %collective-permute-done.7.rest_5_) | copy-start | bytes 1843204
  96.6 15.9 %collective-permute-start.17 = (bf16[4,96,768]{2,1,0:T(8,128)(2,1)}, bf16[4,96,768]{2,1,0:T(8,128)(2,1)}, u32[]{:S(2)}, u32[]{:S(2)}) collective-permute-start(bf16[4,96,768]{2,1,0:T(8,128)(2,1)} %slice_bitcast_fusion.5), channel_id=1, source_target_pairs={{0,16},{4,20},{8,24},{12,28},{16,0},{20,4},{24,8},{28,12},{1,17},{... | collective-permute-start | bytes 1769480 | tf_op jit(solution)/shard_map/ppermute | solution.py:997
  98.9 15.5 %collective-permute-start.18 = (bf16[4,96,768]{2,1,0:T(8,128)(2,1)}, bf16[4,96,768]{2,1,0:T(8,128)(2,1)}, u32[]{:S(2)}, u32[]{:S(2)}) collective-permute-start(bf16[4,96,768]{2,1,0:T(8,128)(2,1)} %slice_bitcast_fusion.4), channel_id=1, source_target_pairs={{0,8},{4,12},{8,0},{12,4},{16,24},{20,28},{24,16},{28,20},{1,9},{5... | collective-permute-start | bytes 1769480 | tf_op jit(solution)/shard_map/ppermute | solution.py:997
  101.6 35.0 %collective-permute-start.19 = (bf16[4,2,96,768]{3,2,0,1:T(8,128)(2,1)S(1)}, bf16[4,2,96,768]{3,2,0,1:T(8,128)(2,1)}, u32[]{:S(2)}, u32[]{:S(2)}) collective-permute-start(bf16[4,2,96,768]{3,2,0,1:T(8,128)(2,1)S(1)} %pad_maximum_fusion), channel_id=1, source_target_pairs={{0,4},{4,0},{8,12},{12,8},{16,20},{20,16},{24,28},{28,24},{1,5},{5... | collective-permute-start | bytes 3538952 | tf_op jit(solution)/shard_map/ppermute | solution.py:997
  101.6 37.4 %collective-permute-start.20 = (bf16[4,2,96,768]{3,2,0,1:T(8,128)(2,1)}, bf16[4,2,96,768]{3,2,0,1:T(8,128)(2,1)}, u32[]{:S(2)}, u32[]{:S(2)}) collective-permute-start(bf16[4,2,96,768]{3,2,0,1:T(8,128)(2,1)} %copy-done.3), channel_id=1, source_target_pairs={{0,4},{4,0},{8,12},{12,8},{16,20},{20,16},{24,28},{28,24},{1,5},{5... | collective-permute-start | bytes 3538952 | tf_op jit(solution)/shard_map/ppermute | solution.py:997
  102.2 39.3 %collective-permute-start.21 = (bf16[4,2,96,768]{3,2,0,1:T(8,128)(2,1)}, bf16[4,2,96,768]{3,2,0,1:T(8,128)(2,1)}, u32[]{:S(2)}, u32[]{:S(2)}) collective-permute-start(bf16[4,2,96,768]{3,2,0,1:T(8,128)(2,1)} %copy-done.5), channel_id=1, source_target_pairs={{0,4},{4,0},{8,12},{12,8},{16,20},{20,16},{24,28},{28,24},{1,5},{5... | collective-permute-start | bytes 3538952 | tf_op jit(solution)/shard_map/ppermute | solution.py:997
  112.5 31.4 %collective-permute-start.22 = (bf16[4,96,768]{2,1,0:T(8,128)(2,1)}, bf16[4,96,768]{2,1,0:T(8,128)(2,1)}, u32[]{:S(2)}, u32[]{:S(2)}) collective-permute-start(bf16[4,96,768]{2,1,0:T(8,128)(2,1)} %collective-permute-done.17.rest_3_), channel_id=1, source_target_pairs={{0,4},{4,0},{8,12},{12,8},{16,20},{20,16},{24,28},{28,24},{1,5},{5... | collective-permute-start | bytes 1769480 | tf_op jit(solution)/shard_map/ppermute | solution.py:997
  114.4 29.4 %collective-permute-start.23 = (bf16[4,96,768]{2,1,0:T(8,128)(2,1)}, bf16[4,96,768]{2,1,0:T(8,128)(2,1)}, u32[]{:S(2)}, u32[]{:S(2)}) collective-permute-start(bf16[4,96,768]{2,1,0:T(8,128)(2,1)} %collective-permute-done.18.rest_4_), channel_id=1, source_target_pairs={{0,4},{4,0},{8,12},{12,8},{16,20},{20,16},{24,28},{28,24},{1,5},{5... | collective-permute-start | bytes 1769480 | tf_op jit(solution)/shard_map/ppermute | solution.py:997
  116.9 17.0 %copy-start.4 = (bf16[4,2,96,768]{3,2,0,1:T(8,128)(2,1)S(1)}, bf16[4,2,96,768]{3,2,0,1:T(8,128)(2,1)}, u32[]{:S(2)}) copy-start(bf16[4,2,96,768]{3,2,0,1:T(8,128)(2,1)} %copy-done.3) | copy-start | bytes 3538948
  133.9 1.7 copy-start.6
  207.6 8.7 %copy-start.10 = (bf16[2,2,112,1536]{3,2,1,0:T(8,128)(2,1)S(1)}, bf16[2,2,112,1536]{3,2,1,0:T(8,128)(2,1)}, u32[]{:S(2)}) copy-start(bf16[2,2,112,1536]{3,2,1,0:T(8,128)(2,1)} %get-tuple-element.49) | copy-start | bytes 4128772
  207.6 4.1 %collective-permute-start.24 = (bf16[2,2,96,1536]{3,2,1,0:T(8,128)(2,1)}, bf16[2,2,96,1536]{3,2,1,0:T(8,128)(2,1)S(1)}, u32[]{:S(2)}, u32[]{:S(2)}) collective-permute-start(bf16[2,2,96,1536]{3,2,1,0:T(8,128)(2,1)} %get-tuple-element.48), channel_id=1, source_target_pairs={{0,4},{4,0},{8,12},{12,8},{16,20},{20,16},{24,28},{28,24},{1,5},{5... | collective-permute-start | bytes 3538952 | tf_op jit(solution)/shard_map/ppermute | solution.py:997
  208.1 8.2 %collective-permute-start.27 = (bf16[2,2,112,1536]{3,2,1,0:T(8,128)(2,1)}, bf16[2,2,112,1536]{3,2,1,0:T(8,128)(2,1)}, u32[]{:S(2)}, u32[]{:S(2)}) collective-permute-start(bf16[2,2,112,1536]{3,2,1,0:T(8,128)(2,1)} %get-tuple-element.50), channel_id=1, source_target_pairs={{0,4},{4,0},{8,12},{12,8},{16,20},{20,16},{24,28},{28,24},{1,5},{5... | collective-permute-start | bytes 4128776 | tf_op jit(solution)/shard_map/ppermute | solution.py:997
  208.2 35.5 %collective-permute-start.33 = (bf16[2,2,384,768]{3,2,1,0:T(8,128)(2,1)}, bf16[2,2,384,768]{3,2,1,0:T(8,128)(2,1)}, u32[]{:S(2)}, u32[]{:S(2)}) collective-permute-start(bf16[2,2,384,768]{3,2,1,0:T(8,128)(2,1)} %get-tuple-element.52), channel_id=1, source_target_pairs={{0,4},{4,0},{8,12},{12,8},{16,20},{20,16},{24,28},{28,24},{1,5},{5... | collective-permute-start | bytes 7077896 | tf_op jit(solution)/shard_map/ppermute | solution.py:997
  211.7 1.1 copy-start.14
  214.8 15.9 %collective-permute-start.25 = (bf16[2,96,1536]{2,1,0:T(8,128)(2,1)}, bf16[2,96,1536]{2,1,0:T(8,128)(2,1)}, u32[]{:S(2)}, u32[]{:S(2)}) collective-permute-start(bf16[2,96,1536]{2,1,0:T(8,128)(2,1)} %fusion.12), channel_id=1, source_target_pairs={{0,8},{4,12},{8,0},{12,4},{16,24},{20,28},{24,16},{28,20},{1,9},{5... | collective-permute-start | bytes 1769480 | tf_op jit(solution)/shard_map/ppermute | solution.py:997
  218.4 18.6 %collective-permute-start.28 = (bf16[2,112,1536]{2,1,0:T(8,128)(2,1)}, bf16[2,112,1536]{2,1,0:T(8,128)(2,1)}, u32[]{:S(2)}, u32[]{:S(2)}) collective-permute-start(bf16[2,112,1536]{2,1,0:T(8,128)(2,1)} %fusion.6), channel_id=1, source_target_pairs={{0,16},{4,20},{8,24},{12,28},{16,0},{20,4},{24,8},{28,12},{1,17},{... | collective-permute-start | bytes 2064392 | tf_op jit(solution)/shard_map/ppermute | solution.py:997
  218.9 39.8 %collective-permute-start.36 = (bf16[2,2,400,768]{3,2,1,0:T(8,128)(2,1)}, bf16[2,2,400,768]{3,2,1,0:T(8,128)(2,1)S(1)}, u32[]{:S(2)}, u32[]{:S(2)}) collective-permute-start(bf16[2,2,400,768]{3,2,1,0:T(8,128)(2,1)} %get-tuple-element.54), channel_id=1, source_target_pairs={{0,4},{4,0},{8,12},{12,8},{16,20},{20,16},{24,28},{28,24},{1,5},{5... | collective-permute-start | bytes 7372808 | tf_op jit(solution)/shard_map/ppermute | solution.py:997
  232.0 10.4 %collective-permute-start.26 = (bf16[96,1536]{1,0:T(8,128)(2,1)S(1)}, bf16[96,1536]{1,0:T(8,128)(2,1)S(1)}, u32[]{:S(2)}, u32[]{:S(2)}) collective-permute-start(bf16[96,1536]{1,0:T(8,128)(2,1)S(1)} %fusion.13), channel_id=1, source_target_pairs={{0,16},{4,20},{8,24},{12,28},{16,0},{20,4},{24,8},{28,12},{1,17},{... | collective-permute-start | bytes 884744 | tf_op jit(solution)/shard_map/ppermute | solution.py:997
  237.0 6.6 %copy-start.9 = (bf16[2,2,384,768]{3,2,1,0:T(8,128)(2,1)S(1)}, bf16[2,2,384,768]{3,2,1,0:T(8,128)(2,1)}, u32[]{:S(2)}) copy-start(bf16[2,2,384,768]{3,2,1,0:T(8,128)(2,1)} %get-tuple-element.51) | copy-start | bytes 7077892
  238.4 8.4 %collective-permute-start.29 = (bf16[112,1536]{1,0:T(8,128)(2,1)S(1)}, bf16[112,1536]{1,0:T(8,128)(2,1)S(1)}, u32[]{:S(2)}, u32[]{:S(2)}) collective-permute-start(bf16[112,1536]{1,0:T(8,128)(2,1)S(1)} %fusion.7), channel_id=1, source_target_pairs={{0,8},{4,12},{8,0},{12,4},{16,24},{20,28},{24,16},{28,20},{1,9},{5... | collective-permute-start | bytes 1032200 | tf_op jit(solution)/shard_map/ppermute | solution.py:997
  245.3 27.2 %collective-permute-start.34 = (bf16[2,384,768]{2,1,0:T(8,128)(2,1)S(1)}, bf16[2,384,768]{2,1,0:T(8,128)(2,1)S(1)}, u32[]{:S(2)}, u32[]{:S(2)}) collective-permute-start(bf16[2,384,768]{2,1,0:T(8,128)(2,1)S(1)} %fusion.3), channel_id=1, source_target_pairs={{0,8},{4,12},{8,0},{12,4},{16,24},{20,28},{24,16},{28,20},{1,9},{5... | collective-permute-start | bytes 3538952 | tf_op jit(solution)/shard_map/ppermute | solution.py:997
  248.1 10.6 %copy-start.8 = (bf16[2,2,400,768]{3,2,1,0:T(8,128)(2,1)S(1)}, bf16[2,2,400,768]{3,2,1,0:T(8,128)(2,1)}, u32[]{:S(2)}) copy-start(bf16[2,2,400,768]{3,2,1,0:T(8,128)(2,1)} %get-tuple-element.53) | copy-start | bytes 7372804
  248.3 15.8 %collective-permute-start.30 = (bf16[25,3072]{1,0:T(8,128)(2,1)S(1)}, bf16[25,3072]{1,0:T(8,128)(2,1)S(1)}, u32[]{:S(2)}, u32[]{:S(2)}) collective-permute-start(bf16[25,3072]{1,0:T(8,128)(2,1)S(1)} %get-tuple-element.80), channel_id=1, source_target_pairs={{0,1},{1,2},{2,3},{3,0},{4,5},{5,6},{6,7},{7,4},{8,9},{9,10},{10,1... | collective-permute-start | bytes 460808 | tf_op jit(solution)/shard_map/ppermute | solution.py:1001
  255.3 14.5 %collective-permute-start.31 = (bf16[25,3072]{1,0:T(8,128)(2,1)S(1)}, bf16[25,3072]{1,0:T(8,128)(2,1)S(1)}, u32[]{:S(2)}, u32[]{:S(2)}) collective-permute-start(bf16[25,3072]{1,0:T(8,128)(2,1)S(1)} %get-tuple-element.81), channel_id=1, source_target_pairs={{0,2},{1,3},{2,0},{3,1},{4,6},{5,7},{6,4},{7,5},{8,10},{9,11},{10,... | collective-permute-start | bytes 460808 | tf_op jit(solution)/shard_map/ppermute | solution.py:1001
  258.7 11.1 %collective-permute-start.32 = (bf16[25,3072]{1,0:T(8,128)(2,1)S(1)}, bf16[25,3072]{1,0:T(8,128)(2,1)S(1)}, u32[]{:S(2)}, u32[]{:S(2)}) collective-permute-start(bf16[25,3072]{1,0:T(8,128)(2,1)S(1)} %get-tuple-element.82), channel_id=1, source_target_pairs={{0,3},{1,0},{2,1},{3,2},{4,7},{5,4},{6,5},{7,6},{8,11},{9,8},{10,9... | collective-permute-start | bytes 460808 | tf_op jit(solution)/shard_map/ppermute | solution.py:1001
  259.0 30.0 %collective-permute-start.37 = (bf16[2,400,768]{2,1,0:T(8,128)(2,1)S(1)}, bf16[2,400,768]{2,1,0:T(8,128)(2,1)S(1)}, u32[]{:S(2)}, u32[]{:S(2)}) collective-permute-start(bf16[2,400,768]{2,1,0:T(8,128)(2,1)S(1)} %fusion), channel_id=1, source_target_pairs={{0,16},{4,20},{8,24},{12,28},{16,0},{20,4},{24,8},{28,12},{1,17},{... | collective-permute-start | bytes 3686408 | tf_op jit(solution)/shard_map/ppermute | solution.py:997
  273.7 24.4 %collective-permute-start.35 = (bf16[384,768]{1,0:T(8,128)(2,1)S(1)}, bf16[384,768]{1,0:T(8,128)(2,1)S(1)}, u32[]{:S(2)}, u32[]{:S(2)}) collective-permute-start(bf16[384,768]{1,0:T(8,128)(2,1)S(1)} %fusion.4), channel_id=1, source_target_pairs={{0,16},{4,20},{8,24},{12,28},{16,0},{20,4},{24,8},{28,12},{1,17},{... | collective-permute-start | bytes 1769480 | tf_op jit(solution)/shard_map/ppermute | solution.py:997
  289.3 10.3 %collective-permute-start.38 = (bf16[400,768]{1,0:T(8,128)(2,1)S(1)}, bf16[400,768]{1,0:T(8,128)(2,1)S(1)}, u32[]{:S(2)}, u32[]{:S(2)}) collective-permute-start(bf16[400,768]{1,0:T(8,128)(2,1)S(1)} %fusion.1), channel_id=1, source_target_pairs={{0,8},{4,12},{8,0},{12,4},{16,24},{20,28},{24,16},{28,20},{1,9},{5... | collective-permute-start | bytes 1843208 | tf_op jit(solution)/shard_map/ppermute | solution.py:997
  300.0 5.3 %copy-start.22 = (bf16[24]{0:T(256)(128)(2,1)S(1)}, bf16[24]{0:T(256)(128)(2,1)}, u32[]{:S(2)}) copy-start(bf16[24]{0:T(256)(128)(2,1)} %param.17) | copy-start | bytes 148
  300.0 5.3 %copy-start.23 = (bf16[24]{0:T(256)(128)(2,1)S(1)}, bf16[24]{0:T(256)(128)(2,1)}, u32[]{:S(2)}) copy-start(bf16[24]{0:T(256)(128)(2,1)} %param.14) | copy-start | bytes 148
  300.1 12.1 %collective-permute-start.39 = (bf16[193,768]{1,0:T(8,128)(2,1)S(1)}, bf16[193,768]{1,0:T(8,128)(2,1)S(1)}, u32[]{:S(2)}, u32[]{:S(2)}) collective-permute-start(bf16[193,768]{1,0:T(8,128)(2,1)S(1)} %pad_maximum_fusion.4), channel_id=1, source_target_pairs={{0,1},{1,2},{2,3},{3,0},{4,5},{5,6},{6,7},{7,4},{8,9},{9,10},{10,1... | collective-permute-start | bytes 889352 | tf_op jit(solution)/shard_map/ppermute | solution.py:1001
  302.1 18.9 %collective-permute-start.40 = (bf16[193,768]{1,0:T(8,128)(2,1)S(1)}, bf16[193,768]{1,0:T(8,128)(2,1)S(1)}, u32[]{:S(2)}, u32[]{:S(2)}) collective-permute-start(bf16[193,768]{1,0:T(8,128)(2,1)S(1)} %pad_maximum_fusion.5), channel_id=1, source_target_pairs={{0,2},{1,3},{2,0},{3,1},{4,6},{5,7},{6,4},{7,5},{8,10},{9,11},{10,... | collective-permute-start | bytes 889352 | tf_op jit(solution)/shard_map/ppermute | solution.py:1001
  302.3 18.7 %collective-permute-start.41 = (bf16[193,768]{1,0:T(8,128)(2,1)S(1)}, bf16[193,768]{1,0:T(8,128)(2,1)S(1)}, u32[]{:S(2)}, u32[]{:S(2)}) collective-permute-start(bf16[193,768]{1,0:T(8,128)(2,1)S(1)} %pad_maximum_fusion.6), channel_id=1, source_target_pairs={{0,3},{1,0},{2,1},{3,2},{4,7},{5,4},{6,5},{7,6},{8,11},{9,8},{10,9... | collective-permute-start | bytes 889352 | tf_op jit(solution)/shard_map/ppermute | solution.py:1001
  (2 other events, 1.5 us)

commit v4 on v3

--- a/solution.py
+++ b/solution.py
@@ -547,7 +547,7 @@
 
 
 def fast_forward_kernel(meta, bucket, x, *rest):
-    pieces, rest = rest[:10], rest[10:]
+    pieces, rest = rest[:10], rest[11:]
     qkv, lse, o, h, c, gains, w, out_t, bias, sem = rest
     copies = load_attn(meta, pieces, w, sem)
     bias[...] = causal_bias()
@@ -556,7 +556,7 @@
     attn_forward_kernel(bucket, x, w, w.at[:, 3 * D : 4 * D], gains, qkv, lse, o, h, c, out_t, bias)
 
 
-def fast_forward(meta, bucket, x, pieces):
+def fast_forward(meta, bucket, x, pieces, earlier):
     total = x.shape[0]
     shape = jax.ShapeDtypeStruct
     return pl.pallas_call(
@@ -569,7 +569,7 @@
             shape((total, D), BF16),
             shape((8, D), F32),
         ),
-        in_specs=smem(2) + vmem(1) + [pl.BlockSpec(memory_space=pl.ANY)] * 10,
+        in_specs=smem(2) + vmem(1) + [pl.BlockSpec(memory_space=pl.ANY)] * 11,
         out_specs=tuple(vmem(6)),
         scratch_shapes=[
             pltpu.VMEM((D, 4 * D + GAIN_LANES), BF16),
@@ -580,7 +580,7 @@
         compiler_params=params(),
         cost_estimate=cost(4.2e9, 10e6),
         name="attn_forward",
-    )(meta, bucket, x, *pieces)
+    )(meta, bucket, x, *pieces, *earlier)
 
 
 def smem(n):
@@ -593,24 +593,77 @@
     )
 
 
+def pack_kernel(qk, value, out, attn_gain, inner_gain, ffn_gain, packed):
+    rows = value.shape[0]
+    packed[:, 0:D] = qk[0]
+    packed[:, D : 2 * D] = qk[1]
+    packed[:, 2 * D : 3 * D] = value[...]
+    packed[:, 3 * D : 4 * D] = out[...]
+    gains = [gain[...].astype(F32) for gain in (attn_gain, inner_gain, ffn_gain)]
+    gains = jnp.concatenate(gains + [jnp.zeros((GAIN_LANES - 3, rows), F32)], axis=0)
+    gains = jnp.concatenate([gains, jnp.zeros((GAIN_LANES, GAIN_LANES - rows), F32)], axis=1)
+    packed[:, 4 * D :] = jnp.transpose(gains)[:rows].astype(BF16)
+
+
+def pack(qk, value, out, gains):
+    rows = value.shape[0]
+    return pl.pallas_call(
+        pack_kernel,
+        out_shape=jax.ShapeDtypeStruct((rows, 4 * D + GAIN_LANES), BF16),
+        in_specs=vmem(6),
+        out_specs=vmem(1)[0],
+        compiler_params=params(),
+        cost_estimate=cost(0, 3e5),
+        name="pack",
+    )(qk, value, out, *[gain.reshape(1, rows) for gain in gains])
+
+
+def order_kernel(meta, *refs):
+    pieces, target = refs[:-1], refs[-1]
+    n = len(pieces)
+    values = [piece[...].astype(F32) for piece in pieces]
+    ordered = []
+    for place in range(n):
+        k = lax.rem(meta[1] + (n - place), n)
+        chosen = values[0]
+        for i in range(1, n):
+            chosen = jnp.where(k == i, values[i], chosen)
+        ordered.append(chosen)
+    target[...] = jnp.concatenate(ordered, axis=0).astype(BF16)
+
+
+def order(meta, pieces):
+    rows, lanes = pieces[0].shape
+    return pl.pallas_call(
+        order_kernel,
+        out_shape=jax.ShapeDtypeStruct((len(pieces) * rows, lanes), BF16),
+        in_specs=smem(1) + vmem(len(pieces)),
+        out_specs=vmem(1)[0],
+        compiler_params=params(),
+        cost_estimate=cost(0, 1e6),
+        name="order",
+    )(meta, *pieces)
+
+
 def load_ffn(meta, pieces, w1, w2, sem):
     blocks, rows = w1.shape[0], pieces[0].shape[2]
     copies = []
-    for core in range(2):
-        own, from_x, from_y, first, second = pieces[5 * core : 5 * core + 5]
+    for group in range(4):
+        core, start = group // 2, group % 2
+        own, from_x, from_y, first, second = pieces[5 * group : 5 * group + 5]
         for flip, one, two in (
-            (0, own.at[:, 0], own.at[:, 1]),
-            (ALONG_X, from_x.at[:, 0], from_x.at[:, 1]),
-            (ALONG_Y, from_y.at[:, 0], from_y.at[:, 1]),
+            (0, own.at[0], own.at[1]),
+            (ALONG_X, from_x.at[0], from_x.at[1]),
+            (ALONG_Y, from_y.at[0], from_y.at[1]),
             (ALONG_X | ALONG_Y, first, second),
         ):
             top = pl.multiple_of((meta[0] ^ (flip | core)) * rows, rows)
-            for k in range(blocks):
-                block = lax.rem(meta[1] + (blocks - k), blocks)
+            for i in range(one.shape[0]):
+                block = lax.rem(meta[1] + (blocks - start - i), blocks)
                 for source, target, slot in ((one, w1, 0), (two, w2, 1)):
                     copies.append(
                         pltpu.make_async_copy(
-                            source.at[k], target.at[block, pl.ds(top, rows)], sem.at[slot]
+                            source.at[i], target.at[block, pl.ds(top, rows)], sem.at[slot]
                         )
                     )
     for copy in copies:
@@ -629,7 +682,7 @@
 
 
 def fast_ffn_kernel(meta, c, h, cot, gain, *rest):
-    pieces, rest = rest[:10], rest[10:]
+    pieces, rest = rest[:20], rest[20:]
     (out, keep1, send1, keep2, send2, dc) = rest[:6]
     (w1, w2, act, slope, back, squeezed, grad_f, grad_gain, c_t, cot_t, turned, sem) = rest[6:]
     blocks, _, cols = w1.shape
@@ -741,7 +794,8 @@
 
 def fast_ffn(meta, c, h, cot, gain, pieces):
     total = c.shape[0]
-    blocks, _, rows, cols = pieces[0].shape
+    blocks, _, cols = gain.shape
+    rows = pieces[0].shape[2]
     shape = jax.ShapeDtypeStruct
     size = blocks * rows
     one, two = shape((2, 2, size, cols), BF16), shape((2, 2, size + PAD, cols), BF16)
@@ -750,7 +804,7 @@
     return pl.pallas_call(
         fast_ffn_kernel,
         out_shape=(shape((total, D), BF16), one, one, two, two, shape((total, D), F32)),
-        in_specs=smem(1) + vmem(4) + [pl.BlockSpec(memory_space=pl.ANY)] * 10,
+        in_specs=smem(1) + vmem(4) + [pl.BlockSpec(memory_space=pl.ANY)] * 20,
         out_specs=tuple(vmem(6)),
         scratch_shapes=[
             pltpu.VMEM((blocks, D, cols), BF16),
@@ -826,7 +880,7 @@
 
 
 def fast_attn_backward_kernel(
-    meta, bucket, x, qkv, do, lse, gains, dy, mixed, gain_rows,
+    meta, bucket, x, qkv, do, lse, gains, dy, mixed, gain_rows, _, __,
     joined, keep1, send1, keep2, send2, grad_q_t, bias, normed, normed_t, mixed_t, turned,
 ):
     rows = normed_t.shape[1]
@@ -932,7 +986,7 @@
     lax.fori_loop(0, PAIRS, heads, 0)
 
 
-def fast_attn_backward(meta, bucket, x, qkv, do, lse, gains, dy, mixed, gain_rows):
+def fast_attn_backward(meta, bucket, x, qkv, do, lse, gains, dy, mixed, gain_rows, earlier):
     total = x.shape[0]
     rows = D // 8
     shape = jax.ShapeDtypeStruct
@@ -940,7 +994,7 @@
     return pl.pallas_call(
         fast_attn_backward_kernel,
         out_shape=(shape((3 * PAIRS, total, PAIR), BF16), one, one, two, two),
-        in_specs=smem(2) + vmem(8),
+        in_specs=smem(2) + vmem(8) + [pl.BlockSpec(memory_space=pl.ANY)] * 2,
         out_specs=tuple(vmem(5)),
         scratch_shapes=[
             pltpu.VMEM((PAIRS, PAIR, total), BF16),
@@ -953,11 +1007,11 @@
         compiler_params=params(),
         cost_estimate=cost(9e9, 15e6),
         name="attn_backward",
-    )(meta, bucket, x, qkv, do, lse, gains, dy, mixed, gain_rows)
+    )(meta, bucket, x, qkv, do, lse, gains, dy, mixed, gain_rows, *earlier)
 
 
 def fast_input_backward_kernel(meta, x, joined, dh, gains, *rest):
-    pieces, rest = rest[:10], rest[10:]
+    pieces, rest = rest[:10], rest[12:]
     grad_x, w, sem = rest
     total = x.shape[0]
     input_gain = gains[0:1]
@@ -976,12 +1030,12 @@
     tiles(total, part)
 
 
-def fast_input_backward(meta, x, joined, dh, gains, pieces):
+def fast_input_backward(meta, x, joined, dh, gains, pieces, earlier):
     total = x.shape[0]
     return pl.pallas_call(
         fast_input_backward_kernel,
         out_shape=jax.ShapeDtypeStruct((total, D), F32),
-        in_specs=smem(1) + vmem(4) + [pl.BlockSpec(memory_space=pl.ANY)] * 10,
+        in_specs=smem(1) + vmem(4) + [pl.BlockSpec(memory_space=pl.ANY)] * 12,
         out_specs=pl.BlockSpec(memory_space=pltpu.VMEM),
         scratch_shapes=[
             pltpu.VMEM((D, 4 * D + GAIN_LANES), BF16),
@@ -990,7 +1044,7 @@
         compiler_params=params(),
         cost_estimate=cost(1.8e9, 10e6),
         name="input_backward",
-    )(meta, x, joined, dh, gains, *pieces)
+    )(meta, x, joined, dh, gains, *pieces, *earlier)
 
 
 def swap(values, flip):
@@ -1005,11 +1059,25 @@
     return values.astype(F32)
 
 
-def reduce_rows(keep, send, first, second):
-    other = swap(send, CORE)
-    one = swap((wide(keep[1]) + wide(other[1])).astype(BF16), first)
-    two = swap((wide(keep[0, 1]) + wide(other[0, 1]) + wide(one[1])).astype(BF16), second)
-    return wide(keep[0, 0]) + wide(other[0, 0]) + wide(one[0]) + wide(two)
+def after(values, *earlier):
+    return lax.optimization_barrier((values, *earlier))[0]
+
+
+def around(own):
+    from_x, from_y = swap(own, ALONG_X), swap(own, ALONG_Y)
+    return [own, from_x, from_y, swap(from_x[0], ALONG_Y), swap(from_y[1], ALONG_X)]
+
+
+def first_sum(keep, core):
+    return (wide(keep[1]) + wide(core[1])).astype(BF16)
+
+
+def second_sum(keep, core, near):
+    return (wide(keep[0, 1]) + wide(core[0, 1]) + wide(near[1])).astype(BF16)
+
+
+def third_sum(keep, core, near, far):
+    return wide(keep[0, 0]) + wide(core[0, 0]) + wide(near[0]) + wide(far)
 
 
 def fast_on_device(n_mp):
@@ -1030,16 +1098,18 @@
         at_dp, at_mp = lax.axis_index("dp"), lax.axis_index("mp")
         meta = jnp.stack([at_dp, at_mp]).astype(jnp.int32)
         slim = value_weight.shape[0]
+        slim_rows = slim * n_mp
         rows, cols = fc1_weight.shape
 
-        gains = jnp.stack([attn_gain, inner_gain, ffn_gain], axis=1)
-        gains = jnp.pad(gains, ((0, 0), (0, GAIN_LANES - 3)))
-        shard = jnp.concatenate(
-            [qk_weight[0], qk_weight[1], value_weight, out_weight, gains], axis=1
+        shard2 = jnp.concatenate(
+            [fc1_weight, fc2_weight.T, jnp.pad(ffn_inner_gain[None], ((0, PAD - 1), (0, 0)))],
+            axis=0,
         )
-        ring = [turn(shard, k, n_mp) for k in range(n_mp - 1, 0, -1)] + [shard]
-        ring = jnp.concatenate(ring + ring[:-1], axis=0)
-        own = lax.dynamic_slice_in_dim(ring, (n_mp - 1 - at_mp) * slim, n_mp * slim, 0)
+        near0 = around(shard2[: 2 * rows].reshape(2, 1, rows, cols))
+
+        shard = pack(qk_weight, value_weight, out_weight, (attn_gain, inner_gain, ffn_gain))
+        own = order(meta, [shard] + [turn(shard, k, n_mp) for k in range(1, n_mp)])
+        own = after(own, near0[3], near0[4])
         from_x, from_y = swap(own, ALONG_X), swap(own, ALONG_Y)
         cut = own.shape[1] // 2 // 128 * 128
         near = [
@@ -1051,29 +1121,47 @@
         ]
         attn_pieces = near + [swap(piece, CORE) for piece in near]
 
-        shard = jnp.concatenate(
-            [fc1_weight, fc2_weight.T, jnp.pad(ffn_inner_gain[None], ((0, PAD - 1), (0, 0)))],
-            axis=0,
-        )
-        ring = [shard] + [turn(shard, k, n_mp) for k in range(1, n_mp)]
-        hidden_gain = jnp.stack([piece[2 * rows] for piece in ring]).astype(F32)[:, None]
-        own = jnp.stack([piece[: 2 * rows].reshape(2, rows, cols) for piece in ring])
-        from_x, from_y = swap(own, ALONG_X), swap(own, ALONG_Y)
-        near = [
-            own,
-            from_x,
-            from_y,
-            swap(from_x[:, 0], ALONG_Y),
-            swap(from_y[:, 1], ALONG_X),
-        ]
-        ffn_pieces = near + [swap(piece, CORE) for piece in near]
-
-        qkv, lse, o, h, c, gains = fast_forward(meta, bucket, tokens, attn_pieces)
+        shard2 = after(shard2, own)
+        ring = [turn(shard2, k, n_mp) for k in range(1, n_mp)]
+        ring = [after(piece, near[3], near[4]) for piece in ring]
+        hidden_gain = [shard2[2 * rows]] + [piece[2 * rows] for piece in ring]
+        hidden_gain = jnp.stack(hidden_gain).astype(F32)[:, None]
+        others = jnp.concatenate(
+            [piece[half * rows : (half + 1) * rows] for half in range(2) for piece in ring], axis=0
+        ).reshape(2, n_mp - 1, rows, cols)
+        from_x, from_y = swap(others, ALONG_X), swap(others, ALONG_Y)
+        qkv, lse, o, h, c, gains = fast_forward(meta, bucket, tokens, attn_pieces, [others])
+        late_x, late_y = after(from_x[0], c), after(from_y[1], c)
+        near = [others, from_x, from_y, swap(late_x, ALONG_Y), swap(late_y, ALONG_X)]
+        ffn_pieces = near0 + near + [swap(piece, CORE) for piece in near0 + near]
+
         output, keep1, send1, keep2, send2, dc = fast_ffn(
             meta, c, h, cotangent, hidden_gain, ffn_pieces
         )
-        sum1 = reduce_rows(keep1, send1, ALONG_X, ALONG_Y)
-        sum2 = reduce_rows(keep2, send2, ALONG_Y, ALONG_X)
+        core1, core2 = swap(send1, CORE), swap(send2, CORE)
+        dh, do, dy, mixed, gain_rows = fast_out_backward(
+            meta, dc, cotangent, h, o, gains, attn_pieces
+        )
+        core1, core2 = after(core1, dy), after(core2, dy)
+        first1, first2 = first_sum(keep1, core1), first_sum(keep2, core2)
+        near1, near2 = swap(first1, ALONG_X), swap(first2, ALONG_Y)
+        joined, keep3, send3, keep4, send4 = fast_attn_backward(
+            meta, bucket, tokens, qkv, do, lse, gains, dy, mixed, gain_rows, [first1, first2]
+        )
+        near1, near2 = after(near1, send3), after(near2, send3)
+        core3 = swap(after(send3, near1, near2), CORE)
+        core4 = swap(after(send4, near1, near2), CORE)
+        second1, second2 = second_sum(keep1, core1, near1), second_sum(keep2, core2, near2)
+        far1, far2 = swap(second1, ALONG_Y), swap(second2, ALONG_X)
+        core3, core4 = after(core3, second1, second2), after(core4, second1, second2)
+        first3, first4 = first_sum(keep3, core3), first_sum(keep4, core4)
+        near3, near4 = swap(first3, ALONG_X), swap(first4, ALONG_Y)
+        token_gradient = fast_input_backward(
+            meta, tokens, joined, dh, gains, attn_pieces, [first3, first4]
+        )
+        far1, far2 = after(far1, token_gradient), after(far2, token_gradient)
+        sum1 = third_sum(keep1, core1, near1, far1)
+        sum2 = third_sum(keep2, core2, near2, far2)
         size = n_mp * rows
         blocks = [
             jnp.concatenate(
@@ -1086,21 +1174,18 @@
             )
             for k in range(n_mp)
         ]
+        turned = [turn(blocks[k].astype(BF16), k, n_mp) for k in range(1, n_mp)]
+
+        near3, near4 = after(near3, sum1, sum2), after(near4, sum1, sum2)
+        far3 = swap(second_sum(keep3, core3, near3), ALONG_Y)
+        far4 = swap(second_sum(keep4, core4, near4), ALONG_X)
+        sum1 = third_sum(keep3, core3, near3, far3)
+        sum2 = third_sum(keep4, core4, near4, far4)
         ffn_share = blocks[0]
-        for k in range(1, n_mp):
-            ffn_share = ffn_share + wide(turn(blocks[k].astype(BF16), k, n_mp))
-
-        dh, do, dy, mixed, gain_rows = fast_out_backward(
-            meta, dc, cotangent, h, o, gains, attn_pieces
-        )
-        joined, keep1, send1, keep2, send2 = fast_attn_backward(
-            meta, bucket, tokens, qkv, do, lse, gains, dy, mixed, gain_rows
-        )
-        token_gradient = fast_input_backward(meta, tokens, joined, dh, gains, attn_pieces)
-        sum1 = reduce_rows(keep1, send1, ALONG_X, ALONG_Y)
-        sum2 = reduce_rows(keep2, send2, ALONG_Y, ALONG_X)
-        both = jnp.concatenate([sum1, sum2[:rows]], axis=1)
-        extra = jnp.pad(sum2[rows : rows + 1], ((0, 0), (0, 2 * D)))
+        for piece in turned:
+            ffn_share = ffn_share + wide(after(piece, sum1, sum2))
+        both = jnp.concatenate([sum1, sum2[:slim_rows]], axis=1)
+        extra = jnp.pad(sum2[slim_rows : slim_rows + 1], ((0, 0), (0, 2 * D)))
 
         def block(k):
             at = lax.rem(at_mp + k, n_mp) * slim

time: 329 us -> 263 us (0.80)
  waiting for transfers between devices: 143 us -> 63.3 us
  starting transfers between devices: 43.7 us -> 56.4 us
  local copies, waits for them, and re-layouts: 24 us -> 17.7 us
  other arithmetic: 21.1 us -> 27.1 us
  Pallas kernels: 89.3 us -> 93.2 us
    ppermute x30 -> x39, waiting for transfers between devices: 92.2 us -> 45.2 us  [swap(): return lax.ppermute(values, 'dp', [(i, i ^ flip) for i in range(8)])]
    ppermute x12, waiting for transfers between devices: 50.4 us -> 18.1 us  [turn(): return lax.ppermute(values, 'mp', [(i, (i + k) % n) for i in range(n)])]
    ppermute x5 -> x0, local copies, waits for them, and re-layouts: 9.44 us -> none  [swap(): return lax.ppermute(values, 'dp', [(i, i ^ flip) for i in range(8)])]
    ppermute x30 -> x39, starting transfers between devices: 17.5 us -> 25.8 us  [swap(): return lax.ppermute(values, 'dp', [(i, i ^ flip) for i in range(8)])]
    convert_element_type x9, other arithmetic: 10.8 us -> 15.6 us  [the longest x4 7.86 us: first_sum(): return (wide(keep[1]) + wide(core[1])).astype(BF16)]
    ppermute x12, starting transfers between devices: 26.2 us -> 30.6 us  [turn(): return lax.ppermute(values, 'mp', [(i, (i + k) % n) for i in range(n)])]
    pallas_call x0 -> x2, Pallas kernels: none -> 3.87 us  [the longest x1 2.2 us: order(): pl.pallas_call(order_kernel, out_shape=jax.ShapeDtypeStruct((len(pieces)...]
    unnamed x62 -> x95, local copies, waits for them, and re-layouts: 6.24 us -> 8.66 us
  transfers between devices with their start and end apart: 42 -> 51, of which waited for: 19 -> 16; matrix products, arithmetic and copies ran while one was open for 11% -> 12% of each run, Pallas kernels for 8% -> 23%
where the time goes in v4:
time: 263 us; the launch traced here: 260 us
  Pallas kernels  93.2 us (35%)
  waiting for transfers between devices  63.3 us (24%)
  starting transfers between devices  56.4 us (21%)
  other arithmetic  27.1 us (10%)
  local copies, waits for them, and re-layouts  17.7 us (7%)
    ppermute x39, waiting for transfers between devices, swap(): return lax.ppermute(values, 'dp', [(i, i ^ flip) for i in range(8)])  45.2 us
    pallas_call x1, Pallas kernels, fast_ffn(): pl.pallas_call(fast_ffn_kernel, out_shape=(shape((total, D), BF16), one,...  33.2 us
    ppermute x12, starting transfers between devices, turn(): return lax.ppermute(values, 'mp', [(i, (i + k) % n) for i in range(n)])  30.6 us
    ppermute x39, starting transfers between devices, swap(): return lax.ppermute(values, 'dp', [(i, i ^ flip) for i in range(8)])  25.8 us
    pallas_call x1, Pallas kernels, fast_attn_backward(): pl.pallas_call(fast_attn_backward_kernel, out_shape=(shape((3 * PAIRS, to...  21.8 us
    ppermute x12, waiting for transfers between devices, turn(): return lax.ppermute(values, 'mp', [(i, (i + k) % n) for i in range(n)])  18.1 us
    pallas_call x1, Pallas kernels, fast_forward(): pl.pallas_call(fast_forward_kernel, out_shape=(shape((3 * PAIRS, total, P...  16.9 us
    pallas_call x1, Pallas kernels, fast_out_backward(): pl.pallas_call(fast_out_backward_kernel, out_shape=(shape((total, D), F32...  8.92 us
  transfers between devices with their start and end apart: 51, of which 16 were waited for; matrix products, arithmetic and copies ran while one was open for 12% of the time, Pallas kernels for 23%

profile of v4, /device:TPU:0, one launch (start us, length us, event | category | flops | bytes accessed | tf_op | source)
XLA Modules:
  0.0 259.8 jit_solution(13496923764157297762)
XLA Ops:
  0.7 1.8 pad_maximum_fusion.6
  2.4 2.9 %collective-permute-start.3 = (bf16[2,1,96,768]{3,2,1,0:T(8,128)(2,1)}, bf16[2,1,96,768]{3,2,1,0:T(8,128)(2,1)}, u32[]{:S(2)}, u32[]{:S(2)}) collective-permute-start(bf16[2,1,96,768]{3,2,1,0:T(8,128)(2,1)} %bitcast.6.rest_0_), channel_id=1, source_target_pairs={{0,8},{4,12},{8,0},{12,4},{16,24},{20,28},{24,16},{28,20},{1,9},{5... | collective-permute-start | bytes 884744 | tf_op jit(solution)/shard_map/ppermute | solution.py:1051
  5.4 1.5 collective-permute-start.5
  6.9 1.7 pack.1.refs_0_
  8.6 1.6 collective-permute-start
  10.1 2.6 collective-permute-start.1
  12.7 1.3 collective-permute-start.2
  14.1 0.9 slice_bitcast_fusion.4
  15.6 0.9 slice_bitcast_fusion.3
  16.5 1.4 collective-permute-start.6
  18.5 3.9 %collective-permute-done.1.refs_2_ = bf16[24,3200]{1,0:T(8,128)(2,1)S(1)} collective-permute-done((bf16[24,3200]{1,0:T(8,128)(2,1)}, bf16[24,3200]{1,0:T(8,128)(2,1)S(1)}, u32[]{:S(2)}, u32[]{:S(2)}) %collective-permute-start.1) | collective-permute-done | bytes 153632 | tf_op jit(solution)/shard_map/ppermute | solution.py:1055
  23.8 2.2 order.1.rest_0_
  27.8 2.4 collective-permute-start.17
  30.2 12.4 %collective-permute-done.8.rest_2_ = bf16[96,3200]{1,0:T(8,128)(2,1)S(1)} collective-permute-done((bf16[96,3200]{1,0:T(8,128)(2,1)}, bf16[96,3200]{1,0:T(8,128)(2,1)S(1)}, u32[]{:S(2)}, u32[]{:S(2)}) %collective-permute-start.8) | collective-permute-done | bytes 614432 | tf_op jit(solution)/shard_map/ppermute | solution.py:1051
  43.2 3.2 %collective-permute-start.16 = (bf16[208,768]{1,0:T(8,128)(2,1)S(1)}, bf16[208,768]{1,0:T(8,128)(2,1)S(1)}, u32[]{:S(2)}, u32[]{:S(2)}) collective-permute-start(bf16[208,768]{1,0:T(8,128)(2,1)S(1)} %fusion.17), channel_id=1, source_target_pairs={{0,1},{1,2},{2,3},{3,0},{4,5},{5,6},{6,7},{7,4},{8,9},{9,10},{10,1... | collective-permute-start | bytes 958472 | tf_op jit(solution)/shard_map/ppermute | solution.py:1055
  47.0 1.7 collective-permute-start.18
  48.8 5.2 %collective-permute-done.9.rest_3_ = bf16[96,1536]{1,0:T(8,128)(2,1)S(1)} collective-permute-done((bf16[96,1536]{1,0:T(8,128)(2,1)S(1)}, bf16[96,1536]{1,0:T(8,128)(2,1)S(1)}, u32[]{:S(2)}, u32[]{:S(2)}) %collective-permute-start.9) | collective-permute-done | bytes 294944 | tf_op jit(solution)/shard_map/ppermute | solution.py:1051
  54.5 1.0 collective-permute-done.16
  56.2 3.8 %collective-permute-done.18 = bf16[208,768]{1,0:T(8,128)(2,1)S(1)} collective-permute-done((bf16[208,768]{1,0:T(8,128)(2,1)S(1)}, bf16[208,768]{1,0:T(8,128)(2,1)S(1)}, u32[]{:S(2)}, u32[]{:S(2)}) %collective-permute-start.18) | collective-permute-done | bytes 319520 | tf_op jit(solution)/shard_map/ppermute | solution.py:1055
  64.0 1.6 collective-permute-start.19
  66.5 0.8 copy-done.7
  68.5 16.9 %attn_forward.1 = (bf16[18,512,128]{2,1,0:T(8,128)(2,1)}, f32[12,1,512]{2,1,0:T(1,128)}, f32[512,768]{1,0:T(8,128)}, f32[512,768]{1,0:T(8,128)}, bf16[512,768]{1,0:T(8,128)(2,1)}, /*index=5*/f32[8,768]{1,0:T(8,128)}) custom-call(s32[2]{0:T(128)} %pad_add_fusion.meta, s32[1]{0:T(128)S(6)} %copy.28.bucket, bf16[512,768]{1,0:T(8,128)(2,1)} %x.9, ...), custom_call_target="tpu_custom_call" | custom-call | flops 4200000000 | bytes 10000000 | tf_op jit(solution)/shard_map/attn_forward/pallas_call | solution.py:562
  85.6 1.0 slice_bitcast_fusion
  87.1 1.0 slice_bitcast_fusion.1
  88.1 1.5 collective-permute-start.22
  89.6 0.9 collective-permute-start.21
  91.9 8.5 %collective-permute-done.22.rest_9_ = bf16[3,96,768]{2,1,0:T(8,128)(2,1)S(1)} collective-permute-done((bf16[3,96,768]{2,1,0:T(8,128)(2,1)S(1)}, bf16[3,96,768]{2,1,0:T(8,128)(2,1)S(1)}, u32[]{:S(2)}, u32[]{:S(2)}) %collective-permute-start.22) | collective-permute-done | bytes 442400 | tf_op jit(solution)/shard_map/ppermute | solution.py:1051
  100.4 1.0 collective-permute-done.21.rest_8_
  103.5 0.8 copy-done.39
  105.3 33.2 %feed_forward.1 = (bf16[512,768]{1,0:T(8,128)(2,1)}, bf16[2,2,384,768]{3,2,1,0:T(8,128)(2,1)}, bf16[2,2,384,768]{3,2,1,0:T(8,128)(2,1)}, bf16[2,2,400,768]{3,2,1...) custom-call(s32[2]{0:T(128)} %pad_add_fusion.meta, bf16[512,768]{1,0:T(8,128)(2,1)} %get-tuple-element.60.c, ...), custom_call_target="tpu_custom_call" | custom-call | flops 14499999744 | bytes 20000000 | tf_op jit(solution)/shard_map/feed_forward/pallas_call | solution.py:804
  139.2 8.9 %out_backward.1 = (f32[512,768]{1,0:T(8,128)}, bf16[6,512,128]{2,1,0:T(8,128)(2,1)}, bf16[512,768]{1,0:T(8,128)(2,1)}, bf16[512,768]{1,0:T(8,128)(2,1)}, f32[8,768]{1,0:T(8,128)}) custom-call(s32[2]{0:T(128)} %pad_add_fusion.meta, f32[512,768]{1,0:T(8,128)} %get-tuple-element.66.dc, bf16[512,768]{1,0:T(8,128)(2,1)} %cot.3, f32[512,768]{1,0:T(8,128)} %get-tuple-element.61.h, ...), custom_call_target="tpu_custom_call" | custom-call | flops 1200000000 | bytes 10000000 | tf_op jit(solution)/shard_map/out_backward/pallas_call | solution.py:861
  148.2 2.8 %fusion.__ = bf16[2,400,768]{2,1,0:T(8,128)(2,1)} fusion(bf16[2,2,400,768]{3,2,1,0:T(8,128)(2,1)} %collective-permute-done.34, bf16[2,2,400,768]{3,2,1,0:T(8,128)(2,1)S(1)} %copy-done.4), kind=kLoop, calls=%fused_computation.11 | loop fusion | flops 2457600 | bytes 3686400 | tf_op jit(solution)/shard_map/convert_element_type | solution.py:1072
  150.9 1.4 collective-permute-start.36
  152.4 2.6 %fusion.3._ = bf16[2,384,768]{2,1,0:T(8,128)(2,1)} fusion(bf16[2,2,384,768]{3,2,1,0:T(8,128)(2,1)} %collective-permute-done.33, bf16[2,2,384,768]{3,2,1,0:T(8,128)(2,1)S(1)} %copy-done.9), kind=kLoop, calls=%fused_computation.16 | loop fusion | flops 2359296 | bytes 3538944 | tf_op jit(solution)/shard_map/convert_element_type | solution.py:1072
  155.0 0.8 collective-permute-start.35
  155.9 21.8 %attn_backward.1 = (bf16[18,512,128]{2,1,0:T(8,128)(2,1)}, bf16[2,2,96,1536]{3,2,1,0:T(8,128)(2,1)}, bf16[2,2,96,1536]{3,2,1,0:T(8,128)(2,1)}, bf16[2,2,112,1536...) custom-call(s32[2]{0:T(128)} %pad_add_fusion.meta, s32[1]{0:T(128)S(6)} %copy.28.bucket, bf16[512,768]{1,0:T(8,128)(2,1)} %x.9, ...), custom_call_target="tpu_custom_call" | custom-call | flops 8999999488 | bytes 15000000 | tf_op jit(solution)/shard_map/attn_backward/pallas_call | solution.py:994
  177.7 5.7 %collective-permute-done.35 = bf16[2,384,768]{2,1,0:T(8,128)(2,1)} collective-permute-done((bf16[2,384,768]{2,1,0:T(8,128)(2,1)}, bf16[2,384,768]{2,1,0:T(8,128)(2,1)}, u32[]{:S(2)}, u32[]{:S(2)}) %collective-permute-start.35) | collective-permute-done | bytes 1179680 | tf_op jit(solution)/shard_map/ppermute | solution.py:1051
  183.9 2.5 fusion.5
  187.0 2.3 fusion.2
  190.0 1.2 fusion.12.rest_10_
  191.2 1.3 collective-permute-start.39
  192.6 1.3 fusion.6.rest_11_
  193.8 1.5 collective-permute-start.43
  195.4 8.5 %input_backward.1 = f32[512,768]{1,0:T(8,128)} custom-call(s32[2]{0:T(128)} %pad_add_fusion.meta, bf16[512,768]{1,0:T(8,128)(2,1)} %x.9, bf16[18,512,128]{2,1,0:T(8,128)(2,1)} %get-tuple-element.80.joined, f32[512,768]{1,0:T(8,128)} %get-tuple-element.81.dh, f32[8,768]{1,0:T(8,128)} %get-tuple-element.68.gains, bf16[96,3200]{1,0:T(8,128)(2,1)} %order.1.rest_0_, ...), custom_call_target="tpu_custom_call" | custom-call | flops 1800000000 | bytes 10000000 | tf_op jit(solution)/shard_map/input_backward/pallas_call | solution.py:1035
  203.9 2.4 collective-permute-done.41
  206.3 1.8 fusion.29
  208.1 1.9 fusion.27
  210.8 3.2 %collective-permute-start.49 = (bf16[193,768]{1,0:T(8,128)(2,1)S(1)}, bf16[193,768]{1,0:T(8,128)(2,1)S(1)}, u32[]{:S(2)}, u32[]{:S(2)}) collective-permute-start(bf16[193,768]{1,0:T(8,128)(2,1)S(1)} %pad_maximum_fusion.4), channel_id=1, source_target_pairs={{0,2},{1,3},{2,0},{3,1},{4,6},{5,7},{6,4},{7,5},{8,10},{9,11},{10,... | collective-permute-start | bytes 889352 | tf_op jit(solution)/shard_map/ppermute | solution.py:1055
  214.3 3.5 %collective-permute-done.39 = bf16[2,96,1536]{2,1,0:T(8,128)(2,1)} collective-permute-done((bf16[2,96,1536]{2,1,0:T(8,128)(2,1)S(1)}, bf16[2,96,1536]{2,1,0:T(8,128)(2,1)}, u32[]{:S(2)}, u32[]{:S(2)}) %collective-permute-start.39) | collective-permute-done | bytes 589856 | tf_op jit(solution)/shard_map/ppermute | solution.py:1051
  217.7 1.2 fusion.13
  218.9 1.5 collective-permute-start.42
  220.4 1.2 fusion.7
  221.6 0.9 collective-permute-start.44
  222.5 4.3 %collective-permute-done.42 = bf16[96,1536]{1,0:T(8,128)(2,1)S(1)} collective-permute-done((bf16[96,1536]{1,0:T(8,128)(2,1)S(1)}, bf16[96,1536]{1,0:T(8,128)(2,1)S(1)}, u32[]{:S(2)}, u32[]{:S(2)}) %collective-permute-start.42) | collective-permute-done | bytes 294944 | tf_op jit(solution)/shard_map/ppermute | solution.py:1051
  226.8 1.2 fusion.14
  228.0 2.2 collective-permute-done.44
  230.2 1.2 fusion.8
  232.3 11.3 %collective-permute-start.45 = (bf16[25,3072]{1,0:T(8,128)(2,1)S(1)}, bf16[25,3072]{1,0:T(8,128)(2,1)S(1)}, u32[]{:S(2)}, u32[]{:S(2)}) collective-permute-start(bf16[25,3072]{1,0:T(8,128)(2,1)S(1)} %get-tuple-element.124), channel_id=1, source_target_pairs={{0,1},{1,2},{2,3},{3,0},{4,5},{5,6},{6,7},{7,4},{8,9},{9,10},{10,1... | collective-permute-start | bytes 460808 | tf_op jit(solution)/shard_map/ppermute | solution.py:1055
  243.6 2.4 collective-permute-start.47
  246.2 0.8 slice_bitcast_fusion.2
  247.7 1.2 collective-permute-done.45
  248.9 6.3 %collective-permute-done.46 = bf16[25,3072]{1,0:T(8,128)(2,1)S(1)} collective-permute-done((bf16[25,3072]{1,0:T(8,128)(2,1)S(1)}, bf16[25,3072]{1,0:T(8,128)(2,1)S(1)}, u32[]{:S(2)}, u32[]{:S(2)}) %collective-permute-start.46) | collective-permute-done | bytes 153632 | tf_op jit(solution)/shard_map/ppermute | solution.py:1055
  255.1 1.3 collective-permute-done.47
  256.5 0.8 multiply_reduce_fusion
  (195 shorter events, 24.8 us)
Async XLA Ops:
  0.6 27.1 %copy-start.30 = (bf16[768]{0:T(1024)(128)(2,1)S(1)}, bf16[768]{0:T(1024)(128)(2,1)}, u32[]{:S(2)}) copy-start(bf16[768]{0:T(1024)(128)(2,1)} %param.21) | copy-start | bytes 4612
  0.7 27.1 %copy-start.18 = (bf16[768,96]{0,1:T(8,128)(2,1)S(1)}, bf16[768,96]{0,1:T(8,128)(2,1)}, u32[]{:S(2)}) copy-start(bf16[768,96]{0,1:T(8,128)(2,1)} %param.22) | copy-start | bytes 442372
  0.7 27.1 %copy-start.19 = (bf16[96,768]{1,0:T(8,128)(2,1)S(1)}, bf16[96,768]{1,0:T(8,128)(2,1)}, u32[]{:S(2)}) copy-start(bf16[96,768]{1,0:T(8,128)(2,1)} %param.20) | copy-start | bytes 442372
  2.4 11.6 %collective-permute-start.3 = (bf16[2,1,96,768]{3,2,1,0:T(8,128)(2,1)}, bf16[2,1,96,768]{3,2,1,0:T(8,128)(2,1)}, u32[]{:S(2)}, u32[]{:S(2)}) collective-permute-start(bf16[2,1,96,768]{3,2,1,0:T(8,128)(2,1)} %bitcast.6.rest_0_), channel_id=1, source_target_pairs={{0,8},{4,12},{8,0},{12,4},{16,24},{20,28},{24,16},{28,20},{1,9},{5... | collective-permute-start | bytes 884744 | tf_op jit(solution)/shard_map/ppermute | solution.py:1051
  5.4 10.2 %collective-permute-start.5 = (bf16[2,1,96,768]{3,2,1,0:T(8,128)(2,1)}, bf16[2,1,96,768]{3,2,1,0:T(8,128)(2,1)}, u32[]{:S(2)}, u32[]{:S(2)}) collective-permute-start(bf16[2,1,96,768]{3,2,1,0:T(8,128)(2,1)} %bitcast.6.rest_0_), channel_id=1, source_target_pairs={{0,16},{4,20},{8,24},{12,28},{16,0},{20,4},{24,8},{28,12},{1,17},{... | collective-permute-start | bytes 884744 | tf_op jit(solution)/shard_map/ppermute | solution.py:1051
  8.6 10.0 %collective-permute-start = (bf16[24,3200]{1,0:T(8,128)(2,1)}, bf16[24,3200]{1,0:T(8,128)(2,1)S(1)}, u32[]{:S(2)}, u32[]{:S(2)}) collective-permute-start(bf16[24,3200]{1,0:T(8,128)(2,1)} %pack.1.refs_0_), channel_id=1, source_target_pairs={{0,1},{1,2},{2,3},{3,0},{4,5},{5,6},{6,7},{7,4},{8,9},{9,10},{10,1... | collective-permute-start | bytes 460808 | tf_op jit(solution)/shard_map/ppermute | solution.py:1055
  10.1 12.3 %collective-permute-start.1 = (bf16[24,3200]{1,0:T(8,128)(2,1)}, bf16[24,3200]{1,0:T(8,128)(2,1)S(1)}, u32[]{:S(2)}, u32[]{:S(2)}) collective-permute-start(bf16[24,3200]{1,0:T(8,128)(2,1)} %pack.1.refs_0_), channel_id=1, source_target_pairs={{0,2},{1,3},{2,0},{3,1},{4,6},{5,7},{6,4},{7,5},{8,10},{9,11},{10,... | collective-permute-start | bytes 460808 | tf_op jit(solution)/shard_map/ppermute | solution.py:1055
  12.7 9.7 %collective-permute-start.2 = (bf16[24,3200]{1,0:T(8,128)(2,1)}, bf16[24,3200]{1,0:T(8,128)(2,1)S(1)}, u32[]{:S(2)}, u32[]{:S(2)}) collective-permute-start(bf16[24,3200]{1,0:T(8,128)(2,1)} %pack.1.refs_0_), channel_id=1, source_target_pairs={{0,3},{1,0},{2,1},{3,2},{4,7},{5,4},{6,5},{7,6},{8,11},{9,8},{10,9... | collective-permute-start | bytes 460808 | tf_op jit(solution)/shard_map/ppermute | solution.py:1055
  15.0 11.0 %collective-permute-start.4 = (bf16[1,96,768]{2,1,0:T(8,128)(2,1)S(1)}, bf16[1,96,768]{2,1,0:T(8,128)(2,1)S(1)}, u32[]{:S(2)}, u32[]{:S(2)}) collective-permute-start(bf16[1,96,768]{2,1,0:T(8,128)(2,1)S(1)} %slice_bitcast_fusion.4), channel_id=1, source_target_pairs={{0,16},{4,20},{8,24},{12,28},{16,0},{20,4},{24,8},{28,12},{1,17},{... | collective-permute-start | bytes 442376 | tf_op jit(solution)/shard_map/ppermute | solution.py:1051
  16.5 10.2 %collective-permute-start.6 = (bf16[1,96,768]{2,1,0:T(8,128)(2,1)S(1)}, bf16[1,96,768]{2,1,0:T(8,128)(2,1)}, u32[]{:S(2)}, u32[]{:S(2)}) collective-permute-start(bf16[1,96,768]{2,1,0:T(8,128)(2,1)S(1)} %slice_bitcast_fusion.3), channel_id=1, source_target_pairs={{0,8},{4,12},{8,0},{12,4},{16,24},{20,28},{24,16},{28,20},{1,9},{5... | collective-permute-start | bytes 442376 | tf_op jit(solution)/shard_map/ppermute | solution.py:1051
  26.0 22.7 %copy-start = (bf16[96,3200]{1,0:T(8,128)(2,1)S(1)}, bf16[96,3200]{1,0:T(8,128)(2,1)}, u32[]{:S(2)}) copy-start(bf16[96,3200]{1,0:T(8,128)(2,1)} %order.1.rest_0_) | copy-start | bytes 1843204
  26.7 15.9 %collective-permute-start.8 = (bf16[96,3200]{1,0:T(8,128)(2,1)}, bf16[96,3200]{1,0:T(8,128)(2,1)S(1)}, u32[]{:S(2)}, u32[]{:S(2)}) collective-permute-start(bf16[96,3200]{1,0:T(8,128)(2,1)} %order.1.rest_0_), channel_id=1, source_target_pairs={{0,16},{4,20},{8,24},{12,28},{16,0},{20,4},{24,8},{28,12},{1,17},{... | collective-permute-start | bytes 1843208 | tf_op jit(solution)/shard_map/ppermute | solution.py:1051
  27.2 19.2 %collective-permute-start.7 = (bf16[96,3200]{1,0:T(8,128)(2,1)}, bf16[96,3200]{1,0:T(8,128)(2,1)S(1)}, u32[]{:S(2)}, u32[]{:S(2)}) collective-permute-start(bf16[96,3200]{1,0:T(8,128)(2,1)} %order.1.rest_0_), channel_id=1, source_target_pairs={{0,8},{4,12},{8,0},{12,4},{16,24},{20,28},{24,16},{28,20},{1,9},{5... | collective-permute-start | bytes 1843208 | tf_op jit(solution)/shard_map/ppermute | solution.py:1051
  27.8 35.0 %copy-start.20 = (bf16[208,768]{1,0:T(8,128)(2,1)}, bf16[208,768]{1,0:T(8,128)(2,1)S(1)}, u32[]{:S(2)}) copy-start(bf16[208,768]{1,0:T(8,128)(2,1)S(1)} %fusion.17) | copy-start | bytes 958468
  27.8 20.9 %collective-permute-start.17 = (bf16[208,768]{1,0:T(8,128)(2,1)S(1)}, bf16[208,768]{1,0:T(8,128)(2,1)S(1)}, u32[]{:S(2)}, u32[]{:S(2)}) collective-permute-start(bf16[208,768]{1,0:T(8,128)(2,1)S(1)} %fusion.17), channel_id=1, source_target_pairs={{0,2},{1,3},{2,0},{3,1},{4,6},{5,7},{6,4},{7,5},{8,10},{9,11},{10,... | collective-permute-start | bytes 958472 | tf_op jit(solution)/shard_map/ppermute | solution.py:1055
  42.6 20.2 %copy-start.1 = (bf16[96,3200]{1,0:T(8,128)(2,1)}, bf16[96,3200]{1,0:T(8,128)(2,1)S(1)}, u32[]{:S(2)}) copy-start(bf16[96,3200]{1,0:T(8,128)(2,1)S(1)} %collective-permute-done.8.rest_2_) | copy-start | bytes 1843204
  42.6 11.4 %collective-permute-start.10 = (bf16[96,1664]{1,0:T(8,128)(2,1)S(1)}, bf16[96,1664]{1,0:T(8,128)(2,1)S(1)}, u32[]{:S(2)}, u32[]{:S(2)}) collective-permute-start(bf16[96,1664]{1,0:T(8,128)(2,1)S(1)} %slice.313), channel_id=1, source_target_pairs={{0,8},{4,12},{8,0},{12,4},{16,24},{20,28},{24,16},{28,20},{1,9},{5... | collective-permute-start | bytes 958472 | tf_op jit(solution)/shard_map/ppermute | solution.py:1051
  43.2 12.3 %collective-permute-start.16 = (bf16[208,768]{1,0:T(8,128)(2,1)S(1)}, bf16[208,768]{1,0:T(8,128)(2,1)S(1)}, u32[]{:S(2)}, u32[]{:S(2)}) collective-permute-start(bf16[208,768]{1,0:T(8,128)(2,1)S(1)} %fusion.17), channel_id=1, source_target_pairs={{0,1},{1,2},{2,3},{3,0},{4,5},{5,6},{6,7},{7,4},{8,9},{9,10},{10,1... | collective-permute-start | bytes 958472 | tf_op jit(solution)/shard_map/ppermute | solution.py:1055
  46.4 21.6 %copy-start.2 = (bf16[96,3200]{1,0:T(8,128)(2,1)}, bf16[96,3200]{1,0:T(8,128)(2,1)S(1)}, u32[]{:S(2)}) copy-start(bf16[96,3200]{1,0:T(8,128)(2,1)S(1)} %collective-permute-done.7.rest_1_) | copy-start | bytes 1843204
  46.4 7.6 %collective-permute-start.9 = (bf16[96,1536]{1,0:T(8,128)(2,1)S(1)}, bf16[96,1536]{1,0:T(8,128)(2,1)S(1)}, u32[]{:S(2)}, u32[]{:S(2)}) collective-permute-start(bf16[96,1536]{1,0:T(8,128)(2,1)S(1)} %slice.312), channel_id=1, source_target_pairs={{0,16},{4,20},{8,24},{12,28},{16,0},{20,4},{24,8},{28,12},{1,17},{... | collective-permute-start | bytes 884744 | tf_op jit(solution)/shard_map/ppermute | solution.py:1051
  47.0 13.1 %collective-permute-start.18 = (bf16[208,768]{1,0:T(8,128)(2,1)S(1)}, bf16[208,768]{1,0:T(8,128)(2,1)S(1)}, u32[]{:S(2)}, u32[]{:S(2)}) collective-permute-start(bf16[208,768]{1,0:T(8,128)(2,1)S(1)} %fusion.17), channel_id=1, source_target_pairs={{0,3},{1,0},{2,1},{3,2},{4,7},{5,4},{6,5},{7,6},{8,11},{9,8},{10,9... | collective-permute-start | bytes 958472 | tf_op jit(solution)/shard_map/ppermute | solution.py:1055
  48.7 19.0 %copy-start.22 = (bf16[208,768]{1,0:T(8,128)(2,1)}, bf16[208,768]{1,0:T(8,128)(2,1)S(1)}, u32[]{:S(2)}) copy-start(bf16[208,768]{1,0:T(8,128)(2,1)S(1)} %collective-permute-done.17) | copy-start | bytes 958468
  48.7 15.3 %collective-permute-start.11 = (bf16[96,3200]{1,0:T(8,128)(2,1)S(1)}, bf16[96,3200]{1,0:T(8,128)(2,1)S(1)}, u32[]{:S(2)}, u32[]{:S(2)}) collective-permute-start(bf16[96,3200]{1,0:T(8,128)(2,1)S(1)} %copy-done), channel_id=1, source_target_pairs={{0,4},{4,0},{8,12},{12,8},{16,20},{20,16},{24,28},{28,24},{1,5},{5... | collective-permute-start | bytes 1843208 | tf_op jit(solution)/shard_map/ppermute | solution.py:1051
  54.0 13.7 %copy-start.14 = (bf16[96,1536]{1,0:T(8,128)(2,1)}, bf16[96,1536]{1,0:T(8,128)(2,1)S(1)}, u32[]{:S(2)}) copy-start(bf16[96,1536]{1,0:T(8,128)(2,1)S(1)} %collective-permute-done.9.rest_3_) | copy-start | bytes 884740
  54.0 12.2 %collective-permute-start.12 = (bf16[96,3200]{1,0:T(8,128)(2,1)S(1)}, bf16[96,3200]{1,0:T(8,128)(2,1)S(1)}, u32[]{:S(2)}, u32[]{:S(2)}) collective-permute-start(bf16[96,3200]{1,0:T(8,128)(2,1)S(1)} %collective-permute-done.7.rest_1_), channel_id=1, source_target_pairs={{0,4},{4,0},{8,12},{12,8},{16,20},{20,16},{24,28},{28,24},{1,5},{5... | collective-permute-start | bytes 1843208 | tf_op jit(solution)/shard_map/ppermute | solution.py:1051
  54.0 13.9 %copy-start.12 = (bf16[96,1664]{1,0:T(8,128)(2,1)}, bf16[96,1664]{1,0:T(8,128)(2,1)S(1)}, u32[]{:S(2)}) copy-start(bf16[96,1664]{1,0:T(8,128)(2,1)S(1)} %collective-permute-done.10.rest_4_) | copy-start | bytes 958468
  54.0 12.5 %collective-permute-start.13 = (bf16[96,3200]{1,0:T(8,128)(2,1)S(1)}, bf16[96,3200]{1,0:T(8,128)(2,1)S(1)}, u32[]{:S(2)}, u32[]{:S(2)}) collective-permute-start(bf16[96,3200]{1,0:T(8,128)(2,1)S(1)} %collective-permute-done.8.rest_2_), channel_id=1, source_target_pairs={{0,4},{4,0},{8,12},{12,8},{16,20},{20,16},{24,28},{28,24},{1,5},{5... | collective-permute-start | bytes 1843208 | tf_op jit(solution)/shard_map/ppermute | solution.py:1051
  55.5 8.5 %collective-permute-start.14 = (bf16[96,1536]{1,0:T(8,128)(2,1)S(1)}, bf16[96,1536]{1,0:T(8,128)(2,1)S(1)}, u32[]{:S(2)}, u32[]{:S(2)}) collective-permute-start(bf16[96,1536]{1,0:T(8,128)(2,1)S(1)} %collective-permute-done.9.rest_3_), channel_id=1, source_target_pairs={{0,4},{4,0},{8,12},{12,8},{16,20},{20,16},{24,28},{28,24},{1,5},{5... | collective-permute-start | bytes 884744 | tf_op jit(solution)/shard_map/ppermute | solution.py:1051
  63.5 21.9 %collective-permute-start.20 = (bf16[2,3,96,768]{3,2,1,0:T(8,128)(2,1)}, bf16[2,3,96,768]{3,2,1,0:T(8,128)(2,1)}, u32[]{:S(2)}, u32[]{:S(2)}) collective-permute-start(bf16[2,3,96,768]{3,2,1,0:T(8,128)(2,1)} %bitcast.9.rest_10_.rest_5_), channel_id=1, source_target_pairs={{0,16},{4,20},{8,24},{12,28},{16,0},{20,4},{24,8},{28,12},{1,17},{... | collective-permute-start | bytes 2654216 | tf_op jit(solution)/shard_map/ppermute | solution.py:1051
  64.0 3.7 %collective-permute-start.15 = (bf16[96,1664]{1,0:T(8,128)(2,1)S(1)}, bf16[96,1664]{1,0:T(8,128)(2,1)S(1)}, u32[]{:S(2)}, u32[]{:S(2)}) collective-permute-start(bf16[96,1664]{1,0:T(8,128)(2,1)S(1)} %collective-permute-done.10.rest_4_), channel_id=1, source_target_pairs={{0,4},{4,0},{8,12},{12,8},{16,20},{20,16},{24,28},{28,24},{1,5},{5... | collective-permute-start | bytes 958472 | tf_op jit(solution)/shard_map/ppermute | solution.py:1051
  64.0 22.6 %collective-permute-start.19 = (bf16[2,3,96,768]{3,2,1,0:T(8,128)(2,1)}, bf16[2,3,96,768]{3,2,1,0:T(8,128)(2,1)}, u32[]{:S(2)}, u32[]{:S(2)}) collective-permute-start(bf16[2,3,96,768]{3,2,1,0:T(8,128)(2,1)} %bitcast.9.rest_10_.rest_5_), channel_id=1, source_target_pairs={{0,8},{4,12},{8,0},{12,4},{16,24},{20,28},{24,16},{28,20},{1,9},{5... | collective-permute-start | bytes 2654216 | tf_op jit(solution)/shard_map/ppermute | solution.py:1051
  66.2 19.1 %copy-start.42 = (bf16[1,96,768]{2,1,0:T(8,128)(2,1)S(1)}, bf16[1,96,768]{2,1,0:T(8,128)(2,1)}, u32[]{:S(2)}) copy-start(bf16[1,96,768]{2,1,0:T(8,128)(2,1)} %copy-done.41) | copy-start | bytes 442372
  66.3 21.8 %collective-permute-start.23 = (bf16[2,1,96,768]{3,2,1,0:T(8,128)(2,1)}, bf16[2,1,96,768]{3,2,1,0:T(8,128)(2,1)S(1)}, u32[]{:S(2)}, u32[]{:S(2)}) collective-permute-start(bf16[2,1,96,768]{3,2,1,0:T(8,128)(2,1)} %bitcast.6.rest_0_), channel_id=1, source_target_pairs={{0,4},{4,0},{8,12},{12,8},{16,20},{20,16},{24,28},{28,24},{1,5},{5... | collective-permute-start | bytes 884744 | tf_op jit(solution)/shard_map/ppermute | solution.py:1051
  67.3 23.3 %collective-permute-start.24 = (bf16[2,1,96,768]{3,2,1,0:T(8,128)(2,1)}, bf16[2,1,96,768]{3,2,1,0:T(8,128)(2,1)}, u32[]{:S(2)}, u32[]{:S(2)}) collective-permute-start(bf16[2,1,96,768]{3,2,1,0:T(8,128)(2,1)} %collective-permute-done.3.rest_1_), channel_id=1, source_target_pairs={{0,4},{4,0},{8,12},{12,8},{16,20},{20,16},{24,28},{28,24},{1,5},{5... | collective-permute-start | bytes 884744 | tf_op jit(solution)/shard_map/ppermute | solution.py:1051
  67.7 23.4 %collective-permute-start.25 = (bf16[2,1,96,768]{3,2,1,0:T(8,128)(2,1)}, bf16[2,1,96,768]{3,2,1,0:T(8,128)(2,1)}, u32[]{:S(2)}, u32[]{:S(2)}) collective-permute-start(bf16[2,1,96,768]{3,2,1,0:T(8,128)(2,1)} %collective-permute-done.5.rest_2_), channel_id=1, source_target_pairs={{0,4},{4,0},{8,12},{12,8},{16,20},{20,16},{24,28},{28,24},{1,5},{5... | collective-permute-start | bytes 884744 | tf_op jit(solution)/shard_map/ppermute | solution.py:1051
  85.4 4.2 %collective-permute-start.26 = (bf16[1,96,768]{2,1,0:T(8,128)(2,1)S(1)}, bf16[1,96,768]{2,1,0:T(8,128)(2,1)S(1)}, u32[]{:S(2)}, u32[]{:S(2)}) collective-permute-start(bf16[1,96,768]{2,1,0:T(8,128)(2,1)S(1)} %copy-done.42), channel_id=1, source_target_pairs={{0,4},{4,0},{8,12},{12,8},{16,20},{20,16},{24,28},{28,24},{1,5},{5... | collective-permute-start | bytes 442376 | tf_op jit(solution)/shard_map/ppermute | solution.py:1051
  86.6 3.9 %collective-permute-start.27 = (bf16[1,96,768]{2,1,0:T(8,128)(2,1)}, bf16[1,96,768]{2,1,0:T(8,128)(2,1)S(1)}, u32[]{:S(2)}, u32[]{:S(2)}) collective-permute-start(bf16[1,96,768]{2,1,0:T(8,128)(2,1)} %collective-permute-done.6.rest_4_), channel_id=1, source_target_pairs={{0,4},{4,0},{8,12},{12,8},{16,20},{20,16},{24,28},{28,24},{1,5},{5... | collective-permute-start | bytes 442376 | tf_op jit(solution)/shard_map/ppermute | solution.py:1051
  88.1 12.3 %collective-permute-start.22 = (bf16[3,96,768]{2,1,0:T(8,128)(2,1)S(1)}, bf16[3,96,768]{2,1,0:T(8,128)(2,1)S(1)}, u32[]{:S(2)}, u32[]{:S(2)}) collective-permute-start(bf16[3,96,768]{2,1,0:T(8,128)(2,1)S(1)} %slice_bitcast_fusion), channel_id=1, source_target_pairs={{0,8},{4,12},{8,0},{12,4},{16,24},{20,28},{24,16},{28,20},{1,9},{5... | collective-permute-start | bytes 1327112 | tf_op jit(solution)/shard_map/ppermute | solution.py:1051
  89.6 14.7 %copy-start.43 = (bf16[1,96,768]{2,1,0:T(8,128)(2,1)}, bf16[1,96,768]{2,1,0:T(8,128)(2,1)S(1)}, u32[]{:S(2)}) copy-start(bf16[1,96,768]{2,1,0:T(8,128)(2,1)S(1)} %collective-permute-done.26.rest_13_) | copy-start | bytes 442372
  89.6 11.8 %collective-permute-start.21 = (bf16[3,96,768]{2,1,0:T(8,128)(2,1)S(1)}, bf16[3,96,768]{2,1,0:T(8,128)(2,1)S(1)}, u32[]{:S(2)}, u32[]{:S(2)}) collective-permute-start(bf16[3,96,768]{2,1,0:T(8,128)(2,1)S(1)} %slice_bitcast_fusion.1), channel_id=1, source_target_pairs={{0,16},{4,20},{8,24},{12,28},{16,0},{20,4},{24,8},{28,12},{1,17},{... | collective-permute-start | bytes 1327112 | tf_op jit(solution)/shard_map/ppermute | solution.py:1051
  90.6 12.9 %collective-permute-start.28 = (bf16[2,3,96,768]{3,2,1,0:T(8,128)(2,1)}, bf16[2,3,96,768]{3,2,1,0:T(8,128)(2,1)S(1)}, u32[]{:S(2)}, u32[]{:S(2)}) collective-permute-start(bf16[2,3,96,768]{3,2,1,0:T(8,128)(2,1)} %bitcast.9.rest_10_.rest_5_), channel_id=1, source_target_pairs={{0,4},{4,0},{8,12},{12,8},{16,20},{20,16},{24,28},{28,24},{1,5},{5... | collective-permute-start | bytes 2654216 | tf_op jit(solution)/shard_map/ppermute | solution.py:1051
  90.6 12.9 %collective-permute-start.29 = (bf16[2,3,96,768]{3,2,1,0:T(8,128)(2,1)}, bf16[2,3,96,768]{3,2,1,0:T(8,128)(2,1)S(1)}, u32[]{:S(2)}, u32[]{:S(2)}) collective-permute-start(bf16[2,3,96,768]{3,2,1,0:T(8,128)(2,1)} %collective-permute-done.19.rest_6_), channel_id=1, source_target_pairs={{0,4},{4,0},{8,12},{12,8},{16,20},{20,16},{24,28},{28,24},{1,5},{5... | collective-permute-start | bytes 2654216 | tf_op jit(solution)/shard_map/ppermute | solution.py:1051
  91.1 12.4 %collective-permute-start.30 = (bf16[2,3,96,768]{3,2,1,0:T(8,128)(2,1)}, bf16[2,3,96,768]{3,2,1,0:T(8,128)(2,1)S(1)}, u32[]{:S(2)}, u32[]{:S(2)}) collective-permute-start(bf16[2,3,96,768]{3,2,1,0:T(8,128)(2,1)} %collective-permute-done.20.rest_7_), channel_id=1, source_target_pairs={{0,4},{4,0},{8,12},{12,8},{16,20},{20,16},{24,28},{28,24},{1,5},{5... | collective-permute-start | bytes 2654216 | tf_op jit(solution)/shard_map/ppermute | solution.py:1051
  100.4 3.1 %collective-permute-start.32 = (bf16[3,96,768]{2,1,0:T(8,128)(2,1)S(1)}, bf16[3,96,768]{2,1,0:T(8,128)(2,1)S(1)}, u32[]{:S(2)}, u32[]{:S(2)}) collective-permute-start(bf16[3,96,768]{2,1,0:T(8,128)(2,1)S(1)} %collective-permute-done.22.rest_9_), channel_id=1, source_target_pairs={{0,4},{4,0},{8,12},{12,8},{16,20},{20,16},{24,28},{28,24},{1,5},{5... | collective-permute-start | bytes 1327112 | tf_op jit(solution)/shard_map/ppermute | solution.py:1051
  101.4 2.1 collective-permute-start.31
  138.5 9.6 %collective-permute-start.34 = (bf16[2,2,400,768]{3,2,1,0:T(8,128)(2,1)}, bf16[2,2,400,768]{3,2,1,0:T(8,128)(2,1)}, u32[]{:S(2)}, u32[]{:S(2)}) collective-permute-start(bf16[2,2,400,768]{3,2,1,0:T(8,128)(2,1)} %get-tuple-element.78), channel_id=1, source_target_pairs={{0,4},{4,0},{8,12},{12,8},{16,20},{20,16},{24,28},{28,24},{1,5},{5... | collective-permute-start | bytes 7372808 | tf_op jit(solution)/shard_map/ppermute | solution.py:1051
  139.1 9.0 %collective-permute-start.33 = (bf16[2,2,384,768]{3,2,1,0:T(8,128)(2,1)}, bf16[2,2,384,768]{3,2,1,0:T(8,128)(2,1)}, u32[]{:S(2)}, u32[]{:S(2)}) collective-permute-start(bf16[2,2,384,768]{3,2,1,0:T(8,128)(2,1)} %get-tuple-element.75), channel_id=1, source_target_pairs={{0,4},{4,0},{8,12},{12,8},{16,20},{20,16},{24,28},{28,24},{1,5},{5... | collective-permute-start | bytes 7077896 | tf_op jit(solution)/shard_map/ppermute | solution.py:1051
  150.9 32.4 %collective-permute-start.36 = (bf16[2,400,768]{2,1,0:T(8,128)(2,1)}, bf16[2,400,768]{2,1,0:T(8,128)(2,1)}, u32[]{:S(2)}, u32[]{:S(2)}) collective-permute-start(bf16[2,400,768]{2,1,0:T(8,128)(2,1)} %fusion.__), channel_id=1, source_target_pairs={{0,16},{4,20},{8,24},{12,28},{16,0},{20,4},{24,8},{28,12},{1,17},{... | collective-permute-start | bytes 3686408 | tf_op jit(solution)/shard_map/ppermute | solution.py:1051
  155.0 28.4 %collective-permute-start.35 = (bf16[2,384,768]{2,1,0:T(8,128)(2,1)}, bf16[2,384,768]{2,1,0:T(8,128)(2,1)}, u32[]{:S(2)}, u32[]{:S(2)}) collective-permute-start(bf16[2,384,768]{2,1,0:T(8,128)(2,1)} %fusion.3._), channel_id=1, source_target_pairs={{0,8},{4,12},{8,0},{12,4},{16,24},{20,28},{24,16},{28,20},{1,9},{5... | collective-permute-start | bytes 3538952 | tf_op jit(solution)/shard_map/ppermute | solution.py:1051
  155.9 28.0 %copy-start.21 = (bf16[2,24,768]{2,1,0:T(8,128)(2,1)S(1)}, bf16[2,24,768]{2,1,0:T(8,128)(2,1)}, u32[]{:S(2)}) copy-start(bf16[2,24,768]{2,1,0:T(8,128)(2,1)} %qk.1) | copy-start | bytes 221188
  183.4 6.6 %collective-permute-start.37 = (bf16[2,2,96,1536]{3,2,1,0:T(8,128)(2,1)}, bf16[2,2,96,1536]{3,2,1,0:T(8,128)(2,1)}, u32[]{:S(2)}, u32[]{:S(2)}) collective-permute-start(bf16[2,2,96,1536]{3,2,1,0:T(8,128)(2,1)} %get-tuple-element.86), channel_id=1, source_target_pairs={{0,4},{4,0},{8,12},{12,8},{16,20},{20,16},{24,28},{28,24},{1,5},{5... | collective-permute-start | bytes 3538952 | tf_op jit(solution)/shard_map/ppermute | solution.py:1051
  183.4 9.2 %collective-permute-start.38 = (bf16[2,2,112,1536]{3,2,1,0:T(8,128)(2,1)}, bf16[2,2,112,1536]{3,2,1,0:T(8,128)(2,1)}, u32[]{:S(2)}, u32[]{:S(2)}) collective-permute-start(bf16[2,2,112,1536]{3,2,1,0:T(8,128)(2,1)} %get-tuple-element.90), channel_id=1, source_target_pairs={{0,4},{4,0},{8,12},{12,8},{16,20},{20,16},{24,28},{28,24},{1,5},{5... | collective-permute-start | bytes 4128776 | tf_op jit(solution)/shard_map/ppermute | solution.py:1051
  186.4 21.7 %collective-permute-start.40 = (bf16[384,768]{1,0:T(8,128)(2,1)}, bf16[384,768]{1,0:T(8,128)(2,1)}, u32[]{:S(2)}, u32[]{:S(2)}) collective-permute-start(bf16[384,768]{1,0:T(8,128)(2,1)} %fusion.5), channel_id=1, source_target_pairs={{0,16},{4,20},{8,24},{12,28},{16,0},{20,4},{24,8},{28,12},{1,17},{... | collective-permute-start | bytes 1769480 | tf_op jit(solution)/shard_map/ppermute | solution.py:1051
  189.3 17.1 %collective-permute-start.41 = (bf16[400,768]{1,0:T(8,128)(2,1)}, bf16[400,768]{1,0:T(8,128)(2,1)}, u32[]{:S(2)}, u32[]{:S(2)}) collective-permute-start(bf16[400,768]{1,0:T(8,128)(2,1)} %fusion.2), channel_id=1, source_target_pairs={{0,8},{4,12},{8,0},{12,4},{16,24},{20,28},{24,16},{28,20},{1,9},{5... | collective-permute-start | bytes 1843208 | tf_op jit(solution)/shard_map/ppermute | solution.py:1051
  191.2 26.5 %collective-permute-start.39 = (bf16[2,96,1536]{2,1,0:T(8,128)(2,1)S(1)}, bf16[2,96,1536]{2,1,0:T(8,128)(2,1)}, u32[]{:S(2)}, u32[]{:S(2)}) collective-permute-start(bf16[2,96,1536]{2,1,0:T(8,128)(2,1)S(1)} %fusion.12.rest_10_), channel_id=1, source_target_pairs={{0,8},{4,12},{8,0},{12,4},{16,24},{20,28},{24,16},{28,20},{1,9},{5... | collective-permute-start | bytes 1769480 | tf_op jit(solution)/shard_map/ppermute | solution.py:1051
  193.8 26.5 %collective-permute-start.43 = (bf16[2,112,1536]{2,1,0:T(8,128)(2,1)S(1)}, bf16[2,112,1536]{2,1,0:T(8,128)(2,1)}, u32[]{:S(2)}, u32[]{:S(2)}) collective-permute-start(bf16[2,112,1536]{2,1,0:T(8,128)(2,1)S(1)} %fusion.6.rest_11_), channel_id=1, source_target_pairs={{0,16},{4,20},{8,24},{12,28},{16,0},{20,4},{24,8},{28,12},{1,17},{... | collective-permute-start | bytes 2064392 | tf_op jit(solution)/shard_map/ppermute | solution.py:1051
  210.2 21.3 %collective-permute-start.48 = (bf16[193,768]{1,0:T(8,128)(2,1)S(1)}, bf16[193,768]{1,0:T(8,128)(2,1)S(1)}, u32[]{:S(2)}, u32[]{:S(2)}) collective-permute-start(bf16[193,768]{1,0:T(8,128)(2,1)S(1)} %pad_maximum_fusion.3), channel_id=1, source_target_pairs={{0,1},{1,2},{2,3},{3,0},{4,5},{5,6},{6,7},{7,4},{8,9},{9,10},{10,1... | collective-permute-start | bytes 889352 | tf_op jit(solution)/shard_map/ppermute | solution.py:1055
  210.8 21.3 %collective-permute-start.49 = (bf16[193,768]{1,0:T(8,128)(2,1)S(1)}, bf16[193,768]{1,0:T(8,128)(2,1)S(1)}, u32[]{:S(2)}, u32[]{:S(2)}) collective-permute-start(bf16[193,768]{1,0:T(8,128)(2,1)S(1)} %pad_maximum_fusion.4), channel_id=1, source_target_pairs={{0,2},{1,3},{2,0},{3,1},{4,6},{5,7},{6,4},{7,5},{8,10},{9,11},{10,... | collective-permute-start | bytes 889352 | tf_op jit(solution)/shard_map/ppermute | solution.py:1055
  214.1 18.0 %collective-permute-start.50 = (bf16[193,768]{1,0:T(8,128)(2,1)S(1)}, bf16[193,768]{1,0:T(8,128)(2,1)S(1)}, u32[]{:S(2)}, u32[]{:S(2)}) collective-permute-start(bf16[193,768]{1,0:T(8,128)(2,1)S(1)} %pad_maximum_fusion.5), channel_id=1, source_target_pairs={{0,3},{1,0},{2,1},{3,2},{4,7},{5,4},{6,5},{7,6},{8,11},{9,8},{10,9... | collective-permute-start | bytes 889352 | tf_op jit(solution)/shard_map/ppermute | solution.py:1055
  218.9 7.9 %collective-permute-start.42 = (bf16[96,1536]{1,0:T(8,128)(2,1)S(1)}, bf16[96,1536]{1,0:T(8,128)(2,1)S(1)}, u32[]{:S(2)}, u32[]{:S(2)}) collective-permute-start(bf16[96,1536]{1,0:T(8,128)(2,1)S(1)} %fusion.13), channel_id=1, source_target_pairs={{0,16},{4,20},{8,24},{12,28},{16,0},{20,4},{24,8},{28,12},{1,17},{... | collective-permute-start | bytes 884744 | tf_op jit(solution)/shard_map/ppermute | solution.py:1051
  221.6 8.6 %collective-permute-start.44 = (bf16[112,1536]{1,0:T(8,128)(2,1)S(1)}, bf16[112,1536]{1,0:T(8,128)(2,1)S(1)}, u32[]{:S(2)}, u32[]{:S(2)}) collective-permute-start(bf16[112,1536]{1,0:T(8,128)(2,1)S(1)} %fusion.7), channel_id=1, source_target_pairs={{0,8},{4,12},{8,0},{12,4},{16,24},{20,28},{24,16},{28,20},{1,9},{5... | collective-permute-start | bytes 1032200 | tf_op jit(solution)/shard_map/ppermute | solution.py:1051
  232.3 16.6 %collective-permute-start.45 = (bf16[25,3072]{1,0:T(8,128)(2,1)S(1)}, bf16[25,3072]{1,0:T(8,128)(2,1)S(1)}, u32[]{:S(2)}, u32[]{:S(2)}) collective-permute-start(bf16[25,3072]{1,0:T(8,128)(2,1)S(1)} %get-tuple-element.124), channel_id=1, source_target_pairs={{0,1},{1,2},{2,3},{3,0},{4,5},{5,6},{6,7},{7,4},{8,9},{9,10},{10,1... | collective-permute-start | bytes 460808 | tf_op jit(solution)/shard_map/ppermute | solution.py:1055
  243.6 11.5 %collective-permute-start.46 = (bf16[25,3072]{1,0:T(8,128)(2,1)S(1)}, bf16[25,3072]{1,0:T(8,128)(2,1)S(1)}, u32[]{:S(2)}, u32[]{:S(2)}) collective-permute-start(bf16[25,3072]{1,0:T(8,128)(2,1)S(1)} %get-tuple-element.125), channel_id=1, source_target_pairs={{0,2},{1,3},{2,0},{3,1},{4,6},{5,7},{6,4},{7,5},{8,10},{9,11},{10,... | collective-permute-start | bytes 460808 | tf_op jit(solution)/shard_map/ppermute | solution.py:1055
  243.6 12.8 %collective-permute-start.47 = (bf16[25,3072]{1,0:T(8,128)(2,1)S(1)}, bf16[25,3072]{1,0:T(8,128)(2,1)S(1)}, u32[]{:S(2)}, u32[]{:S(2)}) collective-permute-start(bf16[25,3072]{1,0:T(8,128)(2,1)S(1)} %get-tuple-element.126), channel_id=1, source_target_pairs={{0,3},{1,0},{2,1},{3,2},{4,7},{5,4},{6,5},{7,6},{8,11},{9,8},{10,9... | collective-permute-start | bytes 460808 | tf_op jit(solution)/shard_map/ppermute | solution.py:1055
  (32 other events, 138.3 us)

commit v5 on v2

--- a/solution.py
+++ b/solution.py
@@ -506,6 +506,800 @@
     return body
 
 
+CORE, ALONG_X, ALONG_Y = 1, 2, 4
+GAIN_LANES = 128
+NEAR = 12
+PAD = 16
+ANY = pl.BlockSpec(memory_space=pl.ANY)
+
+
+def smem(n):
+    return [pl.BlockSpec(memory_space=pltpu.SMEM)] * n
+
+
+def cost(flops, bytes_accessed):
+    return pl.CostEstimate(
+        flops=int(flops), bytes_accessed=int(bytes_accessed), transcendentals=0
+    )
+
+
+def ffn_copies(meta, pieces, half, start, target, sem):
+    rows = pieces[0].shape[2]
+    copies = []
+    for core in range(2):
+        mine = pieces[NEAR * core : NEAR * (core + 1)]
+        if start:
+            sources = (mine[5].at[half], mine[6 + half], mine[8 + half], mine[10 + half])
+        else:
+            sources = (*[ref.at[half] for ref in mine[:3]], mine[3 + half])
+        for flip, source in zip((0, ALONG_X, ALONG_Y, ALONG_X | ALONG_Y), sources):
+            top = pl.multiple_of((meta[0] ^ (flip | core)) * rows, rows)
+            size = source.shape[0]
+            copies.append(
+                pltpu.make_async_copy(source, target.at[start : start + size, pl.ds(top, rows)], sem)
+            )
+    for copy in copies:
+        copy.start()
+    return copies
+
+
+def wait_all(copies):
+    for copy in copies:
+        copy.wait()
+
+
+def place_of(meta, place):
+    flip = meta[0] ^ place
+    return flip & 1, (flip >> 1) & 1, (flip >> 2) & 1
+
+
+def lanes(values):
+    partial = values[:, 0:128]
+    for i in range(1, values.shape[1] // 128):
+        partial = partial + values[:, i * 128 : (i + 1) * 128]
+    return partial
+
+
+def weight_grads(meta, left, right_of, n, rows, both, keep, send, sem):
+    copies = []
+    for part in range(2):
+        for k in range(n // 2):
+            result = dot(left[...], right_of(part * (n // 2) + k)).astype(BF16)
+            for place in range(result.shape[0] // rows):
+                core, x, y = place_of(meta, place)
+                first, second = (y, x) if part else (x, y)
+                block = result[place * rows : (place + 1) * rows]
+                both[core, part, first, second, k * rows : (k + 1) * rows] = block
+        for core, target in ((1, send), (0, keep)):
+            copy = pltpu.make_async_copy(both.at[core, part], target.at[part], sem.at[core])
+            copy.start()
+            copies.append(copy)
+    return copies
+
+
+def feed_forward_near_kernel(meta, c, gain, h_hbm, cot_hbm, *rest):
+    pieces, rest = rest[: 2 * NEAR], rest[2 * NEAR :]
+    out, dc, gain_sums, keep1, send1, keep2, send2 = rest[:7]
+    (w1, w2, hid, act, slope, back, squeezed, grads, grad_gain) = rest[7:16]
+    (c_t, cot_t, both1, both2, h, cot, sem) = rest[16:]
+    total = c.shape[0]
+    blocks, _, cols = w1.shape
+    rows_of_block = pieces[0].shape[2]
+    units = blocks * cols
+    loads = [ffn_copies(meta, pieces, 0, start, w1, sem.at[start]) for start in range(2)]
+    late = [pltpu.make_async_copy(cot_hbm, cot, sem.at[2]), pltpu.make_async_copy(h_hbm, h, sem.at[7])]
+    for copy in late:
+        copy.start()
+    loads2 = [ffn_copies(meta, pieces, 1, start, w2, sem.at[3]) for start in range(2)]
+    wait_all(loads[0] + loads[1] + late + loads2[0] + loads2[1])
+    c_t[...] = jnp.transpose(c[...])
+    zero = jnp.zeros((total, 128), F32)
+
+    hid[0] = dot(c[...], w1[0])
+    sums = (zero, zero)
+    for b in range(blocks):
+        if b + 1 < blocks:
+            hid[(b + 1) % 2] = dot(c[...], w1[b + 1])
+        hidden = hid[b % 2]
+        half_erf = 0.5 + 0.5 * lax.erf(hidden * (0.5**0.5))
+        active = hidden * half_erf
+        act[b] = active
+        slope[b] = half_erf + hidden * (jnp.exp(-0.5 * hidden * hidden) * 0.3989422804014327)
+        sums = sums[0] + lanes(active), sums[1] + lanes(active * active)
+    cot_t[...] = jnp.transpose(cot[...])
+    back[0] = dot(cot[...], w2[0])
+    mean = jnp.sum(sums[0], axis=1, keepdims=True) * (1.0 / units)
+    spread = jnp.sum(sums[1], axis=1, keepdims=True) * (1.0 / units) - mean * mean
+    inverse = lax.rsqrt(spread + EPSILON)
+    shift = mean * inverse
+    sums = (zero, zero)
+    for b in range(blocks):
+        if b + 1 < blocks:
+            back[b + 1] = dot(cot[...], w2[b + 1])
+        centered = act[b] * inverse - shift
+        incoming = back[b]
+        grad_gain[b] = jnp.sum(incoming * centered, axis=0, keepdims=True)
+        weights = gain[b]
+        scaled = incoming * weights
+        act[b] = centered
+        back[b] = scaled
+        squeezed[b] = (centered * weights).astype(BF16)
+        sums = sums[0] + lanes(scaled), sums[1] + lanes(scaled * centered)
+    first_item = jnp.sum(sums[0], axis=1, keepdims=True) * (1.0 / units) * inverse
+    second_item = jnp.sum(sums[1], axis=1, keepdims=True) * (1.0 / units) * inverse
+    result = h[...]
+    for b in range(blocks):
+        result = result + dot_nt(squeezed[b], w2[b])
+        grad = (back[b] * inverse - first_item - act[b] * second_item) * slope[b]
+        grads[b] = grad.astype(BF16)
+    out[...] = result.astype(BF16)
+    copies = []
+    gain_sums[...] = jnp.concatenate(
+        [grad_gain[(blocks - k) % blocks] for k in range(blocks)] + [jnp.zeros((8 - blocks, cols), F32)],
+        axis=0,
+    )
+    for left, rights, both, keep, send, slots in (
+        (cot_t, squeezed, both2, keep2, send2, sem.at[3:5]),
+        (c_t, grads, both1, keep1, send1, sem.at[5:7]),
+    ):
+        copies += weight_grads(
+            meta,
+            left,
+            lambda k, rights=rights: rights[(blocks - k) % blocks],
+            blocks,
+            rows_of_block,
+            both,
+            keep,
+            send,
+            slots,
+        )
+    result = dot_nt(grads[0], w1[0])
+    for b in range(1, blocks):
+        result = result + dot_nt(grads[b], w1[b])
+    dc[...] = result
+    wait_all(copies)
+
+
+def feed_forward_near(meta, c, h, cot, gain, pieces):
+    total = c.shape[0]
+    blocks, _, cols = gain.shape
+    rows = pieces[0].shape[2]
+    shape = jax.ShapeDtypeStruct
+    size = (2, 2, 2, blocks // 2 * rows, cols)
+    one = pltpu.VMEM((blocks, total, cols), F32)
+    weights = pltpu.VMEM((blocks, D, cols), BF16)
+    narrow = pltpu.VMEM((blocks, total, cols), BF16)
+    return pl.pallas_call(
+        feed_forward_near_kernel,
+        out_shape=(
+            shape((total, D), BF16),
+            shape((total, D), F32),
+            shape((8, cols), F32),
+            shape(size, BF16),
+            shape(size, BF16),
+            shape(size, BF16),
+            shape(size, BF16),
+        ),
+        in_specs=smem(1) + vmem(2) + [ANY] * (2 + 2 * NEAR),
+        out_specs=tuple(vmem(3) + [ANY] * 4),
+        scratch_shapes=[
+            weights,
+            weights,
+            pltpu.VMEM((2, total, cols), F32),
+            one,
+            one,
+            one,
+            narrow,
+            narrow,
+            pltpu.VMEM((blocks, 1, cols), F32),
+            pltpu.VMEM((D, total), BF16),
+            pltpu.VMEM((D, total), BF16),
+            pltpu.VMEM((2, *size), BF16),
+            pltpu.VMEM((2, *size), BF16),
+            pltpu.VMEM((total, D), F32),
+            pltpu.VMEM((total, D), BF16),
+            pltpu.SemaphoreType.DMA((8,)),
+        ],
+        compiler_params=params(),
+        cost_estimate=cost(14.5e9, 20e6),
+        name="feed_forward",
+    )(meta, c, gain, h, cot, *pieces)
+
+
+QKV = 3 * D
+LANES = 4 * D + GAIN_LANES
+
+
+def attn_places():
+    cut = LANES // 2 // 128 * 128
+    diagonal = ALONG_X | ALONG_Y
+    near = [
+        (0, 0, LANES),
+        (ALONG_X, 0, LANES),
+        (ALONG_Y, 0, LANES),
+        (diagonal, 0, cut),
+        (diagonal, cut, LANES - cut),
+    ]
+    return near + [(flip | CORE, at, size) for flip, at, size in near]
+
+
+def attn_copies(meta, pieces, w, start, end, sem):
+    rows = pieces[0].shape[0]
+    copies = []
+    for (flip, at, size), ref in zip(attn_places(), pieces):
+        low, high = max(start, at), min(end, at + size)
+        if low >= high:
+            continue
+        top = pl.multiple_of((meta[0] ^ flip) * rows, rows)
+        target = w.at[pl.ds(top, rows), low - start : high - start]
+        copies.append(pltpu.make_async_copy(ref.at[:, low - at : high - at], target, sem))
+    for copy in copies:
+        copy.start()
+    return copies
+
+
+def sides(values, block):
+    rows = values[block * TILE : (block + 1) * TILE]
+    half = lane_half(TILE)
+    zero = jnp.zeros_like(rows)
+    return jnp.concatenate([jnp.where(half == 0, rows, zero), jnp.where(half == 1, rows, zero)], axis=0)
+
+
+def masks(bucket, bias):
+    across = jnp.where(bucket[0] == 0, NEGATIVE, 0.0).astype(F32)
+    own = causal_bias()
+    bias[0] = jnp.broadcast_to(across, (TILE, 2 * TILE))
+    bias[1] = jnp.concatenate([own, own], axis=1)
+
+
+def scores_of(keys, queries, bias, block):
+    scores = dot_nt(keys[: (block + 1) * TILE], queries)
+    added = [bias[0]] * block + [bias[1]]
+    return scores + (jnp.concatenate(added, axis=0) if block else added[0])
+
+
+def forward_pair(j, qkv, bias, out_t, lse, total):
+    scaled = qkv[j] * jnp.asarray(HEAD_DIM**-0.5, BF16)
+    keys = qkv[PAIRS + j]
+    values_t = jnp.transpose(qkv[2 * PAIRS + j])
+    blocks = total // TILE
+    for block in range(blocks):
+        scores = scores_of(keys, sides(scaled, block), bias, block)
+        peak = jnp.max(scores, axis=0, keepdims=True)
+        weights = jnp.exp(scores - peak)
+        totals = jnp.sum(weights, axis=0, keepdims=True)
+        rows_t = dot(values_t[:, : (block + 1) * TILE], weights.astype(BF16)) * (1.0 / totals)
+        cut = slice(block * TILE, (block + 1) * TILE)
+        out_t[j, :HEAD_DIM, cut] = rows_t[:HEAD_DIM, :TILE]
+        out_t[j, HEAD_DIM:, cut] = rows_t[HEAD_DIM:, TILE:]
+        lse[blocks * j + block] = peak + jnp.log(totals)
+
+
+def attn_forward_near_kernel(meta, bucket, x, *rest):
+    pieces, rest = rest[:10], rest[11:]
+    qkv, lse, o, h, c, gains, w, wo, wg, out_t, bias, sem = rest
+    total = x.shape[0]
+    loads = attn_copies(meta, pieces, wg, 4 * D, LANES, sem.at[0])
+    first = attn_copies(meta, pieces, w, 0, QKV, sem.at[1])
+    later = attn_copies(meta, pieces, wo, QKV, 4 * D, sem.at[2])
+    masks(bucket, bias)
+    rows = x[...].astype(F32)
+    centered, _ = apply_norm(rows)
+    wait_all(loads)
+    gains[...] = jnp.transpose(wg[...].astype(F32))[0:8]
+    normed = (centered * gains[0:1]).astype(BF16)
+    wait_all(first)
+    for part in range(3):
+        result = dot(normed, w[:, part * D : (part + 1) * D]).astype(BF16)
+        for j in range(PAIRS):
+            qkv[part * PAIRS + j] = result[:, j * PAIR : (j + 1) * PAIR]
+
+    for j in range(PAIRS):
+        forward_pair(j, qkv, bias, out_t, lse, total)
+    for j in range(PAIRS):
+        o[:, j * PAIR : (j + 1) * PAIR] = jnp.transpose(out_t[j])
+    centered, _ = apply_norm(o[...])
+    mixed = (centered * gains[1:2]).astype(BF16)
+    wait_all(later)
+    residual = x[...].astype(F32) + dot(mixed, wo[...])
+    h[...] = residual
+    centered, _ = apply_norm(residual)
+    c[...] = (centered * gains[2:3]).astype(BF16)
+
+
+def attn_forward_near(meta, bucket, x, pieces, earlier):
+    total = x.shape[0]
+    shape = jax.ShapeDtypeStruct
+    return pl.pallas_call(
+        attn_forward_near_kernel,
+        out_shape=(
+            shape((3 * PAIRS, total, PAIR), BF16),
+            shape((PAIRS * (total // TILE), 1, 2 * TILE), F32),
+            shape((total, D), F32),
+            shape((total, D), F32),
+            shape((total, D), BF16),
+            shape((8, D), F32),
+        ),
+        in_specs=smem(2) + vmem(1) + [ANY] * 11,
+        out_specs=tuple(vmem(6)),
+        scratch_shapes=[
+            pltpu.VMEM((D, QKV), BF16),
+            pltpu.VMEM((D, D), BF16),
+            pltpu.VMEM((D, GAIN_LANES), BF16),
+            pltpu.VMEM((PAIRS, PAIR, total), F32),
+            pltpu.VMEM((2, TILE, 2 * TILE), F32),
+            pltpu.SemaphoreType.DMA((3,)),
+        ],
+        compiler_params=params(),
+        cost_estimate=cost(4.2e9, 10e6),
+        name="attn_forward",
+    )(meta, bucket, x, *pieces, *earlier)
+
+
+def out_backward_near_kernel(meta, dc, cot, h, o, gains, *rest):
+    pieces, rest = rest[:10], rest[10:]
+    dh, do, dy, mixed, gain_rows, wo, sem = rest
+
+    @pl.when(pl.program_id(0) == 0)
+    def _():
+        gain_rows[...] = jnp.zeros(gain_rows.shape, F32)
+        wait_all(attn_copies(meta, pieces, wo, QKV, 4 * D, sem))
+
+    middle_gain, ff_gain = gains[1:2], gains[2:3]
+    incoming = dc[...]
+    centered, inverse = apply_norm(h[...])
+    gain_rows[0:1] += jnp.sum(incoming * centered, axis=0, keepdims=True)
+    residual = cot[...].astype(F32) + norm_backward(incoming, centered, inverse, ff_gain)
+    dh[...] = residual
+    branch = residual.astype(BF16)
+    dy[...] = branch
+    incoming = dot_nt(branch, wo[...])
+    centered, inverse = apply_norm(o[...])
+    mixed[...] = (centered * middle_gain).astype(BF16)
+    result = norm_backward(incoming, centered, inverse, middle_gain).astype(BF16)
+    for j in range(PAIRS):
+        do[j] = result[:, j * PAIR : (j + 1) * PAIR]
+
+
+def row_tiles(width=D):
+    return pl.BlockSpec((TILE, width), lambda i: (i, 0))
+
+
+def out_backward_near(meta, dc, cot, h, o, gains, pieces):
+    total = dc.shape[0]
+    shape = jax.ShapeDtypeStruct
+    whole = pl.BlockSpec((8, D), lambda i: (0, 0))
+    return pl.pallas_call(
+        out_backward_near_kernel,
+        grid=(total // TILE,),
+        out_shape=(
+            shape((total, D), F32),
+            shape((PAIRS, total, PAIR), BF16),
+            shape((total, D), BF16),
+            shape((total, D), BF16),
+            shape((8, D), F32),
+        ),
+        in_specs=smem(1) + [row_tiles()] * 4 + [whole] + [ANY] * 10,
+        out_specs=(
+            row_tiles(),
+            pl.BlockSpec((PAIRS, TILE, PAIR), lambda i: (0, i, 0)),
+            row_tiles(),
+            row_tiles(),
+            whole,
+        ),
+        scratch_shapes=[pltpu.VMEM((D, D), BF16), pltpu.SemaphoreType.DMA],
+        compiler_params=params(),
+        cost_estimate=cost(1.2e9, 10e6),
+        name="out_backward",
+    )(meta, dc, cot, h, o, gains, *pieces)
+
+
+def backward_pair(j, qkv, do, lse, bias, joined, total):
+    scale = HEAD_DIM**-0.5
+    scaled = qkv[j] * jnp.asarray(scale, BF16)
+    keys = qkv[PAIRS + j]
+    keys_t = jnp.transpose(keys)
+    values = qkv[2 * PAIRS + j]
+    grads = do[j]
+    blocks = total // TILE
+    grad_keys = [None] * blocks
+    grad_values = [None] * blocks
+
+    def add(sums, products, block):
+        for i in range(block + 1):
+            part = products[i * TILE : (i + 1) * TILE]
+            sums[i] = part if sums[i] is None else sums[i] + part
+
+    grad_q_t = []
+    for block in range(blocks):
+        count = (block + 1) * TILE
+        queries, outs = sides(scaled, block), sides(grads, block)
+        probs = jnp.exp(scores_of(keys, queries, bias, block) - lse[blocks * j + block])
+        grad_probs = dot_nt(values[:count], outs)
+        centre = jnp.sum(probs * grad_probs, axis=0, keepdims=True)
+        grad_scores = (probs * (grad_probs - centre)).astype(BF16)
+        turned = dot(keys_t[:, :count], grad_scores) * scale
+        grad_q_t.append(jnp.concatenate([turned[:HEAD_DIM, :TILE], turned[HEAD_DIM:, TILE:]], axis=0))
+        add(grad_keys, dot(grad_scores, queries), block)
+        add(grad_values, dot(probs.astype(BF16), outs), block)
+    joined[j] = jnp.transpose(jnp.concatenate(grad_q_t, axis=1)).astype(BF16)
+    joined[PAIRS + j] = jnp.concatenate(grad_keys, axis=0).astype(BF16)
+    joined[2 * PAIRS + j] = jnp.concatenate(grad_values, axis=0).astype(BF16)
+
+
+def attn_backward_near_kernel(
+    meta, bucket, x, qkv, do, lse, gains, dy, mixed, gain_rows, gain_sums, _, __,
+    joined, keep1, send1, keep2, send2, bias, normed_t, mixed_t, both1, both2, sem,
+):
+    total = x.shape[0]
+    rows = D // 8
+    masks(bucket, bias)
+    centered, _ = apply_norm(x[...].astype(F32))
+    normed_t[...] = jnp.transpose((centered * gains[0:1]).astype(BF16))
+    mixed_t[...] = jnp.transpose(mixed[...])
+
+    for j in range(PAIRS):
+        backward_pair(j, qkv, do, lse, bias, joined, total)
+
+    def place(result, both, swapped, at):
+        result = result.astype(BF16)
+        for place in range(8):
+            core, x, y = place_of(meta, place)
+            first, second = (y, x) if swapped else (x, y)
+            both[core, first, second, :rows, at : at + D] = result[place * rows : (place + 1) * rows]
+
+    def part(k):
+        return jnp.concatenate([joined[k * PAIRS + j] for j in range(PAIRS)], axis=1)
+
+    extra = jnp.concatenate([gain_rows[...], gain_sums[...]], axis=0).astype(BF16)
+    for core in range(2):
+        for a in range(2):
+            for b in range(2):
+                both2[core, a, b, rows:, :D] = extra
+                both2[core, a, b, rows:, D:] = jnp.zeros((PAD, D), BF16)
+    copies = []
+
+    def send_off(both, keep, send, slots):
+        for core, target in ((1, send), (0, keep)):
+            copy = pltpu.make_async_copy(both.at[core], target, slots.at[core])
+            copy.start()
+            copies.append(copy)
+
+    place(dot(normed_t[...], part(0)), both1, False, 0)
+    place(dot(normed_t[...], part(1)), both1, False, D)
+    send_off(both1, keep1, send1, sem.at[0:2])
+    place(dot(normed_t[...], part(2)), both2, True, 0)
+    place(dot(mixed_t[...], dy[...]), both2, True, D)
+    send_off(both2, keep2, send2, sem.at[2:4])
+    wait_all(copies)
+
+
+def attn_backward_near(
+    meta, bucket, x, qkv, do, lse, gains, dy, mixed, gain_rows, gain_sums, earlier
+):
+    total = x.shape[0]
+    rows = D // 8
+    shape = jax.ShapeDtypeStruct
+    less, more = (2, 2, rows, 2 * D), (2, 2, rows + PAD, 2 * D)
+    turned = pltpu.VMEM((D, total), BF16)
+    return pl.pallas_call(
+        attn_backward_near_kernel,
+        out_shape=(
+            shape((3 * PAIRS, total, PAIR), BF16),
+            shape(less, BF16),
+            shape(less, BF16),
+            shape(more, BF16),
+            shape(more, BF16),
+        ),
+        in_specs=smem(2) + vmem(9) + [ANY] * 2,
+        out_specs=tuple(vmem(1) + [ANY] * 4),
+        scratch_shapes=[
+            pltpu.VMEM((2, TILE, 2 * TILE), F32),
+            turned,
+            turned,
+            pltpu.VMEM((2, *less), BF16),
+            pltpu.VMEM((2, *more), BF16),
+            pltpu.SemaphoreType.DMA((4,)),
+        ],
+        compiler_params=params(),
+        cost_estimate=cost(9e9, 15e6),
+        name="attn_backward",
+    )(meta, bucket, x, qkv, do, lse, gains, dy, mixed, gain_rows, gain_sums, *earlier)
+
+
+def input_backward_near_kernel(meta, x, joined, dh, gains, *rest):
+    pieces, rest = rest[:10], rest[12:]
+    grad_x, w, sem = rest
+
+    @pl.when(pl.program_id(0) == 0)
+    def _():
+        wait_all(attn_copies(meta, pieces, w, 0, QKV, sem))
+
+    left = jnp.concatenate([joined[j] for j in range(3 * PAIRS)], axis=1)
+    incoming = dot_nt(left, w[...])
+    centered, inverse = apply_norm(x[...].astype(F32))
+    grad_x[...] = dh[...] + norm_backward(incoming, centered, inverse, gains[0:1])
+
+
+def input_backward_near(meta, x, joined, dh, gains, pieces, earlier):
+    total = x.shape[0]
+    return pl.pallas_call(
+        input_backward_near_kernel,
+        grid=(total // TILE,),
+        out_shape=jax.ShapeDtypeStruct((total, D), F32),
+        in_specs=smem(1)
+        + [
+            row_tiles(),
+            pl.BlockSpec((3 * PAIRS, TILE, PAIR), lambda i: (0, i, 0)),
+            row_tiles(),
+            pl.BlockSpec((8, D), lambda i: (0, 0)),
+        ]
+        + [ANY] * 12,
+        out_specs=row_tiles(),
+        scratch_shapes=[pltpu.VMEM((D, QKV), BF16), pltpu.SemaphoreType.DMA],
+        compiler_params=params(),
+        cost_estimate=cost(1.8e9, 10e6),
+        name="input_backward",
+    )(meta, x, joined, dh, gains, *pieces, *earlier)
+
+def pack_kernel(qk, value, out, attn_gain, inner_gain, ffn_gain, packed):
+    rows = value.shape[0]
+    packed[:, 0:D] = qk[0]
+    packed[:, D : 2 * D] = qk[1]
+    packed[:, 2 * D : 3 * D] = value[...]
+    packed[:, 3 * D : 4 * D] = out[...]
+    gains = [gain[...].astype(F32) for gain in (attn_gain, inner_gain, ffn_gain)]
+    gains = jnp.concatenate(gains + [jnp.zeros((GAIN_LANES - 3, rows), F32)], axis=0)
+    gains = jnp.concatenate([gains, jnp.zeros((GAIN_LANES, GAIN_LANES - rows), F32)], axis=1)
+    packed[:, 4 * D :] = jnp.transpose(gains)[:rows].astype(BF16)
+
+
+def pack(qk, value, out, gains):
+    rows = value.shape[0]
+    return pl.pallas_call(
+        pack_kernel,
+        out_shape=jax.ShapeDtypeStruct((rows, 4 * D + GAIN_LANES), BF16),
+        in_specs=vmem(6),
+        out_specs=vmem(1)[0],
+        compiler_params=params(),
+        cost_estimate=cost(0, 3e5),
+        name="pack",
+    )(qk, value, out, *[gain.reshape(1, rows) for gain in gains])
+
+
+def order_kernel(meta, *refs):
+    pieces, target = refs[:-1], refs[-1]
+    n = len(pieces)
+    values = [piece[...].astype(F32) for piece in pieces]
+    ordered = []
+    for place in range(n):
+        k = lax.rem(meta[1] + (n - place), n)
+        chosen = values[0]
+        for i in range(1, n):
+            chosen = jnp.where(k == i, values[i], chosen)
+        ordered.append(chosen)
+    target[...] = jnp.concatenate(ordered, axis=0).astype(BF16)
+
+
+def order(meta, pieces):
+    rows, lanes = pieces[0].shape
+    return pl.pallas_call(
+        order_kernel,
+        out_shape=jax.ShapeDtypeStruct((len(pieces) * rows, lanes), BF16),
+        in_specs=smem(1) + vmem(len(pieces)),
+        out_specs=vmem(1)[0],
+        compiler_params=params(),
+        cost_estimate=cost(0, 1e6),
+        name="order",
+    )(meta, *pieces)
+
+
+def collect_kernel(meta, gathered, others, first, second, gain):
+    n = gathered.shape[0]
+    rows = others.shape[2]
+    for k in range(n):
+        place = lax.rem(meta[1] + (n - k), n)
+        gain[k] = gathered[place, 2 * rows : 2 * rows + PAD].astype(F32)[0:1]
+        if k:
+            for half, target in ((0, first), (1, second)):
+                block = gathered[place, half * rows : (half + 1) * rows]
+                others[half, k - 1] = block
+                target[k - 1] = block
+
+
+def collect(meta, gathered, rows):
+    n, _, cols = gathered.shape
+    shape = jax.ShapeDtypeStruct
+    part = shape((n - 1, rows, cols), BF16)
+    return pl.pallas_call(
+        collect_kernel,
+        out_shape=(shape((2, n - 1, rows, cols), BF16), part, part, shape((n, 1, cols), F32)),
+        in_specs=smem(1) + vmem(1),
+        out_specs=tuple(vmem(4)),
+        compiler_params=params(),
+        cost_estimate=cost(0, 2e6),
+        name="collect",
+    )(meta, gathered)
+
+
+def swap(values, flip):
+    return lax.ppermute(values, "dp", [(i, i ^ flip) for i in range(8)])
+
+
+def turn(values, k, n):
+    return lax.ppermute(values, "mp", [(i, (i + k) % n) for i in range(n)])
+
+
+def wide(values):
+    return values.astype(F32)
+
+
+def after(values, *earlier):
+    return lax.optimization_barrier((values, *earlier))[0]
+
+
+def around(own):
+    from_x, from_y = swap(own, ALONG_X), swap(own, ALONG_Y)
+    return [own, from_x, from_y, swap(from_x[0], ALONG_Y), swap(from_y[1], ALONG_X)]
+
+
+def first_sum(keep, core):
+    return (wide(keep[1]) + wide(core[1])).astype(BF16)
+
+
+def second_sum(keep, core, near):
+    return (wide(keep[0, 1]) + wide(core[0, 1]) + wide(near[1])).astype(BF16)
+
+
+def third_sum(keep, core, near, far):
+    return wide(keep[0, 0]) + wide(core[0, 0]) + wide(near[0]) + wide(far)
+
+
+def fast_on_device(n_mp):
+    def body(
+        tokens,
+        bucket,
+        attn_gain,
+        qk_weight,
+        value_weight,
+        inner_gain,
+        out_weight,
+        ffn_gain,
+        fc1_weight,
+        ffn_inner_gain,
+        fc2_weight,
+        cotangent,
+    ):
+        at_dp, at_mp = lax.axis_index("dp"), lax.axis_index("mp")
+        meta = jnp.stack([at_dp, at_mp]).astype(jnp.int32)
+        slim = value_weight.shape[0]
+        slim_rows = slim * n_mp
+        rows, cols = fc1_weight.shape
+
+        shard = pack(qk_weight, value_weight, out_weight, (attn_gain, inner_gain, ffn_gain))
+        ring = [shard] + [turn(shard, k, n_mp) for k in range(1, n_mp)]
+
+        shard2 = jnp.concatenate(
+            [fc1_weight, fc2_weight.T, jnp.pad(ffn_inner_gain[None], ((0, PAD - 1), (0, 0)))],
+            axis=0,
+        )
+        near0 = around(shard2[: 2 * rows].reshape(2, 1, rows, cols))
+        own = after(order(meta, ring), near0[3], near0[4])
+        copies = jnp.broadcast_to(after(shard2, own)[None], (n_mp, *shard2.shape))
+        gathered = lax.all_to_all(copies, "mp", 0, 0, tiled=True)
+        from_x, from_y = swap(own, ALONG_X), swap(own, ALONG_Y)
+        cut = own.shape[1] // 2 // 128 * 128
+        near = [
+            own,
+            from_x,
+            from_y,
+            swap(from_x[:, :cut], ALONG_Y),
+            swap(from_y[:, cut:], ALONG_X),
+        ]
+        attn_pieces = near + [swap(piece, CORE) for piece in near]
+
+        others, first, second, hidden_gain = collect(
+            meta, after(gathered, near[3], near[4]), rows
+        )
+        first_x, second_x = swap(first, ALONG_X), swap(second, ALONG_X)
+        first_y, second_y = swap(first, ALONG_Y), swap(second, ALONG_Y)
+        qkv, lse, o, h, c, gains = attn_forward_near(
+            meta, bucket, tokens, attn_pieces, [others]
+        )
+        near = [others, first_x, second_x, first_y, second_y]
+        near += [swap(after(first_x, c), ALONG_Y), swap(after(second_y, c), ALONG_X)]
+        ffn_pieces = near0 + near + [swap(after(piece, c), CORE) for piece in near0 + near]
+
+        output, dc, gain_sums, keep1, send1, keep2, send2 = feed_forward_near(
+            meta, c, h, cotangent, hidden_gain, ffn_pieces
+        )
+        two = (0, 1)
+        core2, core1 = swap(send2, CORE), swap(send1, CORE)
+        axes = (ALONG_X, ALONG_Y)
+        first2 = [first_sum(keep2[i], core2[i]) for i in two]
+        near2 = [swap(first2[i], axes[i]) for i in two]
+        dh, do, dy, mixed, gain_rows = out_backward_near(
+            meta, dc, cotangent, h, o, gains, attn_pieces
+        )
+        core1 = after(core1, dy)
+        first1 = [first_sum(keep1[i], core1[i]) for i in two]
+        near1 = [swap(first1[i], axes[i]) for i in two]
+        joined, keep3, send3, keep4, send4 = attn_backward_near(
+            meta, bucket, tokens, qkv, do, lse, gains, dy, mixed, gain_rows, gain_sums, first1
+        )
+        near2, near1 = [after(near, send3) for near in near2], [after(near, send3) for near in near1]
+        second2 = [second_sum(keep2[i], core2[i], near2[i]) for i in two]
+        far2 = [swap(second2[i], axes[1 - i]) for i in two]
+        core3 = swap(after(send3, *near2, *near1), CORE)
+        core4 = swap(after(send4, *near2, *near1), CORE)
+        second1 = [second_sum(keep1[i], core1[i], near1[i]) for i in two]
+        far1 = [swap(second1[i], axes[1 - i]) for i in two]
+        core3, core4 = after(core3, *second1, *second2), after(core4, *second1, *second2)
+        first3, first4 = first_sum(keep3, core3), first_sum(keep4, core4)
+        near3, near4 = swap(first3, ALONG_X), swap(first4, ALONG_Y)
+
+        def finish(keep, core, near, far):
+            sums = [third_sum(keep[i], core[i], near[i], far[i]) for i in two]
+            pairs = n_mp // 2
+            blocks = [sums[k // pairs][k % pairs * rows : (k % pairs + 1) * rows] for k in range(n_mp)]
+            turned = [turn(blocks[k].astype(BF16), k, n_mp) for k in range(1, n_mp)]
+            return blocks[0], turned
+
+        far2 = [after(far, first3, first4) for far in far2]
+        mine2, turned2 = finish(keep2, core2, near2, far2)
+        mine1, turned1 = finish(keep1, core1, near1, far1)
+        token_gradient = input_backward_near(
+            meta, tokens, joined, dh, gains, attn_pieces, [mine2, mine1]
+        )
+        near3, near4 = after(near3, token_gradient), after(near4, token_gradient)
+        far3 = swap(second_sum(keep3, core3, near3), ALONG_Y)
+        far4 = swap(second_sum(keep4, core4, near4), ALONG_X)
+        sum1 = third_sum(keep3, core3, near3, far3)
+        sum2 = third_sum(keep4, core4, near4, far4)
+        both = jnp.concatenate([sum1, sum2[:slim_rows]], axis=1)
+
+        def block(k):
+            at = lax.rem(at_mp + k, n_mp) * slim
+            extra = jnp.concatenate(
+                [sum2[slim_rows, :D], sum2[slim_rows + 8 + k, :cols], jnp.zeros(3 * D - cols, F32)]
+            )
+            return jnp.concatenate([lax.dynamic_slice_in_dim(both, at, slim, 0), extra[None]], axis=0)
+
+        share = block(0)
+        turned = [turn(block(k).astype(BF16), k, n_mp) for k in range(1, n_mp)]
+
+        def total(mine, pieces):
+            for piece in pieces:
+                mine = mine + wide(after(piece, sum1, sum2))
+            return mine
+
+        grad_fc2, grad_fc1 = total(mine2, turned2), total(mine1, turned1)
+        for piece in turned:
+            share = share + wide(piece)
+        place = (at_dp * n_mp + at_mp) * slim
+        grad_ffn_gain = lax.dynamic_slice_in_dim(share[slim, :D], place, slim, 0)
+        grad_inner = share[slim, D : D + cols]
+        share = share[:slim]
+        own_qkv = jnp.concatenate([qk_weight[0], qk_weight[1], value_weight], axis=1)
+        grad_attn_gain = jnp.sum(share[:, : 3 * D] * wide(own_qkv), axis=1) / wide(attn_gain)
+        grad_inner_gain = jnp.sum(share[:, 3 * D :] * wide(out_weight), axis=1) / wide(inner_gain)
+        return (
+            output,
+            token_gradient,
+            grad_attn_gain,
+            jnp.stack([share[:, :D], share[:, D : 2 * D]]),
+            share[:, 2 * D : 3 * D],
+            grad_inner_gain,
+            share[:, 3 * D :],
+            grad_ffn_gain,
+            grad_fc1,
+            grad_inner,
+            grad_fc2.T,
+        )
+
+    return body
+
+
 def solution(mesh):
     flat = P(BOTH)
     rows = P(BOTH, None)
@@ -518,8 +1312,13 @@
         rows, rows, flat, pair, rows, flat, rows, flat,
         P("dp", "mp"), P("mp"), P("mp", "dp"),
     )
+    n_dp, n_mp = mesh.shape["dp"], mesh.shape["mp"]
+    if (n_dp, n_mp) == (8, 4):
+        body = fast_on_device(n_mp)
+    else:
+        body = on_device(n_dp, n_mp)
     return jax.shard_map(
-        on_device(mesh.shape["dp"], mesh.shape["mp"]),
+        body,
         mesh=mesh,
         in_specs=placed,
         out_specs=given,

time: 505 us -> 265 us (0.52)
  waiting for transfers between devices: 301 us -> 70.4 us
  starting transfers between devices: 0.16 us -> 54.1 us
  blocking collectives: 44.5 us -> 0 us
  local copies, waits for them, and re-layouts: 42.7 us -> 19.7 us
  between operations: 15.1 us -> 2.2 us
  other arithmetic: 19.2 us -> 27.1 us
    reduce_scatter x1 -> x0, waiting for transfers between devices: 138 us -> none  [body(): lax.psum_scatter(ffn_grads, BOTH, scatter_dimension=0).astype(F32)]
    all_gather x2 -> x0, waiting for transfers between devices: 109 us -> none  [the longest x1 60.3 us: body(): ffn_all = lax.all_gather(ffn_shard, BOTH, axis=0)]
    ppermute x0 -> x59, waiting for transfers between devices: none -> 64.6 us  [the longest x47 45.6 us: swap(): return lax.ppermute(values, 'dp', [(i, i ^ flip) for i in range(8)])]
    unnamed x5 -> x0, waiting for transfers between devices: 54.1 us -> none
    ppermute x0 -> x59, starting transfers between devices: none -> 47.9 us  [the longest x47 31.6 us: swap(): return lax.ppermute(values, 'dp', [(i, i ^ flip) for i in range(8)])]
    unnamed x1 -> x0, blocking collectives: 17.2 us -> none
    all_gather x1 -> x0, blocking collectives: 14.7 us -> none  [body(): inner_all = lax.all_gather(ffn_inner_gain, 'mp', axis=0, tiled=True)]
    psum x1 -> x0, blocking collectives: 12.6 us -> none  [body(): grad_inner = lax.psum(grad_inner, 'dp')]
  transfers between devices with their start and end apart: 4 -> 60, of which waited for: 4 -> 25; matrix products, arithmetic and copies ran while one was open for 6% -> 13% of each run, Pallas kernels for 3% -> 20%
where the time goes in v5:
time: 265 us; the launch traced here: 260 us
  Pallas kernels  86.6 us (33%)
  waiting for transfers between devices  70.4 us (27%)
  starting transfers between devices  54.1 us (20%)
  other arithmetic  27.1 us (10%)
  local copies, waits for them, and re-layouts  19.7 us (7%)
    ppermute x47, waiting for transfers between devices, swap(): return lax.ppermute(values, 'dp', [(i, i ^ flip) for i in range(8)])  45.6 us
    pallas_call x1, Pallas kernels, feed_forward_near(): pl.pallas_call(feed_forward_near_kernel, out_shape=(shape((total, D), BF1...  35.3 us
    ppermute x47, starting transfers between devices, swap(): return lax.ppermute(values, 'dp', [(i, i ^ flip) for i in range(8)])  31.6 us
    ppermute x12, waiting for transfers between devices, turn(): return lax.ppermute(values, 'mp', [(i, (i + k) % n) for i in range(n)])  18.9 us
    pallas_call x1, Pallas kernels, attn_backward_near(): pl.pallas_call(attn_backward_near_kernel, out_shape=(shape((3 * PAIRS, to...  17.2 us
    ppermute x12, starting transfers between devices, turn(): return lax.ppermute(values, 'mp', [(i, (i + k) % n) for i in range(n)])  16.2 us
    pallas_call x1, Pallas kernels, attn_forward_near(): pl.pallas_call(attn_forward_near_kernel, out_shape=(shape((3 * PAIRS, tot...  13.5 us
    pallas_call x1, Pallas kernels, input_backward_near(): pl.pallas_call(input_backward_near_kernel, grid=(total // TILE,), out_sha...  7.52 us
  transfers between devices with their start and end apart: 60, of which 25 were waited for; matrix products, arithmetic and copies ran while one was open for 13% of the time, Pallas kernels for 20%

profile of v5, /device:TPU:0, one launch (start us, length us, event | category | flops | bytes accessed | tf_op | source)
XLA Modules:
  0.0 260.0 jit_solution(18136258239656458226)
XLA Ops:
  0.7 1.1 pad_maximum_fusion
  1.7 3.0 %collective-permute-start.3 = (bf16[2,1,96,768]{3,2,1,0:T(8,128)(2,1)S(1)}, bf16[2,1,96,768]{3,2,1,0:T(8,128)(2,1)S(1)}, u32[]{:S(2)}, u32[]{:S(2)}) collective-permute-start(bf16[2,1,96,768]{3,2,1,0:T(8,128)(2,1)S(1)} %bitcast.116), channel_id=1, source_target_pairs={{0,8},{4,12},{8,0},{12,4},{16,24},{20,28},{24,16},{28,20},{1,9},{5... | collective-permute-start | bytes 884744 | tf_op jit(solution)/shard_map/ppermute | solution.py:1126
  4.8 1.5 collective-permute-start.5
  6.3 1.7 pack.1.refs_0_
  7.9 1.6 collective-permute-start
  9.5 2.6 collective-permute-start.1
  12.1 1.3 collective-permute-start.2
  15.8 1.2 collective-permute-done.refs_1_
  17.0 4.8 %collective-permute-done.1.refs_2_ = bf16[24,3200]{1,0:T(8,128)(2,1)S(1)} collective-permute-done((bf16[24,3200]{1,0:T(8,128)(2,1)}, bf16[24,3200]{1,0:T(8,128)(2,1)S(1)}, u32[]{:S(2)}, u32[]{:S(2)}) %collective-permute-start.1) | collective-permute-done | bytes 153632 | tf_op jit(solution)/shard_map/ppermute | solution.py:1130
  23.2 2.2 order.1.rest_0_
  25.4 1.1 broadcast_in_dim.25
  26.6 6.2 %all-to-all-start = ((bf16[4,208,768]{2,1,0:T(8,128)(2,1)}), bf16[4,208,768]{2,1,0:T(8,128)(2,1)S(1)}, u32[]{:S(2)}, u32[]{:S(2)}) async-start(bf16[4,208,768]{2,1,0:T(8,128)(2,1)} %broadcast_in_dim.25), calls=%async_computation | async-start | bytes 2555904 | tf_op jit(solution)/shard_map/all_to_all | solution.py:1189
  33.9 12.7 %collective-permute-done.8.rest_2_ = bf16[96,3200]{1,0:T(8,128)(2,1)S(1)} collective-permute-done((bf16[96,3200]{1,0:T(8,128)(2,1)S(1)}, bf16[96,3200]{1,0:T(8,128)(2,1)S(1)}, u32[]{:S(2)}, u32[]{:S(2)}) %collective-permute-start.8) | collective-permute-done | bytes 614432 | tf_op jit(solution)/shard_map/ppermute | solution.py:1126
  48.2 2.6 collective-permute-start.9
  51.3 4.3 %collective-permute-done.9.rest_3_ = bf16[96,1536]{1,0:T(8,128)(2,1)} collective-permute-done((bf16[96,1536]{1,0:T(8,128)(2,1)S(1)}, bf16[96,1536]{1,0:T(8,128)(2,1)}, u32[]{:S(2)}, u32[]{:S(2)}) %collective-permute-start.9) | collective-permute-done | bytes 294944 | tf_op jit(solution)/shard_map/ppermute | solution.py:1126
  56.1 5.8 %all-to-all-done.gathered = bf16[4,208,768]{2,1,0:T(8,128)(2,1)S(1)} async-done(((bf16[4,208,768]{2,1,0:T(8,128)(2,1)}), bf16[4,208,768]{2,1,0:T(8,128)(2,1)S(1)}, u32[]{:S(2)}, u32[]{:S(2)}) %all-to-all-start) | async-done | bytes 1277984 | tf_op jit(solution)/shard_map/all_to_all | solution.py:1189
  61.9 1.0 copy-done.3
  62.9 2.6 %collect.1 = (bf16[2,3,96,768]{3,2,1,0:T(8,128)(2,1)}, bf16[3,96,768]{2,1,0:T(8,128)(2,1)}, bf16[3,96,768]{2,1,0:T(8,128)(2,1)}, f32[4,1,768]{2,1,0:T(1,128)}) custom-call(s32[2]{0:T(128)} %pad_add_fusion.meta, bf16[4,208,768]{2,1,0:T(8,128)(2,1)} %copy-done.3), custom_call_target="tpu_custom_call" | custom-call | bytes 2000000 | tf_op jit(solution)/shard_map/collect/pallas_call | solution.py:1114
  67.3 1.6 collective-permute-start.18
  68.9 1.5 collective-permute-start.17
  71.2 13.5 %attn_forward.1 = (bf16[18,512,128]{2,1,0:T(8,128)(2,1)}, f32[12,1,512]{2,1,0:T(1,128)}, f32[512,768]{1,0:T(8,128)}, f32[512,768]{1,0:T(8,128)}, bf16[512,768]{1,0:T(8,128)(2,1)}, /*index=5*/f32[8,768]{1,0:T(8,128)}) custom-call(s32[2]{0:T(128)} %pad_add_fusion.meta, s32[1]{0:T(128)S(6)} %copy.23.bucket, bf16[512,768]{1,0:T(8,128)(2,1)} %x.7, ...), custom_call_target="tpu_custom_call" | custom-call | flops 4200000000 | bytes 10000000 | tf_op jit(solution)/shard_map/attn_forward/pallas_call | solution.py:813
  85.8 1.3 collective-permute-done.18.rest_8_
  90.0 6.1 %collective-permute-done.21.rest_11_ = bf16[3,96,768]{2,1,0:T(8,128)(2,1)S(1)} collective-permute-done((bf16[3,96,768]{2,1,0:T(8,128)(2,1)}, bf16[3,96,768]{2,1,0:T(8,128)(2,1)S(1)}, u32[]{:S(2)}, u32[]{:S(2)}) %collective-permute-start.21) | collective-permute-done | bytes 442400 | tf_op jit(solution)/shard_map/ppermute | solution.py:1126
  96.7 1.0 collective-permute-done.24.rest_14_
  102.2 35.3 %feed_forward.1 = (bf16[512,768]{1,0:T(8,128)(2,1)}, f32[512,768]{1,0:T(8,128)}, f32[8,768]{1,0:T(8,128)}, bf16[2,2,2,192,768]{4,3,2,1,0:T(8,128)(2,1)}, bf16[2,...) custom-call(s32[2]{0:T(128)} %pad_add_fusion.meta, ...), custom_call_target="tpu_custom_call" | custom-call | flops 14499999744 | bytes 20000000 | tf_op jit(solution)/shard_map/feed_forward/pallas_call | solution.py:672
  138.7 6.6 %out_backward.1 = (f32[512,768]{1,0:T(8,128)}, bf16[6,512,128]{2,1,0:T(8,128)(2,1)}, bf16[512,768]{1,0:T(8,128)(2,1)}, bf16[512,768]{1,0:T(8,128)(2,1)}, f32[8,768]{1,0:T(8,128)}) custom-call(s32[2]{0:T(128)} %pad_add_fusion.meta, f32[512,768]{1,0:T(8,128)} %get-tuple-element.95.dc, bf16[512,768]{1,0:T(8,128)(2,1)} %cot.1, ...), custom_call_target="tpu_custom_call" | custom-call | flops 1200000000 | bytes 10000000 | tf_op jit(solution)/shard_map/out_backward/pallas_call | solution.py:872
  145.3 4.3 %slice_bitcast_fusion.2 = (bf16[2,2,192,768]{3,2,1,0:T(8,128)(2,1)}, bf16[2,2,192,768]{3,2,1,0:T(8,128)(2,1)S(1)}, bf16[2,2,192,768]{3,2,1,0:T(8,128)(2,1)}, bf16[2,2,192,768]{3,2,1,0:T(8,128)(2,1)}) fusion(bf16[2,2,2,192,768]{4,3,2,1,0:T(8,128)(2,1)} %get-tuple-element.109, bf16[2,2,2,192,768]{4,3,2,1,0:T(8,128)(2,1)} %get-tuple-element.104), kind=kLoop, calls=%fused_computation.12 | loop fusion | bytes 9437184 | tf_op jit(solution)/shard_map/squeeze | solution.py:1219
  149.7 1.3 fusion.5
  151.6 1.5 collective-permute-start.40
  153.1 2.6 fusion.7
  156.2 1.5 collective-permute-start.36
  157.7 17.2 %attn_backward.1 = (bf16[18,512,128]{2,1,0:T(8,128)(2,1)}, bf16[2,2,96,1536]{3,2,1,0:T(8,128)(2,1)}, bf16[2,2,96,1536]{3,2,1,0:T(8,128)(2,1)}, bf16[2,2,112,1536...) custom-call(s32[2]{0:T(128)} %pad_add_fusion.meta, s32[1]{0:T(128)S(6)} %copy.23.bucket, bf16[512,768]{1,0:T(8,128)(2,1)} %x.7, ...), custom_call_target="tpu_custom_call" | custom-call | flops 8999999488 | bytes 15000000 | tf_op jit(solution)/shard_map/attn_backward/pallas_call | solution.py:985
  175.1 1.9 slice_bitcast_fusion
  177.1 1.4 fusion.18
  178.5 1.6 collective-permute-start.43
  180.7 1.2 fusion.19
  181.9 1.0 collective-permute-start.37
  182.9 1.1 fusion.17
  184.0 1.7 collective-permute-start.52
  185.7 1.1 fusion.16
  186.8 1.5 collective-permute-done.43
  189.1 1.1 fusion.15
  191.6 2.4 collective-permute-done.52
  194.0 1.1 fusion.12
  195.8 1.6 collective-permute-start.53
  198.4 2.4 collective-permute-start.54
  200.8 1.0 fusion
  201.8 1.7 collective-permute-start.44
  203.5 1.1 fusion.20
  205.0 1.1 fusion.10
  207.6 7.5 %input_backward.1 = f32[512,768]{1,0:T(8,128)} custom-call(s32[2]{0:T(128)} %pad_add_fusion.meta, bf16[512,768]{1,0:T(8,128)(2,1)} %x.7, bf16[18,512,128]{2,1,0:T(8,128)(2,1)} %get-tuple-element.107.joined, f32[512,768]{1,0:T(8,128)} %get-tuple-element.108.dh, f32[8,768]{1,0:T(8,128)} %get-tuple-element.97.gains, bf16[96,3200]{1,0:T(8,128)(2,1)} %order.1.rest_0_, ...), custom_call_target="tpu_custom_call" | custom-call | flops 1800000000 | bytes 10000000 | tf_op jit(solution)/shard_map/input_backward/pallas_call | solution.py:1026
  215.8 1.2 fusion.13
  217.1 3.4 %collective-permute-done.46 = bf16[2,112,1536]{2,1,0:T(8,128)(2,1)} collective-permute-done((bf16[2,112,1536]{2,1,0:T(8,128)(2,1)}, bf16[2,112,1536]{2,1,0:T(8,128)(2,1)}, u32[]{:S(2)}, u32[]{:S(2)}) %collective-permute-start.46) | collective-permute-done | bytes 688160 | tf_op jit(solution)/shard_map/ppermute | solution.py:1126
  220.8 1.1 fusion.1
  221.9 5.3 %collective-permute-done.45 = bf16[96,1536]{1,0:T(8,128)(2,1)S(1)} collective-permute-done((bf16[96,1536]{1,0:T(8,128)(2,1)S(1)}, bf16[96,1536]{1,0:T(8,128)(2,1)S(1)}, u32[]{:S(2)}, u32[]{:S(2)}) %collective-permute-start.45) | collective-permute-done | bytes 294944 | tf_op jit(solution)/shard_map/ppermute | solution.py:1126
  227.6 1.3 fusion.14
  228.9 1.9 collective-permute-start.57
  230.8 3.7 %collective-permute-done.47 = bf16[112,1536]{1,0:T(8,128)(2,1)S(1)} collective-permute-done((bf16[112,1536]{1,0:T(8,128)(2,1)S(1)}, bf16[112,1536]{1,0:T(8,128)(2,1)S(1)}, u32[]{:S(2)}, u32[]{:S(2)}) %collective-permute-start.47) | collective-permute-done | bytes 344096 | tf_op jit(solution)/shard_map/ppermute | solution.py:1126
  234.5 1.1 fusion.33
  236.5 7.3 %collective-permute-done.58 = bf16[96,768]{1,0:T(8,128)(2,1)S(1)} collective-permute-done((bf16[96,768]{1,0:T(8,128)(2,1)S(1)}, bf16[96,768]{1,0:T(8,128)(2,1)S(1)}, u32[]{:S(2)}, u32[]{:S(2)}) %collective-permute-start.58) | collective-permute-done | bytes 147488 | tf_op jit(solution)/shard_map/ppermute | solution.py:1130
  244.1 1.7 collective-permute-start.48
  245.9 2.4 collective-permute-start.50
  249.2 1.8 convert_add_fusion.12
  251.8 4.0 %collective-permute-done.49 = bf16[25,3072]{1,0:T(8,128)(2,1)S(1)} collective-permute-done((bf16[25,3072]{1,0:T(8,128)(2,1)S(1)}, bf16[25,3072]{1,0:T(8,128)(2,1)S(1)}, u32[]{:S(2)}, u32[]{:S(2)}) %collective-permute-start.49) | collective-permute-done | bytes 153632 | tf_op jit(solution)/shard_map/ppermute | solution.py:1130
  (237 shorter events, 35.1 us)
Async XLA Ops:
  1.7 23.7 %copy-start.17 = (bf16[192,768]{1,0:T(8,128)(2,1)}, bf16[192,768]{1,0:T(8,128)(2,1)S(1)}, u32[]{:S(2)}) copy-start(bf16[192,768]{1,0:T(8,128)(2,1)S(1)} %pad_maximum_fusion) | copy-start | bytes 884740
  1.7 11.7 %collective-permute-start.3 = (bf16[2,1,96,768]{3,2,1,0:T(8,128)(2,1)S(1)}, bf16[2,1,96,768]{3,2,1,0:T(8,128)(2,1)S(1)}, u32[]{:S(2)}, u32[]{:S(2)}) collective-permute-start(bf16[2,1,96,768]{3,2,1,0:T(8,128)(2,1)S(1)} %bitcast.116), channel_id=1, source_target_pairs={{0,8},{4,12},{8,0},{12,4},{16,24},{20,28},{24,16},{28,20},{1,9},{5... | collective-permute-start | bytes 884744 | tf_op jit(solution)/shard_map/ppermute | solution.py:1126
  4.8 9.4 %collective-permute-start.5 = (bf16[2,1,96,768]{3,2,1,0:T(8,128)(2,1)S(1)}, bf16[2,1,96,768]{3,2,1,0:T(8,128)(2,1)S(1)}, u32[]{:S(2)}, u32[]{:S(2)}) collective-permute-start(bf16[2,1,96,768]{3,2,1,0:T(8,128)(2,1)S(1)} %bitcast.117), channel_id=1, source_target_pairs={{0,16},{4,20},{8,24},{12,28},{16,0},{20,4},{24,8},{28,12},{1,17},{... | collective-permute-start | bytes 884744 | tf_op jit(solution)/shard_map/ppermute | solution.py:1126
  7.9 9.1 %collective-permute-start = (bf16[24,3200]{1,0:T(8,128)(2,1)}, bf16[24,3200]{1,0:T(8,128)(2,1)S(1)}, u32[]{:S(2)}, u32[]{:S(2)}) collective-permute-start(bf16[24,3200]{1,0:T(8,128)(2,1)} %pack.1.refs_0_), channel_id=1, source_target_pairs={{0,1},{1,2},{2,3},{3,0},{4,5},{5,6},{6,7},{7,4},{8,9},{9,10},{10,1... | collective-permute-start | bytes 460808 | tf_op jit(solution)/shard_map/ppermute | solution.py:1130
  9.5 12.3 %collective-permute-start.1 = (bf16[24,3200]{1,0:T(8,128)(2,1)}, bf16[24,3200]{1,0:T(8,128)(2,1)S(1)}, u32[]{:S(2)}, u32[]{:S(2)}) collective-permute-start(bf16[24,3200]{1,0:T(8,128)(2,1)} %pack.1.refs_0_), channel_id=1, source_target_pairs={{0,2},{1,3},{2,0},{3,1},{4,6},{5,7},{6,4},{7,5},{8,10},{9,11},{10,... | collective-permute-start | bytes 460808 | tf_op jit(solution)/shard_map/ppermute | solution.py:1130
  12.1 9.7 %collective-permute-start.2 = (bf16[24,3200]{1,0:T(8,128)(2,1)}, bf16[24,3200]{1,0:T(8,128)(2,1)S(1)}, u32[]{:S(2)}, u32[]{:S(2)}) collective-permute-start(bf16[24,3200]{1,0:T(8,128)(2,1)} %pack.1.refs_0_), channel_id=1, source_target_pairs={{0,3},{1,0},{2,1},{3,2},{4,7},{5,4},{6,5},{7,6},{8,11},{9,8},{10,9... | collective-permute-start | bytes 460808 | tf_op jit(solution)/shard_map/ppermute | solution.py:1130
  13.5 11.9 %collective-permute-start.4 = (bf16[1,96,768]{2,1,0:T(8,128)(2,1)S(1)}, bf16[1,96,768]{2,1,0:T(8,128)(2,1)S(1)}, u32[]{:S(2)}, u32[]{:S(2)}) collective-permute-start(bf16[1,96,768]{2,1,0:T(8,128)(2,1)S(1)} %slice_bitcast_fusion.9), channel_id=1, source_target_pairs={{0,16},{4,20},{8,24},{12,28},{16,0},{20,4},{24,8},{28,12},{1,17},{... | collective-permute-start | bytes 442376 | tf_op jit(solution)/shard_map/ppermute | solution.py:1126
  14.2 11.2 %collective-permute-start.6 = (bf16[1,96,768]{2,1,0:T(8,128)(2,1)S(1)}, bf16[1,96,768]{2,1,0:T(8,128)(2,1)S(1)}, u32[]{:S(2)}, u32[]{:S(2)}) collective-permute-start(bf16[1,96,768]{2,1,0:T(8,128)(2,1)S(1)} %slice_bitcast_fusion.8), channel_id=1, source_target_pairs={{0,8},{4,12},{8,0},{12,4},{16,24},{20,28},{24,16},{28,20},{1,9},{5... | collective-permute-start | bytes 442376 | tf_op jit(solution)/shard_map/ppermute | solution.py:1126
  26.6 35.3 %all-to-all-start = ((bf16[4,208,768]{2,1,0:T(8,128)(2,1)}), bf16[4,208,768]{2,1,0:T(8,128)(2,1)S(1)}, u32[]{:S(2)}, u32[]{:S(2)}) async-start(bf16[4,208,768]{2,1,0:T(8,128)(2,1)} %broadcast_in_dim.25), calls=%async_computation | async-start | bytes 2555904 | tf_op jit(solution)/shard_map/all_to_all | solution.py:1189
  32.8 13.8 %collective-permute-start.8 = (bf16[96,3200]{1,0:T(8,128)(2,1)S(1)}, bf16[96,3200]{1,0:T(8,128)(2,1)S(1)}, u32[]{:S(2)}, u32[]{:S(2)}) collective-permute-start(bf16[96,3200]{1,0:T(8,128)(2,1)S(1)} %copy-done), channel_id=1, source_target_pairs={{0,16},{4,20},{8,24},{12,28},{16,0},{20,4},{24,8},{28,12},{1,17},{... | collective-permute-start | bytes 1843208 | tf_op jit(solution)/shard_map/ppermute | solution.py:1126
  33.3 13.9 %collective-permute-start.7 = (bf16[96,3200]{1,0:T(8,128)(2,1)S(1)}, bf16[96,3200]{1,0:T(8,128)(2,1)}, u32[]{:S(2)}, u32[]{:S(2)}) collective-permute-start(bf16[96,3200]{1,0:T(8,128)(2,1)S(1)} %copy-done), channel_id=1, source_target_pairs={{0,8},{4,12},{8,0},{12,4},{16,24},{20,28},{24,16},{28,20},{1,9},{5... | collective-permute-start | bytes 1843208 | tf_op jit(solution)/shard_map/ppermute | solution.py:1126
  33.9 31.7 %collective-permute-start.11 = (bf16[96,3200]{1,0:T(8,128)(2,1)S(1)}, bf16[96,3200]{1,0:T(8,128)(2,1)}, u32[]{:S(2)}, u32[]{:S(2)}) collective-permute-start(bf16[96,3200]{1,0:T(8,128)(2,1)S(1)} %copy-done), channel_id=1, source_target_pairs={{0,4},{4,0},{8,12},{12,8},{16,20},{20,16},{24,28},{28,24},{1,5},{5... | collective-permute-start | bytes 1843208 | tf_op jit(solution)/shard_map/ppermute | solution.py:1126
  46.6 9.0 %collective-permute-start.10 = (bf16[96,1664]{1,0:T(8,128)(2,1)S(1)}, bf16[96,1664]{1,0:T(8,128)(2,1)S(1)}, u32[]{:S(2)}, u32[]{:S(2)}) collective-permute-start(bf16[96,1664]{1,0:T(8,128)(2,1)S(1)} %slice.388), channel_id=1, source_target_pairs={{0,8},{4,12},{8,0},{12,4},{16,24},{20,28},{24,16},{28,20},{1,9},{5... | collective-permute-start | bytes 958472 | tf_op jit(solution)/shard_map/ppermute | solution.py:1126
  48.2 7.4 %collective-permute-start.9 = (bf16[96,1536]{1,0:T(8,128)(2,1)S(1)}, bf16[96,1536]{1,0:T(8,128)(2,1)}, u32[]{:S(2)}, u32[]{:S(2)}) collective-permute-start(bf16[96,1536]{1,0:T(8,128)(2,1)S(1)} %slice.387), channel_id=1, source_target_pairs={{0,16},{4,20},{8,24},{12,28},{16,0},{20,4},{24,8},{28,12},{1,17},{... | collective-permute-start | bytes 884744 | tf_op jit(solution)/shard_map/ppermute | solution.py:1126
  50.8 16.6 %collective-permute-start.12 = (bf16[96,3200]{1,0:T(8,128)(2,1)}, bf16[96,3200]{1,0:T(8,128)(2,1)}, u32[]{:S(2)}, u32[]{:S(2)}) collective-permute-start(bf16[96,3200]{1,0:T(8,128)(2,1)} %collective-permute-done.7.rest_1_), channel_id=1, source_target_pairs={{0,4},{4,0},{8,12},{12,8},{16,20},{20,16},{24,28},{28,24},{1,5},{5... | collective-permute-start | bytes 1843208 | tf_op jit(solution)/shard_map/ppermute | solution.py:1126
  50.8 18.2 %collective-permute-start.13 = (bf16[96,3200]{1,0:T(8,128)(2,1)S(1)}, bf16[96,3200]{1,0:T(8,128)(2,1)}, u32[]{:S(2)}, u32[]{:S(2)}) collective-permute-start(bf16[96,3200]{1,0:T(8,128)(2,1)S(1)} %collective-permute-done.8.rest_2_), channel_id=1, source_target_pairs={{0,4},{4,0},{8,12},{12,8},{16,20},{20,16},{24,28},{28,24},{1,5},{5... | collective-permute-start | bytes 1843208 | tf_op jit(solution)/shard_map/ppermute | solution.py:1126
  55.6 10.6 %collective-permute-start.14 = (bf16[96,1536]{1,0:T(8,128)(2,1)}, bf16[96,1536]{1,0:T(8,128)(2,1)}, u32[]{:S(2)}, u32[]{:S(2)}) collective-permute-start(bf16[96,1536]{1,0:T(8,128)(2,1)} %collective-permute-done.9.rest_3_), channel_id=1, source_target_pairs={{0,4},{4,0},{8,12},{12,8},{16,20},{20,16},{24,28},{28,24},{1,5},{5... | collective-permute-start | bytes 884744 | tf_op jit(solution)/shard_map/ppermute | solution.py:1126
  55.6 14.8 %collective-permute-start.15 = (bf16[96,1664]{1,0:T(8,128)(2,1)S(1)}, bf16[96,1664]{1,0:T(8,128)(2,1)S(1)}, u32[]{:S(2)}, u32[]{:S(2)}) collective-permute-start(bf16[96,1664]{1,0:T(8,128)(2,1)S(1)} %collective-permute-done.10.rest_4_), channel_id=1, source_target_pairs={{0,4},{4,0},{8,12},{12,8},{16,20},{20,16},{24,28},{28,24},{1,5},{5... | collective-permute-start | bytes 958472 | tf_op jit(solution)/shard_map/ppermute | solution.py:1126
  65.6 19.1 %collective-permute-start.19 = (bf16[3,96,768]{2,1,0:T(8,128)(2,1)}, bf16[3,96,768]{2,1,0:T(8,128)(2,1)}, u32[]{:S(2)}, u32[]{:S(2)}) collective-permute-start(bf16[3,96,768]{2,1,0:T(8,128)(2,1)} %get-tuple-element.80), channel_id=1, source_target_pairs={{0,16},{4,20},{8,24},{12,28},{16,0},{20,4},{24,8},{28,12},{1,17},{... | collective-permute-start | bytes 1327112 | tf_op jit(solution)/shard_map/ppermute | solution.py:1126
  66.1 19.1 %collective-permute-start.16 = (bf16[3,96,768]{2,1,0:T(8,128)(2,1)}, bf16[3,96,768]{2,1,0:T(8,128)(2,1)}, u32[]{:S(2)}, u32[]{:S(2)}) collective-permute-start(bf16[3,96,768]{2,1,0:T(8,128)(2,1)} %get-tuple-element.79), channel_id=1, source_target_pairs={{0,8},{4,12},{8,0},{12,4},{16,24},{20,28},{24,16},{28,20},{1,9},{5... | collective-permute-start | bytes 1327112 | tf_op jit(solution)/shard_map/ppermute | solution.py:1126
  67.3 19.7 %collective-permute-start.18 = (bf16[3,96,768]{2,1,0:T(8,128)(2,1)}, bf16[3,96,768]{2,1,0:T(8,128)(2,1)S(1)}, u32[]{:S(2)}, u32[]{:S(2)}) collective-permute-start(bf16[3,96,768]{2,1,0:T(8,128)(2,1)} %get-tuple-element.79), channel_id=1, source_target_pairs={{0,16},{4,20},{8,24},{12,28},{16,0},{20,4},{24,8},{28,12},{1,17},{... | collective-permute-start | bytes 1327112 | tf_op jit(solution)/shard_map/ppermute | solution.py:1126
  68.9 18.9 %collective-permute-start.17 = (bf16[3,96,768]{2,1,0:T(8,128)(2,1)}, bf16[3,96,768]{2,1,0:T(8,128)(2,1)S(1)}, u32[]{:S(2)}, u32[]{:S(2)}) collective-permute-start(bf16[3,96,768]{2,1,0:T(8,128)(2,1)} %get-tuple-element.80), channel_id=1, source_target_pairs={{0,8},{4,12},{8,0},{12,4},{16,24},{20,28},{24,16},{28,20},{1,9},{5... | collective-permute-start | bytes 1327112 | tf_op jit(solution)/shard_map/ppermute | solution.py:1126
  71.2 25.0 %copy-start.32 = (bf16[2,1,96,768]{3,2,1,0:T(8,128)(2,1)S(1)}, bf16[2,1,96,768]{3,2,1,0:T(8,128)(2,1)}, u32[]{:S(2)}) copy-start(bf16[2,1,96,768]{3,2,1,0:T(8,128)(2,1)} %copy-done.31) | copy-start | bytes 884740
  71.2 25.0 %copy-start.18 = (bf16[192,768]{1,0:T(8,128)(2,1)S(1)}, bf16[192,768]{1,0:T(8,128)(2,1)}, u32[]{:S(2)}) copy-start(bf16[192,768]{1,0:T(8,128)(2,1)} %copy-done.17) | copy-start | bytes 884740
  84.7 11.5 %collective-permute-start.21 = (bf16[3,96,768]{2,1,0:T(8,128)(2,1)}, bf16[3,96,768]{2,1,0:T(8,128)(2,1)S(1)}, u32[]{:S(2)}, u32[]{:S(2)}) collective-permute-start(bf16[3,96,768]{2,1,0:T(8,128)(2,1)} %collective-permute-done.19.rest_9_), channel_id=1, source_target_pairs={{0,8},{4,12},{8,0},{12,4},{16,24},{20,28},{24,16},{28,20},{1,9},{5... | collective-permute-start | bytes 1327112 | tf_op jit(solution)/shard_map/ppermute | solution.py:1126
  85.3 10.9 %collective-permute-start.20 = (bf16[3,96,768]{2,1,0:T(8,128)(2,1)}, bf16[3,96,768]{2,1,0:T(8,128)(2,1)S(1)}, u32[]{:S(2)}, u32[]{:S(2)}) collective-permute-start(bf16[3,96,768]{2,1,0:T(8,128)(2,1)} %collective-permute-done.16.rest_6_), channel_id=1, source_target_pairs={{0,16},{4,20},{8,24},{12,28},{16,0},{20,4},{24,8},{28,12},{1,17},{... | collective-permute-start | bytes 1327112 | tf_op jit(solution)/shard_map/ppermute | solution.py:1126
  85.8 3.9 %collective-permute-start.23 = (bf16[2,1,96,768]{3,2,1,0:T(8,128)(2,1)S(1)}, bf16[2,1,96,768]{3,2,1,0:T(8,128)(2,1)S(1)}, u32[]{:S(2)}, u32[]{:S(2)}) collective-permute-start(bf16[2,1,96,768]{3,2,1,0:T(8,128)(2,1)S(1)} %copy-done.30), channel_id=1, source_target_pairs={{0,4},{4,0},{8,12},{12,8},{16,20},{20,16},{24,28},{28,24},{1,5},{5... | collective-permute-start | bytes 884744 | tf_op jit(solution)/shard_map/ppermute | solution.py:1126
  87.1 1.6 collective-permute-start.25
  87.8 1.7 collective-permute-start.26
  88.7 10.8 %collective-permute-start.27 = (bf16[2,3,96,768]{3,2,1,0:T(8,128)(2,1)S(1)}, bf16[2,3,96,768]{3,2,1,0:T(8,128)(2,1)S(1)}, u32[]{:S(2)}, u32[]{:S(2)}) collective-permute-start(bf16[2,3,96,768]{3,2,1,0:T(8,128)(2,1)S(1)} %copy-done.38), channel_id=1, source_target_pairs={{0,4},{4,0},{8,12},{12,8},{16,20},{20,16},{24,28},{28,24},{1,5},{5... | collective-permute-start | bytes 2654216 | tf_op jit(solution)/shard_map/ppermute | solution.py:1126
  89.5 9.4 %collective-permute-start.30 = (bf16[3,96,768]{2,1,0:T(8,128)(2,1)}, bf16[3,96,768]{2,1,0:T(8,128)(2,1)S(1)}, u32[]{:S(2)}, u32[]{:S(2)}) collective-permute-start(bf16[3,96,768]{2,1,0:T(8,128)(2,1)} %copy-done.40), channel_id=1, source_target_pairs={{0,4},{4,0},{8,12},{12,8},{16,20},{20,16},{24,28},{28,24},{1,5},{5... | collective-permute-start | bytes 1327112 | tf_op jit(solution)/shard_map/ppermute | solution.py:1126
  89.7 9.4 %collective-permute-start.29 = (bf16[3,96,768]{2,1,0:T(8,128)(2,1)}, bf16[3,96,768]{2,1,0:T(8,128)(2,1)S(1)}, u32[]{:S(2)}, u32[]{:S(2)}) collective-permute-start(bf16[3,96,768]{2,1,0:T(8,128)(2,1)} %copy-done.41), channel_id=1, source_target_pairs={{0,4},{4,0},{8,12},{12,8},{16,20},{20,16},{24,28},{28,24},{1,5},{5... | collective-permute-start | bytes 1327112 | tf_op jit(solution)/shard_map/ppermute | solution.py:1126
  96.2 1.6 collective-permute-start.24
  96.2 2.0 collective-permute-start.22
  97.7 2.0 collective-permute-start.31
  98.2 2.2 collective-permute-start.28
  98.9 1.9 collective-permute-start.33
  99.1 2.4 collective-permute-start.32
  102.2 35.8 %copy-start.19 = (bf16[2,24,768]{2,1,0:T(8,128)(2,1)S(1)}, bf16[2,24,768]{2,1,0:T(8,128)(2,1)}, u32[]{:S(2)}) copy-start(bf16[2,24,768]{2,1,0:T(8,128)(2,1)} %qk.1) | copy-start | bytes 221188
  137.5 12.2 %collective-permute-start.34 = (bf16[2,2,2,192,768]{4,3,2,1,0:T(8,128)(2,1)}, bf16[2,2,2,192,768]{4,3,2,1,0:T(8,128)(2,1)S(1)}, u32[]{:S(2)}, u32[]{:S(2)}) collective-permute-start(bf16[2,2,2,192,768]{4,3,2,1,0:T(8,128)(2,1)} %get-tuple-element.105), channel_id=1, source_target_pairs={{0,4},{4,0},{8,12},{12,8},{16,20},{20,16},{24,28},{28,24},{1,5},{5... | collective-permute-start | bytes 7077896 | tf_op jit(solution)/shard_map/ppermute | solution.py:1126
  137.7 15.4 %collective-permute-start.35 = (bf16[2,2,2,192,768]{4,3,2,1,0:T(8,128)(2,1)}, bf16[2,2,2,192,768]{4,3,2,1,0:T(8,128)(2,1)}, u32[]{:S(2)}, u32[]{:S(2)}) collective-permute-start(bf16[2,2,2,192,768]{4,3,2,1,0:T(8,128)(2,1)} %get-tuple-element.110), channel_id=1, source_target_pairs={{0,4},{4,0},{8,12},{12,8},{16,20},{20,16},{24,28},{28,24},{1,5},{5... | collective-permute-start | bytes 7077896 | tf_op jit(solution)/shard_map/ppermute | solution.py:1126
  151.0 26.0 %collective-permute-start.39 = (bf16[2,192,768]{2,1,0:T(8,128)(2,1)}, bf16[2,192,768]{2,1,0:T(8,128)(2,1)}, u32[]{:S(2)}, u32[]{:S(2)}) collective-permute-start(bf16[2,192,768]{2,1,0:T(8,128)(2,1)} %get-tuple-element.145._), channel_id=1, source_target_pairs={{0,8},{4,12},{8,0},{12,4},{16,24},{20,28},{24,16},{28,20},{1,9},{5... | collective-permute-start | bytes 1769480 | tf_op jit(solution)/shard_map/ppermute | solution.py:1126
  151.6 28.5 %collective-permute-start.40 = (bf16[2,192,768]{2,1,0:T(8,128)(2,1)}, bf16[2,192,768]{2,1,0:T(8,128)(2,1)}, u32[]{:S(2)}, u32[]{:S(2)}) collective-permute-start(bf16[2,192,768]{2,1,0:T(8,128)(2,1)} %get-tuple-element.144.__), channel_id=1, source_target_pairs={{0,16},{4,20},{8,24},{12,28},{16,0},{20,4},{24,8},{28,12},{1,17},{... | collective-permute-start | bytes 1769480 | tf_op jit(solution)/shard_map/ppermute | solution.py:1126
  155.7 24.4 %collective-permute-start.38 = (bf16[2,192,768]{2,1,0:T(8,128)(2,1)}, bf16[2,192,768]{2,1,0:T(8,128)(2,1)}, u32[]{:S(2)}, u32[]{:S(2)}) collective-permute-start(bf16[2,192,768]{2,1,0:T(8,128)(2,1)} %get-tuple-element.142), channel_id=1, source_target_pairs={{0,16},{4,20},{8,24},{12,28},{16,0},{20,4},{24,8},{28,12},{1,17},{... | collective-permute-start | bytes 1769480 | tf_op jit(solution)/shard_map/ppermute | solution.py:1126
  156.2 23.9 %collective-permute-start.36 = (bf16[2,192,768]{2,1,0:T(8,128)(2,1)}, bf16[2,192,768]{2,1,0:T(8,128)(2,1)}, u32[]{:S(2)}, u32[]{:S(2)}) collective-permute-start(bf16[2,192,768]{2,1,0:T(8,128)(2,1)} %get-tuple-element.143), channel_id=1, source_target_pairs={{0,8},{4,12},{8,0},{12,4},{16,24},{20,28},{24,16},{28,20},{1,9},{5... | collective-permute-start | bytes 1769480 | tf_op jit(solution)/shard_map/ppermute | solution.py:1126
  178.5 9.8 %collective-permute-start.43 = (bf16[192,768]{1,0:T(8,128)(2,1)S(1)}, bf16[192,768]{1,0:T(8,128)(2,1)S(1)}, u32[]{:S(2)}, u32[]{:S(2)}) collective-permute-start(bf16[192,768]{1,0:T(8,128)(2,1)S(1)} %fusion.18), channel_id=1, source_target_pairs={{0,16},{4,20},{8,24},{12,28},{16,0},{20,4},{24,8},{28,12},{1,17},{... | collective-permute-start | bytes 884744 | tf_op jit(solution)/shard_map/ppermute | solution.py:1126
  180.1 18.3 %collective-permute-start.42 = (bf16[2,2,112,1536]{3,2,1,0:T(8,128)(2,1)S(1)}, bf16[2,2,112,1536]{3,2,1,0:T(8,128)(2,1)S(1)}, u32[]{:S(2)}, u32[]{:S(2)}) collective-permute-start(bf16[2,2,112,1536]{3,2,1,0:T(8,128)(2,1)S(1)} %copy-done.36), channel_id=1, source_target_pairs={{0,4},{4,0},{8,12},{12,8},{16,20},{20,16},{24,28},{28,24},{1,5},{5... | collective-permute-start | bytes 4128776 | tf_op jit(solution)/shard_map/ppermute | solution.py:1126
  180.2 15.6 %collective-permute-start.41 = (bf16[2,2,96,1536]{3,2,1,0:T(8,128)(2,1)S(1)}, bf16[2,2,96,1536]{3,2,1,0:T(8,128)(2,1)S(1)}, u32[]{:S(2)}, u32[]{:S(2)}) collective-permute-start(bf16[2,2,96,1536]{3,2,1,0:T(8,128)(2,1)S(1)} %copy-done.37), channel_id=1, source_target_pairs={{0,4},{4,0},{8,12},{12,8},{16,20},{20,16},{24,28},{28,24},{1,5},{5... | collective-permute-start | bytes 3538952 | tf_op jit(solution)/shard_map/ppermute | solution.py:1126
  181.9 19.9 %collective-permute-start.37 = (bf16[192,768]{1,0:T(8,128)(2,1)S(1)}, bf16[192,768]{1,0:T(8,128)(2,1)S(1)}, u32[]{:S(2)}, u32[]{:S(2)}) collective-permute-start(bf16[192,768]{1,0:T(8,128)(2,1)S(1)} %fusion.19), channel_id=1, source_target_pairs={{0,16},{4,20},{8,24},{12,28},{16,0},{20,4},{24,8},{28,12},{1,17},{... | collective-permute-start | bytes 884744 | tf_op jit(solution)/shard_map/ppermute | solution.py:1126
  184.0 10.0 %collective-permute-start.52 = (bf16[192,768]{1,0:T(8,128)(2,1)S(1)}, bf16[192,768]{1,0:T(8,128)(2,1)S(1)}, u32[]{:S(2)}, u32[]{:S(2)}) collective-permute-start(bf16[192,768]{1,0:T(8,128)(2,1)S(1)} %fusion.17), channel_id=1, source_target_pairs={{0,8},{4,12},{8,0},{12,4},{16,24},{20,28},{24,16},{28,20},{1,9},{5... | collective-permute-start | bytes 884744 | tf_op jit(solution)/shard_map/ppermute | solution.py:1126
  188.4 16.2 %collective-permute-start.56 = (bf16[192,768]{1,0:T(8,128)(2,1)S(1)}, bf16[192,768]{1,0:T(8,128)(2,1)S(1)}, u32[]{:S(2)}, u32[]{:S(2)}) collective-permute-start(bf16[192,768]{1,0:T(8,128)(2,1)S(1)} %fusion.16), channel_id=1, source_target_pairs={{0,8},{4,12},{8,0},{12,4},{16,24},{20,28},{24,16},{28,20},{1,9},{5... | collective-permute-start | bytes 884744 | tf_op jit(solution)/shard_map/ppermute | solution.py:1126
  194.0 49.9 %collective-permute-start.51 = (bf16[96,768]{1,0:T(8,128)(2,1)}, bf16[96,768]{1,0:T(8,128)(2,1)}, u32[]{:S(2)}, u32[]{:S(2)}) collective-permute-start(bf16[96,768]{1,0:T(8,128)(2,1)} %slice.506), channel_id=1, source_target_pairs={{0,1},{1,2},{2,3},{3,0},{4,5},{5,6},{6,7},{7,4},{8,9},{9,10},{10,1... | collective-permute-start | bytes 442376 | tf_op jit(solution)/shard_map/ppermute | solution.py:1130
  195.8 48.0 %collective-permute-start.53 = (bf16[96,768]{1,0:T(8,128)(2,1)}, bf16[96,768]{1,0:T(8,128)(2,1)}, u32[]{:S(2)}, u32[]{:S(2)}) collective-permute-start(bf16[96,768]{1,0:T(8,128)(2,1)} %get-tuple-element.164), channel_id=1, source_target_pairs={{0,2},{1,3},{2,0},{3,1},{4,6},{5,7},{6,4},{7,5},{8,10},{9,11},{10,... | collective-permute-start | bytes 442376 | tf_op jit(solution)/shard_map/ppermute | solution.py:1130
  198.4 45.4 %collective-permute-start.54 = (bf16[96,768]{1,0:T(8,128)(2,1)}, bf16[96,768]{1,0:T(8,128)(2,1)}, u32[]{:S(2)}, u32[]{:S(2)}) collective-permute-start(bf16[96,768]{1,0:T(8,128)(2,1)} %get-tuple-element.165), channel_id=1, source_target_pairs={{0,3},{1,0},{2,1},{3,2},{4,7},{5,4},{6,5},{7,6},{8,11},{9,8},{10,9... | collective-permute-start | bytes 442376 | tf_op jit(solution)/shard_map/ppermute | solution.py:1130
  201.8 13.4 %collective-permute-start.44 = (bf16[2,96,1536]{2,1,0:T(8,128)(2,1)}, bf16[2,96,1536]{2,1,0:T(8,128)(2,1)}, u32[]{:S(2)}, u32[]{:S(2)}) collective-permute-start(bf16[2,96,1536]{2,1,0:T(8,128)(2,1)} %fusion.8), channel_id=1, source_target_pairs={{0,8},{4,12},{8,0},{12,4},{16,24},{20,28},{24,16},{28,20},{1,9},{5... | collective-permute-start | bytes 1769480 | tf_op jit(solution)/shard_map/ppermute | solution.py:1126
  204.6 15.9 %collective-permute-start.46 = (bf16[2,112,1536]{2,1,0:T(8,128)(2,1)}, bf16[2,112,1536]{2,1,0:T(8,128)(2,1)}, u32[]{:S(2)}, u32[]{:S(2)}) collective-permute-start(bf16[2,112,1536]{2,1,0:T(8,128)(2,1)} %fusion), channel_id=1, source_target_pairs={{0,16},{4,20},{8,24},{12,28},{16,0},{20,4},{24,8},{28,12},{1,17},{... | collective-permute-start | bytes 2064392 | tf_op jit(solution)/shard_map/ppermute | solution.py:1126
  215.2 13.7 %collective-permute-start.55 = (bf16[96,768]{1,0:T(8,128)(2,1)S(1)}, bf16[96,768]{1,0:T(8,128)(2,1)S(1)}, u32[]{:S(2)}, u32[]{:S(2)}) collective-permute-start(bf16[96,768]{1,0:T(8,128)(2,1)S(1)} %slice.505), channel_id=1, source_target_pairs={{0,1},{1,2},{2,3},{3,0},{4,5},{5,6},{6,7},{7,4},{8,9},{9,10},{10,1... | collective-permute-start | bytes 442376 | tf_op jit(solution)/shard_map/ppermute | solution.py:1130
  220.5 6.7 %collective-permute-start.45 = (bf16[96,1536]{1,0:T(8,128)(2,1)S(1)}, bf16[96,1536]{1,0:T(8,128)(2,1)S(1)}, u32[]{:S(2)}, u32[]{:S(2)}) collective-permute-start(bf16[96,1536]{1,0:T(8,128)(2,1)S(1)} %fusion.13), channel_id=1, source_target_pairs={{0,16},{4,20},{8,24},{12,28},{16,0},{20,4},{24,8},{28,12},{1,17},{... | collective-permute-start | bytes 884744 | tf_op jit(solution)/shard_map/ppermute | solution.py:1126
  227.2 7.2 %collective-permute-start.47 = (bf16[112,1536]{1,0:T(8,128)(2,1)S(1)}, bf16[112,1536]{1,0:T(8,128)(2,1)S(1)}, u32[]{:S(2)}, u32[]{:S(2)}) collective-permute-start(bf16[112,1536]{1,0:T(8,128)(2,1)S(1)} %fusion.1), channel_id=1, source_target_pairs={{0,8},{4,12},{8,0},{12,4},{16,24},{20,28},{24,16},{28,20},{1,9},{5... | collective-permute-start | bytes 1032200 | tf_op jit(solution)/shard_map/ppermute | solution.py:1126
  228.9 7.7 %collective-permute-start.57 = (bf16[96,768]{1,0:T(8,128)(2,1)S(1)}, bf16[96,768]{1,0:T(8,128)(2,1)S(1)}, u32[]{:S(2)}, u32[]{:S(2)}) collective-permute-start(bf16[96,768]{1,0:T(8,128)(2,1)S(1)} %copy-done.26), channel_id=1, source_target_pairs={{0,2},{1,3},{2,0},{3,1},{4,6},{5,7},{6,4},{7,5},{8,10},{9,11},{10,... | collective-permute-start | bytes 442376 | tf_op jit(solution)/shard_map/ppermute | solution.py:1130
  234.5 9.4 %collective-permute-start.58 = (bf16[96,768]{1,0:T(8,128)(2,1)S(1)}, bf16[96,768]{1,0:T(8,128)(2,1)S(1)}, u32[]{:S(2)}, u32[]{:S(2)}) collective-permute-start(bf16[96,768]{1,0:T(8,128)(2,1)S(1)} %copy-done.25), channel_id=1, source_target_pairs={{0,3},{1,0},{2,1},{3,2},{4,7},{5,4},{6,5},{7,6},{8,11},{9,8},{10,9... | collective-permute-start | bytes 442376 | tf_op jit(solution)/shard_map/ppermute | solution.py:1130
  244.1 7.7 %collective-permute-start.48 = (bf16[25,3072]{1,0:T(8,128)(2,1)S(1)}, bf16[25,3072]{1,0:T(8,128)(2,1)S(1)}, u32[]{:S(2)}, u32[]{:S(2)}) collective-permute-start(bf16[25,3072]{1,0:T(8,128)(2,1)S(1)} %pad_maximum_fusion.1), channel_id=1, source_target_pairs={{0,1},{1,2},{2,3},{3,0},{4,5},{5,6},{6,7},{7,4},{8,9},{9,10},{10,1... | collective-permute-start | bytes 460808 | tf_op jit(solution)/shard_map/ppermute | solution.py:1130
  245.8 10.0 %collective-permute-start.49 = (bf16[25,3072]{1,0:T(8,128)(2,1)S(1)}, bf16[25,3072]{1,0:T(8,128)(2,1)S(1)}, u32[]{:S(2)}, u32[]{:S(2)}) collective-permute-start(bf16[25,3072]{1,0:T(8,128)(2,1)S(1)} %pad_maximum_fusion.2), channel_id=1, source_target_pairs={{0,2},{1,3},{2,0},{3,1},{4,6},{5,7},{6,4},{7,5},{8,10},{9,11},{10,... | collective-permute-start | bytes 460808 | tf_op jit(solution)/shard_map/ppermute | solution.py:1130
  245.9 9.9 %collective-permute-start.50 = (bf16[25,3072]{1,0:T(8,128)(2,1)S(1)}, bf16[25,3072]{1,0:T(8,128)(2,1)S(1)}, u32[]{:S(2)}, u32[]{:S(2)}) collective-permute-start(bf16[25,3072]{1,0:T(8,128)(2,1)S(1)} %pad_maximum_fusion.3), channel_id=1, source_target_pairs={{0,3},{1,0},{2,1},{3,2},{4,7},{5,4},{6,5},{7,6},{8,11},{9,8},{10,9... | collective-permute-start | bytes 460808 | tf_op jit(solution)/shard_map/ppermute | solution.py:1130
  (52 other events, 324.3 us)
